TPU v7x, 32 devices: a whole 2x2x4 slice. The times are simulated.
32 devices in a mesh: hi: 4 (over y, x), lo: 8 (over z, core).
Axes of the slice: x: 2, y: 2, z: 4, core: 2. Of those that a mesh axis runs over, the one named last changes fastest.
Arguments:
- charges: bfloat16 [262144, 128], P(('hi', 'lo')), may hold values from -6 to 6
- source_order: int32 [262144], P(('hi', 'lo')), may hold values from 0 to 8191, as said below
- source_interp: bfloat16 [262144, 128], P(('hi', 'lo')), may hold values from -0.5 to 0.5
- factors: bfloat16 [4096, 8, 128], P(('hi', 'lo')), may hold values from -6 to 6
- transfers: bfloat16 [8, 2, 2, 64, 128], replicated, may hold values from -0.375 to 0.375
- level_bits: int32 [4], replicated, may hold values from 0 to 6
- receiver_interp: bfloat16 [262144, 128], P(('hi', 'lo')), may hold values from -0.5 to 0.5
- receiver_slot: int32 [262144], P(('hi', 'lo')), may hold values from 0 to 8191, as said below
Outputs:
- displacement: bfloat16 [262144, 128], P(('hi', 'lo'))
Inputs may be any that keep to these rules, and one draw needn't show every extreme that they name: `source_order`: each aligned block of 8192 entries is a permutation of 0 to 8191. `receiver_slot`: each aligned block of 8192 entries is a permutation of 0 to 8191.
All inputs are finite; a program needn't handle non-finite values.
Results may differ from a plain program's by a relative error of at most 0.019.
Values may be sent and summed in bfloat16 or wider, within the bound.
No kernel may reach another device: no remote copies, remote signals or barrier semaphores. Data moves between devices by JAX's collectives and lax.ppermute only.
A program may use at most 64 MiB of HBM per device.

v0:
```python
import jax
import jax.numpy as jnp
from jax import lax
from jax.sharding import PartitionSpec as P

LEAF = 64


def partner_2(value, axis, bit):
    mask = 2**bit
    pairs = [(source, source ^ mask) for source in range(lax.axis_size(axis))]
    return lax.ppermute(value, axis, pairs)


def real_form(block_piece):
    rank_size = block_piece.shape[0]
    real_part = block_piece[:, :rank_size]
    imag_part = block_piece[:, rank_size:]
    lower_rows = jnp.concatenate([-imag_part, real_part], axis=1)
    return jnp.concatenate([block_piece, lower_rows], axis=0)


def times_factor(values, factor):
    rank_size = factor.shape[-1] // 2
    widened = factor.astype(jnp.float32)[:, None, :]
    factor_re = widened[..., :rank_size]
    factor_im = widened[..., rank_size:]
    values_re = values[..., :rank_size]
    values_im = values[..., rank_size:]
    return jnp.concatenate(
        [
            values_re * factor_re - values_im * factor_im,
            values_re * factor_im + values_im * factor_re,
        ],
        axis=-1,
    )


def apply_matrix(coeffs, matrix):
    pair_width = coeffs.shape[-1]
    flattened = coeffs.reshape(-1, pair_width)
    return jnp.dot(flattened, real_form(matrix), preferred_element_type=jnp.float32).reshape(
        coeffs.shape
    )


def mix_halves(lower_half, upper_half, matrices):
    child_zero = apply_matrix(lower_half, matrices[0, 0]) + apply_matrix(upper_half, matrices[0, 1])
    child_one = apply_matrix(lower_half, matrices[1, 0]) + apply_matrix(upper_half, matrices[1, 1])
    return (child_zero, child_one)


def local_level(coeffs, factor, matrices, stride):
    blocks_here = coeffs.shape[0]
    half_index = jnp.arange(blocks_here // 2, dtype=jnp.int32)
    lower_index = half_index // stride * (2 * stride) + half_index % stride
    upper_index = lower_index + stride
    child_zero, child_one = mix_halves(coeffs[lower_index], coeffs[upper_index], matrices)
    blocks = jnp.arange(blocks_here, dtype=jnp.int32)
    child_bit = blocks // stride % 2
    position = child_bit * (blocks_here // 2) + blocks // (2 * stride) * stride + blocks % stride
    merged = jnp.concatenate([child_zero, child_one], axis=0)[position]
    return times_factor(merged, factor).astype(jnp.bfloat16)


def remote_level(coeffs, partner, factor, matrices, own_child):
    own_row = lax.dynamic_index_in_dim(matrices, own_child, 0, keepdims=False)
    own_matrix = lax.dynamic_index_in_dim(own_row, own_child, 0, keepdims=False)
    other_matrix = lax.dynamic_index_in_dim(own_row, 1 - own_child, 0, keepdims=False)
    summed = apply_matrix(coeffs, own_matrix) + apply_matrix(partner, other_matrix)
    return times_factor(summed, factor).astype(jnp.bfloat16)


def per_device(
    charges,
    source_order,
    source_interp,
    factors,
    transfers,
    level_bits,
    receiver_interp,
    receiver_slot,
):
    points, twice_rhs = charges.shape
    rhs_count = twice_rhs // 2
    pair_width = source_interp.shape[1]
    rank_size = pair_width // 2
    blocks_here = points // LEAF
    ordered = charges[source_order].reshape(blocks_here, LEAF, twice_rhs)
    products = jnp.einsum(
        "bmk,bmr->bkr",
        ordered,
        source_interp.reshape(blocks_here, LEAF, pair_width),
        preferred_element_type=jnp.float32,
    )
    real_part = products[:, :rhs_count, :rank_size] - products[:, rhs_count:, rank_size:]
    imag_part = products[:, :rhs_count, rank_size:] + products[:, rhs_count:, :rank_size]
    coeffs = jnp.concatenate([real_part, imag_part], axis=-1).astype(jnp.bfloat16)
    strides = jnp.left_shift(jnp.int32(1), level_bits)
    coeffs = local_level(coeffs, factors[:, 0], transfers[0], strides[0])
    coeffs = local_level(coeffs, factors[:, 1], transfers[1], strides[1])
    inner_bit = lax.axis_size("lo").bit_length() - 2
    outer_bit = lax.axis_size("hi").bit_length() - 2
    inner_child = lax.axis_index("lo") >> inner_bit & 1
    outer_child = lax.axis_index("hi") >> outer_bit & 1
    partner = partner_2(coeffs, "lo", inner_bit)
    coeffs = remote_level(coeffs, partner, factors[:, 2], transfers[2], inner_child)
    partner = partner_2(coeffs, "hi", outer_bit)
    coeffs = remote_level(coeffs, partner, factors[:, 3], transfers[3], outer_child)
    carried = factors[:, 4:]
    coeffs, carried = (
        lax.all_to_all(coeffs, ("hi", "lo"), split_axis=0, concat_axis=0, tiled=True),
        lax.all_to_all(carried, ("hi", "lo"), split_axis=0, concat_axis=0, tiled=True),
    )
    coeffs = local_level(coeffs, carried[:, 0], transfers[4], strides[2])
    coeffs = local_level(coeffs, carried[:, 1], transfers[5], strides[3])
    partner = partner_2(coeffs, "lo", inner_bit)
    coeffs = remote_level(coeffs, partner, carried[:, 2], transfers[6], inner_child)
    partner = partner_2(coeffs, "hi", outer_bit)
    coeffs = remote_level(coeffs, partner, carried[:, 3], transfers[7], outer_child)
    coeff_re = coeffs[..., :rank_size]
    coeff_im = coeffs[..., rank_size:]
    stacked = jnp.concatenate(
        [
            jnp.concatenate([coeff_re, -coeff_im], axis=-1),
            jnp.concatenate([coeff_im, coeff_re], axis=-1),
        ],
        axis=1,
    )
    values = jnp.einsum(
        "bmr,bnr->bmn",
        receiver_interp.reshape(blocks_here, LEAF, pair_width),
        stacked,
        preferred_element_type=jnp.float32,
    )
    tree_values = values.astype(jnp.bfloat16).reshape(points, twice_rhs)
    return tree_values[receiver_slot]


def solution(mesh):
    return jax.shard_map(
        per_device,
        mesh=mesh,
        in_specs=(
            P(("hi", "lo"), None),
            P(("hi", "lo")),
            P(("hi", "lo"), None),
            P(("hi", "lo"), None, None),
            P(),
            P(),
            P(("hi", "lo"), None),
            P(("hi", "lo")),
        ),
        out_specs=P(("hi", "lo"), None),
        check_vma=False,
    )
```

profile of v0, /device:TPU:1, one launch (start us, length us, event | category | flops | bytes accessed | tf_op | source)
XLA Modules:
  0.0 557.7 jit_solution(7285945244675413435)
XLA Ops:
  8.8 30.1 %gather_fusion = bf16[8192,128]{1,0:T(8,128)(2,1)} fusion(bf16[8192,128]{1,0:T(8,128)(2,1)} %param.8, s32[8192]{0:T(1024)S(1)} %fusion.8), kind=kCustom, calls=%fused_computation | custom fusion | bytes 4227072 | tf_op jit(solution)/shard_map/gather | solution.py:89
  38.9 2.9 fusion.187
  41.9 2.8 fusion.1
  44.8 2.5 pad_maximum_fusion.4
  47.3 2.4 gather_fusion.1
  49.7 2.3 gather_fusion.2
  56.0 2.5 pad_maximum_fusion
  58.5 5.0 gather_fusion.3
  63.9 5.0 subtract_convert_fusion.3
  68.9 2.5 pad_maximum_fusion.5
  71.4 2.3 gather_fusion.4
  73.7 2.3 gather_fusion.5
  78.2 2.5 pad_maximum_fusion.1
  80.8 5.0 gather_fusion.6
  85.8 5.0 subtract_convert_fusion.2
  92.1 3.2 collective-permute-start
  96.1 1.6 fusion.6
  97.8 88.0 %collective-permute-done = bf16[128,64,128]{2,1,0:T(8,128)(2,1)} collective-permute-done((bf16[128,64,128]{2,1,0:T(8,128)(2,1)S(1)}, bf16[128,64,128]{2,1,0:T(8,128)(2,1)}, u32[]{:S(2)}, u32[]{:S(2)}) %collective-permute-start) | collective-permute-done | bytes 2097184 | tf_op jit(solution)/shard_map/ppermute | solution.py:12
  185.8 3.4 convolution_add_fusion.3
  193.0 6.3 %all-to-all-start.1 = ((bf16[128,4,128]{2,1,0:T(4,128)(2,1)}), bf16[128,4,128]{2,1,0:T(4,128)(2,1)S(1)}, u32[]{:S(2)}, u32[]{:S(2)}) async-start(bf16[128,4,128]{2,1,0:T(4,128)(2,1)} %slice.446), calls=%async_computation.1 | async-start | bytes 262144 | tf_op jit(solution)/shard_map/all_to_all | solution.py:113
  200.5 38.3 %collective-permute-done.1 = bf16[128,64,128]{0,2,1:T(8,128)(2,1)} collective-permute-done((bf16[128,64,128]{0,2,1:T(8,128)(2,1)}, bf16[128,64,128]{0,2,1:T(8,128)(2,1)}, u32[]{:S(2)}, u32[]{:S(2)}) %collective-permute-start.1) | collective-permute-done | bytes 2097184 | tf_op jit(solution)/shard_map/ppermute | solution.py:12
  238.8 2.3 convolution_add_fusion.1
  241.9 2.8 copy.77
  244.7 8.9 %all-to-all-start = ((bf16[128,64,128]{2,1,0:T(8,128)(2,1)}), bf16[128,64,128]{2,1,0:T(8,128)(2,1)}, u32[]{:S(2)}, u32[]{:S(2)}) async-start(bf16[128,64,128]{2,1,0:T(8,128)(2,1)} %copy.77), calls=%async_computation | async-start | bytes 4194304 | tf_op jit(solution)/shard_map/all_to_all | solution.py:112
  263.1 39.7 %all-to-all-done = bf16[128,64,128]{2,1,0:T(8,128)(2,1)} async-done(((bf16[128,64,128]{2,1,0:T(8,128)(2,1)}), bf16[128,64,128]{2,1,0:T(8,128)(2,1)}, u32[]{:S(2)}, u32[]{:S(2)}) %all-to-all-start) | async-done | bytes 2097184 | tf_op jit(solution)/shard_map/all_to_all | solution.py:112
  302.8 2.3 gather_fusion.7
  305.1 1.9 fusion.68
  307.0 1.8 fusion.77
  308.8 2.3 gather_fusion.8
  311.1 2.2 convolution_add_fusion.7
  313.8 2.5 pad_maximum_fusion.2
  316.4 5.0 gather_fusion.9
  321.4 5.0 subtract_convert_fusion.1
  326.4 2.5 pad_maximum_fusion.9
  328.9 2.3 gather_fusion.10
  331.2 2.3 gather_fusion.11
  335.5 2.5 pad_maximum_fusion.3
  338.0 5.0 gather_fusion.12
  343.0 5.0 subtract_convert_fusion
  350.1 1.8 fusion.3
  351.9 88.1 %collective-permute-done.2 = bf16[128,64,128]{2,1,0:T(8,128)(2,1)} collective-permute-done((bf16[128,64,128]{2,1,0:T(8,128)(2,1)S(1)}, bf16[128,64,128]{2,1,0:T(8,128)(2,1)}, u32[]{:S(2)}, u32[]{:S(2)}) %collective-permute-start.2) | collective-permute-done | bytes 2097184 | tf_op jit(solution)/shard_map/ppermute | solution.py:12
  439.9 3.4 convolution_add_fusion.2
  447.9 44.6 %collective-permute-done.3 = bf16[128,64,128]{0,2,1:T(8,128)(2,1)} collective-permute-done((bf16[128,64,128]{0,2,1:T(8,128)(2,1)}, bf16[128,64,128]{0,2,1:T(8,128)(2,1)}, u32[]{:S(2)}, u32[]{:S(2)}) %collective-permute-start.3) | collective-permute-done | bytes 2097184 | tf_op jit(solution)/shard_map/ppermute | solution.py:12
  492.5 2.4 convolution_add_fusion
  496.1 17.8 %maximum_maximum_fusion = bf16[128,128,128]{0,2,1:T(8,128)(2,1)} fusion(bf16[128,64,64]{0,2,1:T(8,128)(2,1)S(1)} %subtract_convert_fusion.4, bf16[128,64,64]{0,2,1:T(8,128)(2,1)S(1)} %get-tuple-element.6, bf16[128,64,64]{0,2,1:T(8,128)(2,1)S(1)} %get-tuple-element.5), kind=kLoop, calls=%fused_computation.22 | loop fusion | flops 16777216 | bytes 7340032 | tf_op jit(solution)/shard_map/concatenate | solution.py:123
  513.9 6.9 %copy.90 = bf16[128,128,128]{2,1,0:T(8,128)(2,1)} copy(bf16[128,128,128]{0,2,1:T(8,128)(2,1)} %maximum_maximum_fusion) | data formatting | bytes 8388608 | tf_op jit(solution)/shard_map/concatenate | solution.py:123
  520.8 6.5 %convolution_convert_fusion = bf16[128,128,64]{1,2,0:T(8,128)(2,1)} fusion(bf16[128,128,128]{2,1,0:T(8,128)(2,1)} %copy.90, bf16[128,64,128]{2,1,0:T(8,128)(2,1)S(1)} %bitcast.195), kind=kOutput, calls=%fused_computation.57 | convolution fusion | flops 269484032 | bytes 8388608 | tf_op jit(solution)/shard_map/bmr,bnr->bmn/dot_general | solution.py:130
  527.3 30.3 %gather_fusion.13 = bf16[8192,128]{1,0:T(8,128)(2,1)} fusion(bf16[8192,128]{1,0:T(8,128)(2,1)} %bitcast.193, s32[8192]{0:T(1024)S(1)} %fusion.9), kind=kCustom, calls=%fused_computation.13 | custom fusion | bytes 4227072 | tf_op jit(solution)/shard_map/gather | solution.py:137
  (117 shorter events, 32.2 us)
Async XLA Ops:
  0.0 38.9 %copy-start = (bf16[8192,128]{1,0:T(8,128)(2,1)S(1)}, bf16[8192,128]{1,0:T(8,128)(2,1)}, u32[]{:S(2)}) copy-start(bf16[8192,128]{1,0:T(8,128)(2,1)} %param.10) | copy-start | bytes 6291460
  41.9 2.9 copy-start.5
  47.3 6.3 %copy-start.4 = (bf16[128,8,128]{2,1,0:T(8,128)(2,1)S(1)}, bf16[128,8,128]{2,1,0:T(8,128)(2,1)}, u32[]{:S(2)}) copy-start(bf16[128,8,128]{2,1,0:T(8,128)(2,1)} %param.11) | copy-start | bytes 786436
  92.1 93.7 %collective-permute-start = (bf16[128,64,128]{2,1,0:T(8,128)(2,1)S(1)}, bf16[128,64,128]{2,1,0:T(8,128)(2,1)}, u32[]{:S(2)}, u32[]{:S(2)}) collective-permute-start(bf16[128,64,128]{2,1,0:T(8,128)(2,1)S(1)} %pad_maximum_fusion.6), channel_id=1, source_target_pairs={{0,4},{1,5},{2,6},{3,7},{4,0},{5,1},{6,2},{7,3},{8,12},{9,13},{10,... | collective-permute-start | bytes 6291464 | tf_op jit(solution)/shard_map/ppermute | solution.py:12
  191.3 47.5 %collective-permute-start.1 = (bf16[128,64,128]{0,2,1:T(8,128)(2,1)}, bf16[128,64,128]{0,2,1:T(8,128)(2,1)}, u32[]{:S(2)}, u32[]{:S(2)}) collective-permute-start(bf16[128,64,128]{0,2,1:T(8,128)(2,1)} %pad_maximum_fusion.7), channel_id=1, source_target_pairs={{0,16},{8,24},{16,0},{24,8},{1,17},{9,25},{17,1},{25,9},{2,18},{10... | collective-permute-start | bytes 6291464 | tf_op jit(solution)/shard_map/ppermute | solution.py:12
  193.0 51.6 %all-to-all-start.1 = ((bf16[128,4,128]{2,1,0:T(4,128)(2,1)}), bf16[128,4,128]{2,1,0:T(4,128)(2,1)S(1)}, u32[]{:S(2)}, u32[]{:S(2)}) async-start(bf16[128,4,128]{2,1,0:T(4,128)(2,1)} %slice.446), calls=%async_computation.1 | async-start | bytes 262144 | tf_op jit(solution)/shard_map/all_to_all | solution.py:113
  244.7 58.1 %all-to-all-start = ((bf16[128,64,128]{2,1,0:T(8,128)(2,1)}), bf16[128,64,128]{2,1,0:T(8,128)(2,1)}, u32[]{:S(2)}, u32[]{:S(2)}) async-start(bf16[128,64,128]{2,1,0:T(8,128)(2,1)} %copy.77), calls=%async_computation | async-start | bytes 4194304 | tf_op jit(solution)/shard_map/all_to_all | solution.py:112
  311.1 2.2 copy-start.2
  349.2 90.7 %collective-permute-start.2 = (bf16[128,64,128]{2,1,0:T(8,128)(2,1)S(1)}, bf16[128,64,128]{2,1,0:T(8,128)(2,1)}, u32[]{:S(2)}, u32[]{:S(2)}) collective-permute-start(bf16[128,64,128]{2,1,0:T(8,128)(2,1)S(1)} %pad_maximum_fusion.10), channel_id=1, source_target_pairs={{0,4},{1,5},{2,6},{3,7},{4,0},{5,1},{6,2},{7,3},{8,12},{9,13},{10,... | collective-permute-start | bytes 6291464 | tf_op jit(solution)/shard_map/ppermute | solution.py:12
  444.0 3.0 copy-start.6
  445.5 47.0 %collective-permute-start.3 = (bf16[128,64,128]{0,2,1:T(8,128)(2,1)}, bf16[128,64,128]{0,2,1:T(8,128)(2,1)}, u32[]{:S(2)}, u32[]{:S(2)}) collective-permute-start(bf16[128,64,128]{0,2,1:T(8,128)(2,1)} %pad_maximum_fusion.11), channel_id=1, source_target_pairs={{0,16},{8,24},{16,0},{24,8},{1,17},{9,25},{17,1},{25,9},{2,18},{10... | collective-permute-start | bytes 6291464 | tf_op jit(solution)/shard_map/ppermute | solution.py:12
  513.9 6.9 %copy-start.3 = (bf16[8192,128]{1,0:T(8,128)(2,1)S(1)}, bf16[8192,128]{1,0:T(8,128)(2,1)}, u32[]{:S(2)}) copy-start(bf16[8192,128]{1,0:T(8,128)(2,1)} %param.14) | copy-start | bytes 6291460
  527.3 30.3 %copy-start.1 = (bf16[8192,128]{1,0:T(8,128)(2,1)S(1)}, bf16[8192,128]{1,0:T(8,128)(2,1)}, u32[]{:S(2)}) copy-start(bf16[8192,128]{1,0:T(8,128)(2,1)} %param.10) | copy-start | bytes 6291460
where the time goes:
time: 563 us; the launch traced here: 558 us
  waiting for transfers between devices  299 us (53%)
  local copies, waits for them, and re-layouts  113 us (20%)
  other arithmetic  76 us (13%)
  matrix products  38.1 us (7%)
  starting transfers between devices  20.7 us (4%)
  between operations  11.1 us (2%)
    ppermute x4, waiting for transfers between devices, partner_2(): return lax.ppermute(value, axis, pairs)  259 us
    all_to_all x1, waiting for transfers between devices, per_device(): lax.all_to_all(coeffs, ('hi', 'lo'), split_axis=0, concat_axis=0, tiled=T...  39.7 us
    gather x1, local copies, waits for them, and re-layouts, per_device(): return tree_values[receiver_slot]  30.3 us
    gather x1, local copies, waits for them, and re-layouts, per_device(): ordered = charges[source_order].reshape(blocks_here, LEAF, twice_rhs)  30.1 us
    dot_general x24, matrix products, apply_matrix(): jnp.dot(flattened, real_form(matrix), preferred_element_type=jnp.float32)  28.7 us
    another operation x8, other arithmetic  24.7 us
    gather x4, local copies, waits for them, and re-layouts, local_level(): merged = jnp.concatenate([child_zero, child_one], axis=0)[position]  20 us
    concatenate x1, other arithmetic, per_device(): jnp.concatenate([jnp.concatenate([coeff_re, -coeff_im], axis=-1), jnp.con...  17.8 us
  transfers between devices with their start and end apart: 6, of which 5 were waited for; matrix products, arithmetic and copies ran while one was open for 3% of the time, Pallas kernels for 0%

commit v1 on v0

v1 whole, which is shorter than its diff:
```python
import functools

import jax
import jax.numpy as jnp
from jax import lax
from jax.experimental import pallas as pl
from jax.experimental.pallas import tpu as pltpu
from jax.sharding import PartitionSpec as P

LEAF = 64
AXES = ("hi", "lo")
BATCH = 16
F32 = jnp.float32
BF16 = jnp.bfloat16


def log2(value):
    return value.bit_length() - 1


def lanes_low(shape):
    return lax.broadcasted_iota(jnp.int32, shape, len(shape) - 1) < 64


def roll64(value):
    return pltpu.roll(value, 64, 1)


def build_weights(w_ref, slot, tr_ref, level, flip=0):
    for i in range(2):
        for c in range(2):
            piece = tr_ref[level, c ^ flip, i ^ flip].astype(F32)
            turned = roll64(piece)
            turned = jnp.where(lanes_low(piece.shape), -turned, turned)
            block = jnp.concatenate([piece, turned], axis=0).astype(BF16)
            w_ref[slot, i * 128 : (i + 1) * 128, c * 128 : (c + 1) * 128] = block


def split_factors(read16, fa_ref, fb_ref, first, rows):
    def body(step, carry):
        for part in range(4):
            at = pl.multiple_of(step * 64 + part * 16, 16)
            fac = read16(at).astype(F32)
            turned = roll64(fac)
            low = lanes_low(fac.shape)
            fa_ref[pl.ds(first + at, 16), :] = jnp.where(low, fac, turned)
            fb_ref[pl.ds(first + at, 16), :] = jnp.where(low, -turned, fac)
        return carry

    lax.fori_loop(0, rows // 64, body, 0)


def scaled(value, fa_ref, fb_ref, row):
    fa = fa_ref[pl.ds(row, 1), :]
    fb = fb_ref[pl.ds(row, 1), :]
    return (value * fa + roll64(value) * fb).astype(BF16)


def gather16(rows_ref, index_ref, first):
    iota = lax.broadcasted_iota(jnp.int32, (8, 128), 0)
    halves = []
    for half in range(2):
        acc = None
        for i in range(8):
            at = index_ref[first + half * 8 + i]
            row = jnp.broadcast_to(rows_ref[pl.ds(at, 1), :], (8, 128))
            acc = row if acc is None else jnp.where(iota == i, row, acc)
        halves.append(acc)
    return jnp.concatenate(halves, axis=0).astype(BF16)


def pair_of(k, bit):
    low = k & (lax.shift_left(1, bit) - 1)
    first = lax.shift_left(lax.shift_right_logical(k, bit), bit + 1) | low
    return first, first + lax.shift_left(1, bit)


def source_kernel(dims, order_ref, bits_ref, ch_ref, si_ref, fac_ref, tr_ref, out_ref, x32, coef, fa, fb, w_ref):
    n_hi, n_lo, share, blocks, rhs = dims
    quarter = rhs // 4
    points = blocks * LEAF

    def widen(step, carry):
        rows = pl.ds(pl.multiple_of(step * 256, 256), 256)
        x32[rows, :] = ch_ref[rows, :].astype(F32)
        return carry

    lax.fori_loop(0, points // 256, widen, 0)
    build_weights(w_ref, 0, tr_ref, 0)
    build_weights(w_ref, 1, tr_ref, 1)
    split_factors(lambda at: fac_ref[pl.ds(at, 16), :], fa, fb, 0, blocks * 8)

    def leaf(step, carry):
        for part in range(2):
            b = step * 2 + part
            first = pl.multiple_of(b * LEAF, LEAF)
            rows = jnp.concatenate([gather16(x32, order_ref, first + g * 16) for g in range(LEAF // 16)], axis=0)
            product = lax.dot_general(
                rows, si_ref[pl.ds(first, LEAF), :], (((0,), (0,)), ((), ())), preferred_element_type=F32
            )
            lower = roll64(product[rhs:])
            lower = jnp.where(lanes_low(lower.shape), -lower, lower)
            coef[b] = (product[:rhs] + lower).astype(BF16)
        return carry

    lax.fori_loop(0, blocks // 2, leaf, 0)

    st, lm, hh = log2(share), log2(n_lo // 4), log2(n_hi // 2)

    def store_first(n, value):
        coef[n] = value

    def store_second(n, value):
        t = n & (share - 1)
        core = (n >> st) & 1
        mid = (n >> (st + 1)) & (n_lo // 4 - 1)
        z1 = (n >> (st + 1 + lm)) & 1
        rest = (n >> (st + 2 + lm)) & (n_hi // 2 - 1)
        y = n >> (st + 2 + lm + hh)
        target = rest * n_lo + core * (n_lo // 2) + mid * 2
        m = (y * 2 + z1) * share + t
        for r in range(4):
            d = target + (r // 2) * (n_hi // 2) * n_lo + r % 2
            out_ref[d * (4 * share) + m] = value[r * quarter : (r + 1) * quarter]

    def level(index, store):
        bit = bits_ref[index]

        def body(step, carry):
            ends = [pair_of(step * 4 + p, bit) for p in range(4)]
            lhs = jnp.concatenate([jnp.concatenate([coef[a], coef[b]], axis=1) for a, b in ends], axis=0)
            res = jnp.dot(lhs, w_ref[index], preferred_element_type=F32)
            for p in range(4):
                for c in range(2):
                    n = ends[p][c]
                    value = res[p * rhs : (p + 1) * rhs, c * 128 : (c + 1) * 128]
                    store(n, scaled(value, fa, fb, n * 8 + index))
            return carry

        lax.fori_loop(0, blocks // 8, body, 0)

    level(0, store_first)
    level(1, store_second)


def middle_kernel(dims, me_ref, bits_ref, g_ref, f0, f1, f2, f3, tr_ref, o0, o1, o2, o3, x, fa, fb, w_ref):
    n_hi, n_lo, share, blocks, rhs = dims
    quarter = rhs // 4
    st = log2(share)
    y, core = me_ref[0], me_ref[1]
    for index in range(4):
        build_weights(w_ref, index, tr_ref, index + 2)
    build_weights(w_ref, 4, tr_ref, 6, core)
    build_weights(w_ref, 5, tr_ref, 7, y)
    for j, f_ref in enumerate((f0, f1, f2, f3)):
        split_factors(lambda at, f_ref=f_ref: f_ref[pl.ds(at, 16), :], fa, fb, j * blocks * 8, blocks * 8)

    rounds = blocks // 2 // BATCH

    def read_arrived(j, n):
        first = (((j >> 1) ^ y) * 2 + ((j & 1) ^ core)) * share
        return g_ref[(n >> st) * (4 * share) + first + (n & (share - 1))]

    def read_held(j, n):
        return x[j * blocks + n]

    def level(index, bit, read):
        def body(step, carry):
            j = step // rounds
            ends = [pair_of((step % rounds) * BATCH + p, bit) for p in range(BATCH)]
            lhs = jnp.concatenate([jnp.concatenate([read(j, a), read(j, b)], axis=1) for a, b in ends], axis=0)
            res = jnp.dot(lhs, w_ref[index - 2], preferred_element_type=F32)
            for p in range(BATCH):
                for c in range(2):
                    n = j * blocks + ends[p][c]
                    value = res[p * quarter : (p + 1) * quarter, c * 128 : (c + 1) * 128]
                    x[n] = scaled(value, fa, fb, n * 8 + index)
            return carry

        lax.fori_loop(0, 4 * rounds, body, 0)

    level(2, st + log2(n_lo) - 1, read_arrived)
    level(3, st + log2(n_lo) + log2(n_hi) - 1, read_held)
    level(4, bits_ref[2], read_held)
    level(5, bits_ref[3], read_held)

    def across(index, pairs, stores):
        for (a, b), store in zip(pairs, stores):

            def body(step, carry, a=a, b=b, store=store):
                first = pl.multiple_of(step * BATCH, BATCH)
                lhs = jnp.concatenate(
                    [x[pl.ds(j * blocks + first, BATCH)].reshape(BATCH * quarter, 128) for j in (a, b)], axis=1
                )
                res = jnp.dot(lhs, w_ref[index - 2], preferred_element_type=F32)
                for p in range(BATCH):
                    for c, j in enumerate((a, b)):
                        value = res[p * quarter : (p + 1) * quarter, c * 128 : (c + 1) * 128]
                        store[c](first + p, scaled(value, fa, fb, (j * blocks + first + p) * 8 + index))
                return carry

            lax.fori_loop(0, blocks // BATCH, body, 0)

    def hold(j):
        def store(n, value):
            x[j * blocks + n] = value

        return store

    def give(o_ref):
        def store(n, value):
            o_ref[n] = value

        return store

    across(6, ((0, 1), (2, 3)), ((hold(0), hold(1)), (hold(2), hold(3))))
    across(7, ((0, 2), (1, 3)), ((give(o0), give(o2)), (give(o1), give(o3))))


def receiver_kernel(dims, me_ref, slot_ref, ri_ref, p0, p1, p2, p3, out_ref, t32, stack):
    n_hi, n_lo, share, blocks, rhs = dims
    quarter = rhs // 4
    y, z1 = me_ref[0], me_ref[2]

    def values(step, carry):
        for part in range(2):
            b = step * 2 + part
            for j, p_ref in enumerate((p0, p1, p2, p3)):
                group = ((j >> 1) ^ y) * 2 + ((j & 1) ^ z1)
                at = pl.multiple_of(group * quarter, quarter)
                piece = p_ref[b].astype(F32)
                upper = jnp.where(lanes_low(piece.shape), piece, -piece)
                stack[part, pl.ds(at, quarter), :] = upper.astype(BF16)
                stack[part, pl.ds(at + rhs, quarter), :] = roll64(piece).astype(BF16)
            rows = pl.ds(pl.multiple_of(b * LEAF, LEAF), LEAF)
            t32[rows, :] = lax.dot_general(
                ri_ref[rows, :], stack[part], (((1,), (1,)), ((), ())), preferred_element_type=F32
            )
        return carry

    lax.fori_loop(0, blocks // 2, values, 0)

    def pick(step, carry):
        for g in range(4):
            first = pl.multiple_of(step * 64 + g * 16, 16)
            out_ref[pl.ds(first, 16), :] = gather16(t32, slot_ref, first)
        return carry

    lax.fori_loop(0, blocks * LEAF // 64, pick, 0)


def on_vmem():
    return pl.BlockSpec(memory_space=pltpu.VMEM)


def on_smem():
    return pl.BlockSpec(memory_space=pltpu.SMEM)


def params():
    return pltpu.CompilerParams(vmem_limit_bytes=48 * 2**20)


def per_device(
    n_hi, n_lo, charges, source_order, source_interp, factors, transfers, level_bits, receiver_interp, receiver_slot
):
    points, twice_rhs = charges.shape
    rhs = twice_rhs // 2
    blocks = points // LEAF
    devices = n_hi * n_lo
    share = blocks // devices
    quarter = rhs // 4
    dims = (n_hi, n_lo, share, blocks, rhs)
    half_hi, half_lo = n_hi // 2 * n_lo, n_lo // 2
    hi, lo = lax.axis_index("hi"), lax.axis_index("lo")
    me = jnp.stack([hi >> (log2(n_hi) - 1), lo & 1, lo >> (log2(n_lo) - 1)]).astype(jnp.int32)

    def swapped(device, j):
        flipped = device ^ (half_hi if j >> 1 else 0)
        core, top = flipped & 1, (flipped // half_lo) & 1
        base = flipped - core - top * half_lo
        return base + (core ^ (j & 1)) * half_lo + top

    spread = factors.reshape(n_hi, 2, n_lo // 4, 2, share, 8, 128).transpose(0, 3, 2, 1, 4, 5, 6)
    spread = lax.all_to_all(spread.reshape(blocks, 8, 128), AXES, split_axis=0, concat_axis=0, tiled=True)
    spread = spread.reshape(blocks * 8, 128)
    facs = [spread]
    for j in range(1, 4):
        mask = (half_hi if j >> 1 else 0) ^ (j & 1)
        facs.append(lax.ppermute(spread, AXES, [(s, s ^ mask) for s in range(devices)]))

    sent = pl.pallas_call(
        functools.partial(source_kernel, dims),
        out_shape=jax.ShapeDtypeStruct((devices * 4 * share, quarter, 128), BF16),
        in_specs=[on_smem(), on_smem(), on_vmem(), on_vmem(), on_vmem(), on_vmem()],
        out_specs=on_vmem(),
        scratch_shapes=[
            pltpu.VMEM((points, 128), F32),
            pltpu.VMEM((blocks, rhs, 128), BF16),
            pltpu.VMEM((blocks * 8, 128), F32),
            pltpu.VMEM((blocks * 8, 128), F32),
            pltpu.VMEM((2, 256, 256), BF16),
        ],
        compiler_params=params(),
        name="source_side",
    )(source_order, level_bits, charges, source_interp, factors.reshape(blocks * 8, 128), transfers)

    arrived = lax.all_to_all(sent, AXES, split_axis=0, concat_axis=0, tiled=True)

    piece = jax.ShapeDtypeStruct((blocks, quarter, 128), BF16)
    pieces = pl.pallas_call(
        functools.partial(middle_kernel, dims),
        out_shape=[piece] * 4,
        in_specs=[on_smem(), on_smem()] + [on_vmem()] * 6,
        out_specs=[on_vmem()] * 4,
        scratch_shapes=[
            pltpu.VMEM((4 * blocks, quarter, 128), BF16),
            pltpu.VMEM((4 * blocks * 8, 128), F32),
            pltpu.VMEM((4 * blocks * 8, 128), F32),
            pltpu.VMEM((6, 256, 256), BF16),
        ],
        compiler_params=params(),
        name="middle_levels",
    )(me, level_bits, arrived, *facs, transfers)

    homes = [
        lax.ppermute(pieces[j], AXES, [(s, swapped(s, j)) for s in range(devices)]) for j in range(4)
    ]

    return pl.pallas_call(
        functools.partial(receiver_kernel, dims),
        out_shape=jax.ShapeDtypeStruct((points, twice_rhs), BF16),
        in_specs=[on_smem(), on_smem()] + [on_vmem()] * 5,
        out_specs=on_vmem(),
        scratch_shapes=[pltpu.VMEM((points, 128), F32), pltpu.VMEM((2, 2 * rhs, 128), BF16)],
        compiler_params=params(),
        name="receiver_side",
    )(me, receiver_slot, receiver_interp, *homes)


def solution(mesh):
    body = functools.partial(per_device, mesh.shape["hi"], mesh.shape["lo"])
    return jax.shard_map(
        body,
        mesh=mesh,
        in_specs=(
            P(AXES, None),
            P(AXES),
            P(AXES, None),
            P(AXES, None, None),
            P(),
            P(),
            P(AXES, None),
            P(AXES),
        ),
        out_specs=P(AXES, None),
        check_vma=False,
    )
```

time: 563 us -> 216 us (0.38)
  waiting for transfers between devices: 299 us -> 90.1 us
  local copies, waits for them, and re-layouts: 113 us -> 6.69 us
  Pallas kernels: 0 us -> 96.8 us
  other arithmetic: 76 us -> 0.08 us
  matrix products: 38.1 us -> 0 us
  between operations: 11.1 us -> 0.08 us
    ppermute x4 -> x7, waiting for transfers between devices: 259 us -> 73.1 us  [the longest x4 42.9 us: per_device(): lax.ppermute(pieces[j], AXES, [(s, swapped(s, j)) for s in range(devices)])]
    gather x14 -> x0, local copies, waits for them, and re-layouts: 99.2 us -> none  [the longest x1 30.3 us: per_device(): return tree_values[receiver_slot]]
    pallas_call x0 -> x3, Pallas kernels: none -> 96.8 us  [the longest x1 37 us: per_device(): pl.pallas_call(functools.partial(source_kernel, dims), out_shape=jax.Shap...]
    concatenate x13 -> x0, other arithmetic: 40.9 us -> none  [the longest x1 17.8 us: per_device(): jnp.concatenate([jnp.concatenate([coeff_re, -coeff_im], axis=-1), jnp.con...]
    dot_general x26 -> x0, matrix products: 38.1 us -> none  [the longest x24 28.7 us: apply_matrix(): jnp.dot(flattened, real_form(matrix), preferred_element_type=jnp.float32)]
    another operation x8 -> x1, other arithmetic: 24.7 us -> 0.08 us  [per_device(): jnp.stack([hi >> log2(n_hi) - 1, lo & 1, lo >> log2(n_lo) - 1])]
    all_to_all x2, waiting for transfers between devices: 39.7 us -> 17 us  [the longest x1 17 us: per_device(): lax.all_to_all(sent, AXES, split_axis=0, concat_axis=0, tiled=True)]
    concatenate x2 -> x0, local copies, waits for them, and re-layouts: 9.66 us -> none  [the longest x1 6.89 us: per_device(): jnp.concatenate([jnp.concatenate([coeff_re, -coeff_im], axis=-1), jnp.con...]
  transfers between devices with their start and end apart: 6 -> 9, of which waited for: 5 -> 5; matrix products, arithmetic and copies ran while one was open for 3% -> 0% of each run, Pallas kernels for 0% -> 17%
where the time goes in v1:
time: 216 us; the launch traced here: 215 us
  Pallas kernels  96.8 us (45%)
  waiting for transfers between devices  90.1 us (42%)
  starting transfers between devices  21.7 us (10%)
  local copies, waits for them, and re-layouts  6.69 us (3%)
    ppermute x4, waiting for transfers between devices, per_device(): lax.ppermute(pieces[j], AXES, [(s, swapped(s, j)) for s in range(devices)])  42.9 us
    pallas_call x1, Pallas kernels, per_device(): pl.pallas_call(functools.partial(source_kernel, dims), out_shape=jax.Shap...  37 us
    pallas_call x1, Pallas kernels, per_device(): pl.pallas_call(functools.partial(middle_kernel, dims), out_shape=[piece]...  34.4 us
    ppermute x3, waiting for transfers between devices, per_device(): lax.ppermute(spread, AXES, [(s, s ^ mask) for s in range(devices)])  30.2 us
    pallas_call x1, Pallas kernels, per_device(): pl.pallas_call(functools.partial(receiver_kernel, dims), out_shape=jax.Sh...  25.5 us
    all_to_all x1, waiting for transfers between devices, per_device(): lax.all_to_all(sent, AXES, split_axis=0, concat_axis=0, tiled=True)  17 us
    all_to_all x1, starting transfers between devices, per_device(): lax.all_to_all(spread.reshape(blocks, 8, 128), AXES, split_axis=0, concat...  7.1 us
    ppermute x4, starting transfers between devices, per_device(): lax.ppermute(pieces[j], AXES, [(s, swapped(s, j)) for s in range(devices)])  6.63 us
  transfers between devices with their start and end apart: 9, of which 5 were waited for; matrix products, arithmetic and copies ran while one was open for 0% of the time, Pallas kernels for 17%

profile of v1, /device:TPU:1, one launch (start us, length us, event | category | flops | bytes accessed | tf_op | source)
XLA Modules:
  0.0 215.4 jit_solution(7460179167918123132)
XLA Ops:
  0.0 1.7 copy.9
  1.7 7.1 %all-to-all-start.1 = ((bf16[128,8,128]{2,1,0:T(8,128)(2,1)}), bf16[128,8,128]{2,1,0:T(8,128)(2,1)S(1)}, u32[]{:S(2)}, u32[]{:S(2)}) async-start(bf16[128,8,128]{2,1,0:T(8,128)(2,1)} %bitcast.6), calls=%async_computation.1 | async-start | bytes 524288 | tf_op jit(solution)/shard_map/all_to_all | solution.py:285
  8.8 0.0 copy-start
  8.8 1.0 copy-done
  9.8 0.0 copy-start.2
  9.8 1.6 copy-done.2
  11.4 0.0 copy-start.4
  11.4 0.9 copy-done.4
  12.4 0.0 copy-start.5
  12.4 0.8 copy-done.5
  13.1 0.0 copy-start.7
  13.1 0.7 copy-done.7
  13.8 37.0 %source_side.1 = bf16[512,16,128]{2,1,0:T(8,128)(2,1)} custom-call(s32[8192]{0:T(1024)S(1)} %copy-done.5, s32[4]{0:T(128)S(1)} %copy-done.7, bf16[8192,128]{1,0:T(8,128)(2,1)S(1)} %copy-done.2, bf16[8192,128]{1,0:T(8,128)(2,1)} %si_ref.1, bf16[1024,128]{1,0:T(8,128)(2,1)S(1)} %bitcast.10, bf16[8,2,2,64,128]{4,3,2,1,0:T(8,128)(2,1)S(1)} %copy-done), custom_call_target="tpu_custom_call" | custom-call | tf_op jit(solution)/shard_map/source_side/pallas_call | solution.py:292
  50.8 0.0 copy-start.1
  50.8 0.0 copy-start.8
  50.8 0.0 all-to-all-done.1
  50.8 5.8 %all-to-all-start = ((bf16[512,16,128]{2,1,0:T(8,128)(2,1)}), bf16[512,16,128]{2,1,0:T(8,128)(2,1)S(1)}, u32[]{:S(2)}, u32[]{:S(2)}) async-start(bf16[512,16,128]{2,1,0:T(8,128)(2,1)} %source_side.1), calls=%async_computation | async-start | bytes 4194304 | tf_op jit(solution)/shard_map/all_to_all | solution.py:308
  56.6 0.0 copy-start.6
  56.6 0.3 collective-permute-start
  56.9 1.5 collective-permute-start.1
  58.4 0.4 collective-permute-start.2
  58.8 0.1 pad_add_fusion.me_ref
  58.9 0.0 collective-permute-done.f1
  58.9 20.3 %collective-permute-done.1.f2 = bf16[1024,128]{1,0:T(8,128)(2,1)S(1)} collective-permute-done((bf16[1024,128]{1,0:T(8,128)(2,1)S(1)}, bf16[1024,128]{1,0:T(8,128)(2,1)S(1)}, u32[]{:S(2)}, u32[]{:S(2)}) %collective-permute-start.1) | collective-permute-done | bytes 262176 | tf_op jit(solution)/shard_map/ppermute | solution.py:290
  79.2 9.9 %collective-permute-done.2.f3 = bf16[1024,128]{1,0:T(8,128)(2,1)} collective-permute-done((bf16[1024,128]{1,0:T(8,128)(2,1)S(1)}, bf16[1024,128]{1,0:T(8,128)(2,1)}, u32[]{:S(2)}, u32[]{:S(2)}) %collective-permute-start.2) | collective-permute-done | bytes 262176 | tf_op jit(solution)/shard_map/ppermute | solution.py:290
  89.1 17.0 %all-to-all-done.g_ref = bf16[512,16,128]{2,1,0:T(8,128)(2,1)S(1)} async-done(((bf16[512,16,128]{2,1,0:T(8,128)(2,1)}), bf16[512,16,128]{2,1,0:T(8,128)(2,1)S(1)}, u32[]{:S(2)}, u32[]{:S(2)}) %all-to-all-start) | async-done | bytes 2097184 | tf_op jit(solution)/shard_map/all_to_all | solution.py:308
  106.1 0.0 copy-done.1
  106.1 0.0 copy-done.8
  106.1 0.0 copy-start.3
  106.1 34.4 %middle_levels.1 = (bf16[128,16,128]{2,1,0:T(8,128)(2,1)S(1)}, bf16[128,16,128]{2,1,0:T(8,128)(2,1)S(1)}, bf16[128,16,128]{2,1,0:T(8,128)(2,1)S(1)}, bf16[128,16,128]{2,1,0:T(8,128)(2,1)S(1)}) custom-call(s32[3]{0:T(128)S(1)} %pad_add_fusion.me_ref, s32[4]{0:T(128)S(1)} %copy-done.8, bf16[512,16,128]{2,1,0:T(8,128)(2,1)S(1)} %all-to-all-done.g_ref, ...), custom_call_target="tpu_custom_call" | custom-call | tf_op jit(solution)/shard_map/middle_levels/pallas_call | solution.py:311
  140.5 1.9 collective-permute-start.3
  142.4 0.1 collective-permute-start.4
  142.5 3.3 %collective-permute-start.5 = (bf16[128,16,128]{2,1,0:T(8,128)(2,1)S(1)}, bf16[128,16,128]{2,1,0:T(8,128)(2,1)S(1)}, u32[]{:S(2)}, u32[]{:S(2)}) collective-permute-start(bf16[128,16,128]{2,1,0:T(8,128)(2,1)S(1)} %get-tuple-element.11), channel_id=1, source_target_pairs={{0,16},{1,20},{2,18},{3,22},{4,17},{5,21},{6,19},{7,23},{8,24},{9,... | collective-permute-start | bytes 1572872 | tf_op jit(solution)/shard_map/ppermute | solution.py:327
  145.8 1.3 collective-permute-start.6
  147.1 30.5 %collective-permute-done.3.p0 = bf16[128,16,128]{2,1,0:T(8,128)(2,1)S(1)} collective-permute-done((bf16[128,16,128]{2,1,0:T(8,128)(2,1)S(1)}, bf16[128,16,128]{2,1,0:T(8,128)(2,1)S(1)}, u32[]{:S(2)}, u32[]{:S(2)}) %collective-permute-start.3) | collective-permute-done | bytes 524320 | tf_op jit(solution)/shard_map/ppermute | solution.py:327
  177.7 0.0 collective-permute-done.4.p1
  177.7 12.3 %collective-permute-done.5.p2 = bf16[128,16,128]{2,1,0:T(8,128)(2,1)S(1)} collective-permute-done((bf16[128,16,128]{2,1,0:T(8,128)(2,1)S(1)}, bf16[128,16,128]{2,1,0:T(8,128)(2,1)S(1)}, u32[]{:S(2)}, u32[]{:S(2)}) %collective-permute-start.5) | collective-permute-done | bytes 524320 | tf_op jit(solution)/shard_map/ppermute | solution.py:327
  190.0 0.0 collective-permute-done.6.p3
  190.0 0.0 copy-done.6
  190.0 0.0 copy-done.3
  190.0 25.5 %receiver_side.1 = bf16[8192,128]{1,0:T(8,128)(2,1)} custom-call(s32[3]{0:T(128)S(1)} %pad_add_fusion.me_ref, s32[8192]{0:T(1024)S(1)} %copy-done.6, bf16[8192,128]{1,0:T(8,128)(2,1)S(1)} %copy-done.3, bf16[128,16,128]{2,1,0:T(8,128)(2,1)S(1)} %collective-permute-done.3.p0, bf16[128,16,128]{2,1,0:T(8,128)(2,1)S(1)} %collective-permute-done.4.p1, ...), custom_call_target="tpu_custom_call" | custom-call | tf_op jit(solution)/shard_map/receiver_side/pallas_call | solution.py:330
Async XLA Ops:
  1.7 49.1 %all-to-all-start.1 = ((bf16[128,8,128]{2,1,0:T(8,128)(2,1)}), bf16[128,8,128]{2,1,0:T(8,128)(2,1)S(1)}, u32[]{:S(2)}, u32[]{:S(2)}) async-start(bf16[128,8,128]{2,1,0:T(8,128)(2,1)} %bitcast.6), calls=%async_computation.1 | async-start | bytes 524288 | tf_op jit(solution)/shard_map/all_to_all | solution.py:285
  8.8 1.0 copy-start
  9.8 1.6 copy-start.2
  11.4 0.9 copy-start.4
  12.4 0.8 copy-start.5
  13.1 0.7 copy-start.7
  50.8 55.3 %copy-start.1 = (bf16[8,2,2,64,128]{4,3,2,1,0:T(8,128)(2,1)S(1)}, bf16[8,2,2,64,128]{4,3,2,1,0:T(8,128)(2,1)}, u32[]{:S(2)}) copy-start(bf16[8,2,2,64,128]{4,3,2,1,0:T(8,128)(2,1)} %tr_ref.3) | copy-start | bytes 1572868
  50.8 55.3 %copy-start.8 = (s32[4]{0:T(128)S(1)}, s32[4]{0:T(128)}, u32[]{:S(2)}) copy-start(s32[4]{0:T(128)} %bits_ref.3) | copy-start | bytes 52
  50.8 55.3 %all-to-all-start = ((bf16[512,16,128]{2,1,0:T(8,128)(2,1)}), bf16[512,16,128]{2,1,0:T(8,128)(2,1)S(1)}, u32[]{:S(2)}, u32[]{:S(2)}) async-start(bf16[512,16,128]{2,1,0:T(8,128)(2,1)} %source_side.1), calls=%async_computation | async-start | bytes 4194304 | tf_op jit(solution)/shard_map/all_to_all | solution.py:308
  56.6 133.4 %copy-start.6 = (s32[8192]{0:T(1024)S(1)}, s32[8192]{0:T(1024)}, u32[]{:S(2)}) copy-start(s32[8192]{0:T(1024)} %slot_ref.1) | copy-start | bytes 98308
  56.6 2.3 %collective-permute-start = (bf16[1024,128]{1,0:T(8,128)(2,1)S(1)}, bf16[1024,128]{1,0:T(8,128)(2,1)S(1)}, u32[]{:S(2)}, u32[]{:S(2)}) collective-permute-start(bf16[1024,128]{1,0:T(8,128)(2,1)S(1)} %bitcast.11), channel_id=1, source_target_pairs={{0,1},{1,0},{2,3},{3,2},{4,5},{5,4},{6,7},{7,6},{8,9},{9,8},{10,11... | collective-permute-start | bytes 786440 | tf_op jit(solution)/shard_map/ppermute | solution.py:290
  56.9 22.3 %collective-permute-start.1 = (bf16[1024,128]{1,0:T(8,128)(2,1)S(1)}, bf16[1024,128]{1,0:T(8,128)(2,1)S(1)}, u32[]{:S(2)}, u32[]{:S(2)}) collective-permute-start(bf16[1024,128]{1,0:T(8,128)(2,1)S(1)} %bitcast.12), channel_id=1, source_target_pairs={{0,16},{1,17},{2,18},{3,19},{4,20},{5,21},{6,22},{7,23},{8,24},{9,... | collective-permute-start | bytes 786440 | tf_op jit(solution)/shard_map/ppermute | solution.py:290
  58.4 30.7 %collective-permute-start.2 = (bf16[1024,128]{1,0:T(8,128)(2,1)S(1)}, bf16[1024,128]{1,0:T(8,128)(2,1)}, u32[]{:S(2)}, u32[]{:S(2)}) collective-permute-start(bf16[1024,128]{1,0:T(8,128)(2,1)S(1)} %bitcast.13), channel_id=1, source_target_pairs={{0,17},{1,16},{2,19},{3,18},{4,21},{5,20},{6,23},{7,22},{8,25},{9,... | collective-permute-start | bytes 786440 | tf_op jit(solution)/shard_map/ppermute | solution.py:290
  106.1 83.9 %copy-start.3 = (bf16[8192,128]{1,0:T(8,128)(2,1)S(1)}, bf16[8192,128]{1,0:T(8,128)(2,1)}, u32[]{:S(2)}) copy-start(bf16[8192,128]{1,0:T(8,128)(2,1)} %ri_ref.1) | copy-start | bytes 6291460
  140.5 37.2 %collective-permute-start.3 = (bf16[128,16,128]{2,1,0:T(8,128)(2,1)S(1)}, bf16[128,16,128]{2,1,0:T(8,128)(2,1)S(1)}, u32[]{:S(2)}, u32[]{:S(2)}) collective-permute-start(bf16[128,16,128]{2,1,0:T(8,128)(2,1)S(1)} %get-tuple-element.9), channel_id=1, source_target_pairs={{0,0},{1,4},{2,2},{3,6},{4,1},{5,5},{6,3},{7,7},{8,8},{9,12},{10,1... | collective-permute-start | bytes 1572872 | tf_op jit(solution)/shard_map/ppermute | solution.py:327
  142.4 35.3 %collective-permute-start.4 = (bf16[128,16,128]{2,1,0:T(8,128)(2,1)S(1)}, bf16[128,16,128]{2,1,0:T(8,128)(2,1)S(1)}, u32[]{:S(2)}, u32[]{:S(2)}) collective-permute-start(bf16[128,16,128]{2,1,0:T(8,128)(2,1)S(1)} %get-tuple-element.10), channel_id=1, source_target_pairs={{0,4},{1,0},{2,6},{3,2},{4,5},{5,1},{6,7},{7,3},{8,12},{9,8},{10,1... | collective-permute-start | bytes 1572872 | tf_op jit(solution)/shard_map/ppermute | solution.py:327
  142.5 47.5 %collective-permute-start.5 = (bf16[128,16,128]{2,1,0:T(8,128)(2,1)S(1)}, bf16[128,16,128]{2,1,0:T(8,128)(2,1)S(1)}, u32[]{:S(2)}, u32[]{:S(2)}) collective-permute-start(bf16[128,16,128]{2,1,0:T(8,128)(2,1)S(1)} %get-tuple-element.11), channel_id=1, source_target_pairs={{0,16},{1,20},{2,18},{3,22},{4,17},{5,21},{6,19},{7,23},{8,24},{9,... | collective-permute-start | bytes 1572872 | tf_op jit(solution)/shard_map/ppermute | solution.py:327
  145.8 44.2 %collective-permute-start.6 = (bf16[128,16,128]{2,1,0:T(8,128)(2,1)S(1)}, bf16[128,16,128]{2,1,0:T(8,128)(2,1)S(1)}, u32[]{:S(2)}, u32[]{:S(2)}) collective-permute-start(bf16[128,16,128]{2,1,0:T(8,128)(2,1)S(1)} %get-tuple-element.12), channel_id=1, source_target_pairs={{0,20},{1,16},{2,22},{3,18},{4,21},{5,17},{6,23},{7,19},{8,28},{9,... | collective-permute-start | bytes 1572872 | tf_op jit(solution)/shard_map/ppermute | solution.py:327

commit v2 on v1

v2 whole, which is shorter than its diff:
```python
import functools

import jax
import jax.numpy as jnp
from jax import lax
from jax.experimental import pallas as pl
from jax.experimental.pallas import tpu as pltpu
from jax.sharding import PartitionSpec as P

LEAF = 64
AXES = ("hi", "lo")
SPLIT = 16
STACKS = 16
LEAVES = 16
SPAIRS = 32
F32 = jnp.float32
BF16 = jnp.bfloat16


def log2(value):
    return value.bit_length() - 1


def lanes_low(shape):
    return lax.broadcasted_iota(jnp.int32, shape, len(shape) - 1) < 64


def roll64(value):
    return pltpu.roll(value, 64, 1)


def build_weights(w_ref, slot, tr_ref, level, flip=0):
    for i in range(2):
        for c in range(2):
            piece = tr_ref[level, c ^ flip, i ^ flip].astype(F32)
            turned = roll64(piece)
            turned = jnp.where(lanes_low(piece.shape), -turned, turned)
            block = jnp.concatenate([piece, turned], axis=0).astype(BF16)
            w_ref[slot, i * 128 : (i + 1) * 128, c * 128 : (c + 1) * 128] = block
            across = roll64(jnp.concatenate([piece, turned], axis=0)).astype(BF16)
            w_ref[slot, i * 128 : (i + 1) * 128, 256 + c * 128 : 256 + (c + 1) * 128] = across


def split_factors(read16, fa_ref, fb_ref, first, rows):
    def body(step, carry):
        for part in range(SPLIT):
            at = pl.multiple_of(step * (16 * SPLIT) + part * 16, 16)
            fac = read16(at).astype(F32)
            turned = roll64(fac)
            low = lanes_low(fac.shape)
            fa_ref[pl.ds(first + at, 16), :] = jnp.where(low, fac, turned)
            fb_ref[pl.ds(first + at, 16), :] = jnp.where(low, -turned, fac)
        return carry

    lax.fori_loop(0, rows // (16 * SPLIT), body, 0)


def scaled(value, other, fa_ref, fb_ref, row):
    fa = fa_ref[pl.ds(row, 1), :]
    fb = fb_ref[pl.ds(row, 1), :]
    return (value * fa + other * fb).astype(BF16)


def gather16(rows_ref, index_ref, first):
    iota = lax.broadcasted_iota(jnp.int32, (8, 128), 0)
    halves = []
    for half in range(2):
        acc = None
        for i in range(8):
            at = index_ref[first + half * 8 + i]
            row = jnp.broadcast_to(rows_ref[pl.ds(at, 1), :], (8, 128))
            acc = row if acc is None else jnp.where(iota == i, row, acc)
        halves.append(acc)
    return jnp.concatenate(halves, axis=0).astype(BF16)


def pair_of(k, bit):
    low = k & (lax.shift_left(1, bit) - 1)
    first = lax.shift_left(lax.shift_right_logical(k, bit), bit + 1) | low
    return first, first + lax.shift_left(1, bit)


def source_kernel(
    dims, order_ref, bits_ref, ch_hbm, si_hbm, fac_hbm, tr_hbm, out_ref,
    ch_ref, si_ref, fac_ref, tr_ref, sems, x32, coef, mid_ref, fa, fb, w_ref,
):
    n_hi, n_lo, share, blocks, rhs = dims
    quarter = rhs // 4
    points = blocks * LEAF
    part = points // 4
    copies = [
        pltpu.make_async_copy(ch_hbm.at[pl.ds(i * part, part)], ch_ref.at[pl.ds(i * part, part)], sems.at[i])
        for i in range(4)
    ]
    copies.append(pltpu.make_async_copy(fac_hbm, fac_ref, sems.at[4]))
    copies.append(pltpu.make_async_copy(tr_hbm.at[pl.ds(0, 2)], tr_ref, sems.at[5]))
    copies.append(pltpu.make_async_copy(si_hbm, si_ref, sems.at[6]))
    for copy in copies:
        copy.start()

    def widen(step, carry):
        rows = pl.ds(pl.multiple_of(step * 512, 512), 512)
        x32[rows, :] = ch_ref[rows, :].astype(F32)
        return carry

    for i in range(4):
        copies[i].wait()
        lax.fori_loop(i * (part // 512), (i + 1) * (part // 512), widen, 0)
    for copy in copies[4:]:
        copy.wait()
    build_weights(w_ref, 0, tr_ref, 0)
    build_weights(w_ref, 1, tr_ref, 1)
    split_factors(lambda at: fac_ref[pl.ds(at, 16), :], fa, fb, 0, blocks * 8)

    def leaf(step, carry):
        for part in range(LEAVES):
            b = step * LEAVES + part
            first = pl.multiple_of(b * LEAF, LEAF)
            rows = jnp.concatenate([gather16(x32, order_ref, first + g * 16) for g in range(LEAF // 16)], axis=0)
            product = lax.dot_general(
                rows, si_ref[pl.ds(first, LEAF), :], (((0,), (0,)), ((), ())), preferred_element_type=F32
            )
            lower = roll64(product[rhs:])
            lower = jnp.where(lanes_low(lower.shape), -lower, lower)
            coef[b] = (product[:rhs] + lower).astype(BF16)
        return carry

    lax.fori_loop(0, blocks // LEAVES, leaf, 0)

    st, lm, hh = log2(share), log2(n_lo // 4), log2(n_hi // 2)

    def store_first(n, value):
        mid_ref[n] = value

    def store_second(n, value):
        t = n & (share - 1)
        core = (n >> st) & 1
        lmid = (n >> (st + 1)) & (n_lo // 4 - 1)
        z1 = (n >> (st + 1 + lm)) & 1
        rest = (n >> (st + 2 + lm)) & (n_hi // 2 - 1)
        y = n >> (st + 2 + lm + hh)
        target = rest * n_lo + core * (n_lo // 2) + lmid * 2
        m = (y * 2 + z1) * share + t
        for r in range(4):
            d = target + (r // 2) * (n_hi // 2) * n_lo + r % 2
            out_ref[d * (4 * share) + m] = value[r * quarter : (r + 1) * quarter]

    def level(index, src, store):
        bit = bits_ref[index]

        def body(step, carry):
            ends = [pair_of(step * SPAIRS + p, bit) for p in range(SPAIRS)]
            lhs = jnp.concatenate([jnp.concatenate([src[a], src[b]], axis=1) for a, b in ends], axis=0)
            res = jnp.dot(lhs, w_ref[index], preferred_element_type=F32)
            for p in range(SPAIRS):
                for c in range(2):
                    n = ends[p][c]
                    value = res[p * rhs : (p + 1) * rhs, c * 128 : (c + 1) * 128]
                    other = res[p * rhs : (p + 1) * rhs, 256 + c * 128 : 256 + (c + 1) * 128]
                    store(n, scaled(value, other, fa, fb, n * 8 + index))
            return carry

        lax.fori_loop(0, blocks // 2 // SPAIRS, body, 0)

    level(0, coef, store_first)
    level(1, mid_ref, store_second)


def spare_bit(bits_ref, dims):
    n_hi, n_lo, share, blocks, rhs = dims
    inner = log2(share) + log2(n_lo) - 1
    outer = log2(share) + log2(n_lo) + log2(n_hi) - 1
    free = [bit for bit in range(outer) if bit != inner][:3]
    spare = jnp.int32(free[2])
    for bit in (free[1], free[0]):
        taken = (bits_ref[2] == bit) | (bits_ref[3] == bit)
        spare = jnp.where(taken, spare, bit)
    return spare, inner, outer


def with_bit(i, bit, value):
    low = i & (lax.shift_left(1, bit) - 1)
    return lax.shift_left(lax.shift_right_logical(i, bit), bit + 1) | low | (value << bit)


def prepare_kernel(dims, me_ref, f0, f1, f2, f3, tr_ref, fa, fb, w_ref):
    blocks = dims[3]
    for j, f_ref in enumerate((f0, f1, f2, f3)):
        split_factors(lambda at, f_ref=f_ref: f_ref[pl.ds(at, 16), :], fa, fb, j * blocks * 8, blocks * 8)
    for index in range(4):
        build_weights(w_ref, index, tr_ref, index + 2)
    build_weights(w_ref, 4, tr_ref, 6, me_ref[1])
    build_weights(w_ref, 5, tr_ref, 7, me_ref[0])


def middle_kernel(dims, half, me_ref, bits_ref, g_ref, fa, fb, w_ref, o0, o1, o2, o3, x, x2):
    n_hi, n_lo, share, blocks, rhs = dims
    quarter = rhs // 4
    st = log2(share)
    y, core = me_ref[0], me_ref[1]
    spare, inner, outer = spare_bit(bits_ref, dims)
    count = blocks // 2

    def read_arrived(j, i):
        n = with_bit(i, spare, half)
        first = (((j >> 1) ^ y) * 2 + ((j & 1) ^ core)) * share
        return g_ref[(n >> st) * (4 * share) + first + (n & (share - 1))]

    def held(x):
        def read(j, i):
            return x[j * count + i]

        return read

    def finish(res, p, c, row):
        value = res[p * quarter : (p + 1) * quarter, c * 128 : (c + 1) * 128]
        other = res[p * quarter : (p + 1) * quarter, 256 + c * 128 : 256 + (c + 1) * 128]
        return scaled(value, other, fa, fb, row)

    def level(index, bit, read, x):
        packed = bit - (bit > spare).astype(jnp.int32)
        ends = [pair_of(k, packed) for k in range(count // 2)]
        homes = [tuple(with_bit(i, spare, half) * 8 + index for i in pair) for pair in ends]
        for j in range(4):
            lhs = jnp.concatenate([jnp.concatenate([read(j, a), read(j, b)], axis=1) for a, b in ends], axis=0)
            res = jnp.dot(lhs, w_ref[index - 2], preferred_element_type=F32)
            for p in range(count // 2):
                for c in range(2):
                    x[j * count + ends[p][c]] = finish(res, p, c, j * blocks * 8 + homes[p][c])

    level(2, inner, read_arrived, x)
    level(3, outer, held(x), x2)
    level(4, bits_ref[2], held(x2), x)
    level(5, bits_ref[3], held(x), x2)

    homes = [with_bit(i, spare, half) * 8 for i in range(count)]

    def across(index, x, pairs, outs):
        for (a, b), (out_a, out_b) in zip(pairs, outs):
            lhs = jnp.concatenate(
                [x[pl.ds(j * count, count)].reshape(count * quarter, 128) for j in (a, b)], axis=1
            )
            res = jnp.dot(lhs, w_ref[index - 2], preferred_element_type=F32)
            for p in range(count):
                for c, (j, out) in enumerate(((a, out_a), (b, out_b))):
                    out[p] = finish(res, p, c, j * blocks * 8 + homes[p] + index)

    rest = [x.at[pl.ds(j * count, count)] for j in range(4)]
    across(6, x2, ((0, 1), (2, 3)), ((rest[0], rest[1]), (rest[2], rest[3])))
    across(7, x, ((0, 2), (1, 3)), ((o0, o2), (o1, o3)))


def receiver_values(dims, half, me_ref, bits_ref, ri_ref, pieces, stack, store):
    n_hi, n_lo, share, blocks, rhs = dims
    quarter = rhs // 4
    y, z1 = me_ref[0], me_ref[2]
    spare, _, _ = spare_bit(bits_ref, dims)

    def values(step, carry):
        for part in range(STACKS):
            i = step * STACKS + part
            for j, p_ref in enumerate(pieces):
                group = ((j >> 1) ^ y) * 2 + ((j & 1) ^ z1)
                at = pl.multiple_of(group * quarter, quarter)
                piece = p_ref[i].astype(F32)
                upper = jnp.where(lanes_low(piece.shape), piece, -piece)
                stack[part, pl.ds(at, quarter), :] = upper.astype(BF16)
                stack[part, pl.ds(at + rhs, quarter), :] = roll64(piece).astype(BF16)
            rows = pl.ds(pl.multiple_of(with_bit(i, spare, half) * LEAF, LEAF), LEAF)
            result = lax.dot_general(
                ri_ref[rows, :], stack[part], (((1,), (1,)), ((), ())), preferred_element_type=F32
            )
            store(pl.multiple_of(i * LEAF, LEAF), result)
        return carry

    lax.fori_loop(0, blocks // 2 // STACKS, values, 0)


def first_receivers(dims, me_ref, bits_ref, ri_ref, p0, p1, p2, p3, out_ref, stack):
    def store(at, result):
        out_ref[pl.ds(at, LEAF), :] = result.astype(BF16)

    receiver_values(dims, 0, me_ref, bits_ref, ri_ref, (p0, p1, p2, p3), stack, store)


def last_receivers(dims, me_ref, bits_ref, slot_ref, ri_ref, p0, p1, p2, p3, done_ref, out_ref, t32, stack):
    blocks = dims[3]
    points = blocks * LEAF

    def store(at, result):
        t32[pl.ds(points // 2 + at, LEAF), :] = result

    def widen(step, carry):
        rows = pl.ds(pl.multiple_of(step * 512, 512), 512)
        t32[rows, :] = done_ref[rows, :].astype(F32)
        return carry

    lax.fori_loop(0, points // 2 // 512, widen, 0)
    receiver_values(dims, 1, me_ref, bits_ref, ri_ref, (p0, p1, p2, p3), stack, store)

    def pick(step, carry):
        for g in range(4):
            first = pl.multiple_of(step * 64 + g * 16, 16)
            out_ref[pl.ds(first, 16), :] = gather16(t32, slot_ref, first)
        return carry

    lax.fori_loop(0, points // 64, pick, 0)


def on_vmem():
    return pl.BlockSpec(memory_space=pltpu.VMEM)


def on_any():
    return pl.BlockSpec(memory_space=pl.ANY)


def on_smem():
    return pl.BlockSpec(memory_space=pltpu.SMEM)


def params():
    return pltpu.CompilerParams(vmem_limit_bytes=48 * 2**20)


def per_device(
    n_hi, n_lo, charges, source_order, source_interp, factors, transfers, level_bits, receiver_interp, receiver_slot
):
    points, twice_rhs = charges.shape
    rhs = twice_rhs // 2
    blocks = points // LEAF
    devices = n_hi * n_lo
    share = blocks // devices
    quarter = rhs // 4
    dims = (n_hi, n_lo, share, blocks, rhs)
    half_hi, half_lo = n_hi // 2 * n_lo, n_lo // 2
    hi, lo = lax.axis_index("hi"), lax.axis_index("lo")
    me = jnp.stack([hi >> (log2(n_hi) - 1), lo & 1, lo >> (log2(n_lo) - 1)]).astype(jnp.int32)

    def swapped(device, j):
        flipped = device ^ (half_hi if j >> 1 else 0)
        core, top = flipped & 1, (flipped // half_lo) & 1
        base = flipped - core - top * half_lo
        return base + (core ^ (j & 1)) * half_lo + top

    spread = factors.reshape(n_hi, 2, n_lo // 4, 2, share, 8, 128).transpose(0, 3, 2, 1, 4, 5, 6)
    spread = lax.all_to_all(spread.reshape(blocks, 8, 128), AXES, split_axis=0, concat_axis=0, tiled=True)
    spread = spread.reshape(blocks * 8, 128)
    facs = [spread]
    for j in range(1, 4):
        mask = (half_hi if j >> 1 else 0) ^ (j & 1)
        facs.append(lax.ppermute(spread, AXES, [(s, s ^ mask) for s in range(devices)]))

    sent = pl.pallas_call(
        functools.partial(source_kernel, dims),
        out_shape=jax.ShapeDtypeStruct((devices * 4 * share, quarter, 128), BF16),
        in_specs=[on_smem(), on_smem()] + [on_any()] * 4,
        out_specs=on_vmem(),
        scratch_shapes=[
            pltpu.VMEM((points, 128), BF16),
            pltpu.VMEM((points, 128), BF16),
            pltpu.VMEM((blocks * 8, 128), BF16),
            pltpu.VMEM((2,) + transfers.shape[1:], BF16),
            pltpu.SemaphoreType.DMA((7,)),
            pltpu.VMEM((points, 128), F32),
            pltpu.VMEM((blocks, rhs, 128), BF16),
            pltpu.VMEM((blocks, rhs, 128), BF16),
            pltpu.VMEM((blocks * 8, 128), F32),
            pltpu.VMEM((blocks * 8, 128), F32),
            pltpu.VMEM((2, 256, 512), BF16),
        ],
        compiler_params=params(),
        name="source_side",
    )(source_order, level_bits, charges, source_interp, factors.reshape(blocks * 8, 128), transfers)

    arrived = lax.all_to_all(sent, AXES, split_axis=0, concat_axis=0, tiled=True)

    prepared = pl.pallas_call(
        functools.partial(prepare_kernel, dims),
        out_shape=[
            jax.ShapeDtypeStruct((4 * blocks * 8, 128), F32),
            jax.ShapeDtypeStruct((4 * blocks * 8, 128), F32),
            jax.ShapeDtypeStruct((6, 256, 512), BF16),
        ],
        in_specs=[on_smem()] + [on_vmem()] * 5,
        out_specs=[on_vmem()] * 3,
        compiler_params=params(),
        name="factors_and_weights",
    )(me, *facs, transfers)

    piece = jax.ShapeDtypeStruct((blocks // 2, quarter, 128), BF16)
    homes = []
    for half in range(2):
        pieces = pl.pallas_call(
            functools.partial(middle_kernel, dims, half),
            out_shape=[piece] * 4,
            in_specs=[on_smem(), on_smem()] + [on_vmem()] * 4,
            out_specs=[on_vmem()] * 4,
            scratch_shapes=[
                pltpu.VMEM((2 * blocks, quarter, 128), BF16),
                pltpu.VMEM((2 * blocks, quarter, 128), BF16),
            ],
            compiler_params=params(),
            name="middle_levels",
        )(me, level_bits, arrived, *prepared)
        homes.append(
            [lax.ppermute(pieces[j], AXES, [(s, swapped(s, j)) for s in range(devices)]) for j in range(4)]
        )

    spare, _, _ = spare_bit(level_bits, dims)
    leaf_of = receiver_slot // LEAF
    low = leaf_of & (lax.shift_left(1, spare) - 1)
    packed = ((leaf_of >> (spare + 1)) << spare) | low
    half_of = (leaf_of >> spare) & 1
    slots = half_of * (points // 2) + packed * LEAF + receiver_slot % LEAF

    done = pl.pallas_call(
        functools.partial(first_receivers, dims),
        out_shape=jax.ShapeDtypeStruct((points // 2, twice_rhs), BF16),
        in_specs=[on_smem(), on_smem()] + [on_vmem()] * 5,
        out_specs=on_vmem(),
        scratch_shapes=[pltpu.VMEM((STACKS, 2 * rhs, 128), BF16)],
        compiler_params=params(),
        name="first_receivers",
    )(me, level_bits, receiver_interp, *homes[0])
    return pl.pallas_call(
        functools.partial(last_receivers, dims),
        out_shape=jax.ShapeDtypeStruct((points, twice_rhs), BF16),
        in_specs=[on_smem(), on_smem(), on_smem()] + [on_vmem()] * 6,
        out_specs=on_vmem(),
        scratch_shapes=[pltpu.VMEM((points, 128), F32), pltpu.VMEM((STACKS, 2 * rhs, 128), BF16)],
        compiler_params=params(),
        name="last_receivers",
    )(me, level_bits, slots, receiver_interp, *homes[1], done)


def solution(mesh):
    body = functools.partial(per_device, mesh.shape["hi"], mesh.shape["lo"])
    return jax.shard_map(
        body,
        mesh=mesh,
        in_specs=(
            P(AXES, None),
            P(AXES),
            P(AXES, None),
            P(AXES, None, None),
            P(),
            P(),
            P(AXES, None),
            P(AXES),
        ),
        out_specs=P(AXES, None),
        check_vma=False,
    )
```

time: 216 us -> 153 us (0.71)
  Pallas kernels: 96.8 us -> 49 us
  waiting for transfers between devices: 90.1 us -> 62.5 us
  local copies, waits for them, and re-layouts: 6.69 us -> 14.1 us
  between operations: 0.08 us -> 2.66 us
  starting transfers between devices: 21.7 us -> 24.1 us
    pallas_call x2 -> x5, Pallas kernels: 59.8 us -> 33.6 us  [the longest x2 14.7 us: per_device(): pl.pallas_call(functools.partial(middle_kernel, dims, half), out_shape=[p...]
    pallas_call x1, Pallas kernels: 37 us -> 15.4 us  [per_device(): pl.pallas_call(functools.partial(source_kernel, dims), out_shape=jax.Shap...]
    ppermute x4 -> x8, waiting for transfers between devices: 42.9 us -> 22.1 us  [per_device(): lax.ppermute(pieces[j], AXES, [(s, swapped(s, j)) for s in range(devices)])]
    all_to_all x1, waiting for transfers between devices: 17 us -> 10.1 us  [per_device(): lax.all_to_all(sent, AXES, split_axis=0, concat_axis=0, tiled=True)]
    unnamed x18 -> x26, local copies, waits for them, and re-layouts: 5.01 us -> 11.8 us
    ppermute x4 -> x8, starting transfers between devices: 6.63 us -> 8.98 us  [per_device(): lax.ppermute(pieces[j], AXES, [(s, swapped(s, j)) for s in range(devices)])]
  transfers between devices with their start and end apart: 9 -> 13, of which waited for: 5 -> 9; matrix products, arithmetic and copies ran while one was open for 0% -> 1% of each run, Pallas kernels for 17% -> 20%
where the time goes in v2:
time: 153 us
  waiting for transfers between devices  62.5 us (41%)
  Pallas kernels  49 us (32%)
  starting transfers between devices  24.1 us (16%)
  local copies, waits for them, and re-layouts  14.1 us (9%)
  between operations  2.66 us (2%)
    ppermute x3, waiting for transfers between devices, per_device(): lax.ppermute(spread, AXES, [(s, s ^ mask) for s in range(devices)])  30.2 us
    ppermute x8, waiting for transfers between devices, per_device(): lax.ppermute(pieces[j], AXES, [(s, swapped(s, j)) for s in range(devices)])  22.1 us
    pallas_call x1, Pallas kernels, per_device(): pl.pallas_call(functools.partial(source_kernel, dims), out_shape=jax.Shap...  15.4 us
    pallas_call x2, Pallas kernels, per_device(): pl.pallas_call(functools.partial(middle_kernel, dims, half), out_shape=[p...  14.7 us
    pallas_call x1, Pallas kernels, per_device(): pl.pallas_call(functools.partial(last_receivers, dims), out_shape=jax.Sha...  12 us
    unnamed x26, local copies, waits for them, and re-layouts  11.8 us
    all_to_all x1, waiting for transfers between devices, per_device(): lax.all_to_all(sent, AXES, split_axis=0, concat_axis=0, tiled=True)  10.1 us
    ppermute x8, starting transfers between devices, per_device(): lax.ppermute(pieces[j], AXES, [(s, swapped(s, j)) for s in range(devices)])  8.98 us
  transfers between devices with their start and end apart: 13, of which 9 were waited for; matrix products, arithmetic and copies ran while one was open for 1% of the time, Pallas kernels for 20%

profile of v2, /device:TPU:1, one launch (start us, length us, event | category | flops | bytes accessed | tf_op | source)
XLA Modules:
  0.0 152.6 jit_solution(10379348516058463022)
XLA Ops:
  0.0 1.7 %copy.9 = bf16[4,2,2,2,4,8,128]{6,5,4,3,2,1,0:T(8,128)(2,1)} copy(bf16[4,2,2,2,4,8,128]{6,5,4,1,2,3,0:T(8,128)(2,1)} %bitcast.10) | data formatting | bytes 524288 | tf_op jit(solution)/shard_map/transpose | solution.py:346
  1.7 7.1 %all-to-all-start.1 = ((bf16[128,8,128]{2,1,0:T(8,128)(2,1)}), bf16[128,8,128]{2,1,0:T(8,128)(2,1)S(1)}, u32[]{:S(2)}, u32[]{:S(2)}) async-start(bf16[128,8,128]{2,1,0:T(8,128)(2,1)} %bitcast.7), calls=%async_computation.1 | async-start | bytes 524288 | tf_op jit(solution)/shard_map/all_to_all | solution.py:347
  8.8 0.0 copy-start.5
  8.8 1.0 copy-done.5
  9.8 1.6 %copy-done.7 = bf16[8192,128]{1,0:T(8,128)(2,1)S(1)} copy-done((bf16[8192,128]{1,0:T(8,128)(2,1)S(1)}, bf16[8192,128]{1,0:T(8,128)(2,1)}, u32[]{:S(2)}) %copy-start.7) | copy-done | bytes 2097176
  11.4 0.9 copy-done.8
  12.4 0.8 copy-done.9
  13.1 0.7 copy-done.10
  13.8 15.4 %source_side.1 = bf16[512,16,128]{2,1,0:T(8,128)(2,1)S(1)} custom-call(s32[8192]{0:T(1024)S(1)} %copy-done.9, s32[4]{0:T(128)S(1)} %copy-done.10, bf16[8192,128]{1,0:T(8,128)(2,1)S(1)} %copy-done.7, bf16[8192,128]{1,0:T(8,128)(2,1)} %si_hbm.1, bf16[1024,128]{1,0:T(8,128)(2,1)S(1)} %bitcast.11, bf16[8,2,2,64,128]{4,3,2,1,0:T(8,128)(2,1)S(1)} %copy-done.5), custom_call_target="tpu_custom_call" | custom-call | tf_op jit(solution)/shard_map/source_side/pallas_call | solution.py:354
  29.2 0.0 copy-start
  29.2 1.3 copy-done
  30.5 0.0 all-to-all-done.1
  30.5 5.8 %all-to-all-start = ((bf16[512,16,128]{2,1,0:T(8,128)(2,1)}), bf16[512,16,128]{2,1,0:T(8,128)(2,1)S(1)}, u32[]{:S(2)}, u32[]{:S(2)}) async-start(bf16[512,16,128]{2,1,0:T(8,128)(2,1)} %copy-done), calls=%async_computation | async-start | bytes 4194304 | tf_op jit(solution)/shard_map/all_to_all | solution.py:376
  36.4 0.3 collective-permute-start
  36.7 1.5 collective-permute-start.1
  38.2 0.4 collective-permute-start.2
  38.6 0.1 pad_add_fusion.me_ref
  38.7 0.0 collective-permute-done.f1
  38.7 20.3 %collective-permute-done.1.f2 = bf16[1024,128]{1,0:T(8,128)(2,1)S(1)} collective-permute-done((bf16[1024,128]{1,0:T(8,128)(2,1)S(1)}, bf16[1024,128]{1,0:T(8,128)(2,1)S(1)}, u32[]{:S(2)}, u32[]{:S(2)}) %collective-permute-start.1) | collective-permute-done | bytes 262176 | tf_op jit(solution)/shard_map/ppermute | solution.py:352
  59.0 9.9 %collective-permute-done.2.f3 = bf16[1024,128]{1,0:T(8,128)(2,1)} collective-permute-done((bf16[1024,128]{1,0:T(8,128)(2,1)S(1)}, bf16[1024,128]{1,0:T(8,128)(2,1)}, u32[]{:S(2)}, u32[]{:S(2)}) %collective-permute-start.2) | collective-permute-done | bytes 262176 | tf_op jit(solution)/shard_map/ppermute | solution.py:352
  68.9 4.4 %factors_and_weights.1 = (f32[4096,128]{1,0:T(8,128)S(1)}, f32[4096,128]{1,0:T(8,128)}, bf16[6,256,512]{2,1,0:T(8,128)(2,1)S(1)}) custom-call(s32[3]{0:T(128)S(1)} %pad_add_fusion.me_ref, bf16[1024,128]{1,0:T(8,128)(2,1)S(1)} %bitcast.15, bf16[1024,128]{1,0:T(8,128)(2,1)S(1)} %collective-permute-done.f1, bf16[1024,128]{1,0:T(8,128)(2,1)S(1)} %collective-permute-done.1.f2, ...), custom_call_target="tpu_custom_call" | custom-call | tf_op jit(solution)/shard_map/factors_and_weights/pallas_call | solution.py:378
  73.3 1.3 copy-done.2
  74.6 1.2 copy-done.3
  75.8 10.1 %all-to-all-done.g_ref = bf16[512,16,128]{2,1,0:T(8,128)(2,1)S(1)} async-done(((bf16[512,16,128]{2,1,0:T(8,128)(2,1)}), bf16[512,16,128]{2,1,0:T(8,128)(2,1)S(1)}, u32[]{:S(2)}, u32[]{:S(2)}) %all-to-all-start) | async-done | bytes 2097184 | tf_op jit(solution)/shard_map/all_to_all | solution.py:376
  85.9 1.4 copy-done.4
  87.3 6.8 %middle_levels.3 = (bf16[64,16,128]{2,1,0:T(8,128)(2,1)S(1)}, bf16[64,16,128]{2,1,0:T(8,128)(2,1)S(1)}, bf16[64,16,128]{2,1,0:T(8,128)(2,1)S(1)}, bf16[64,16,128]{2,1,0:T(8,128)(2,1)S(1)}) custom-call(s32[3]{0:T(128)S(1)} %pad_add_fusion.me_ref, s32[4]{0:T(128)S(1)} %copy-done.11, bf16[512,16,128]{2,1,0:T(8,128)(2,1)S(1)} %all-to-all-done.g_ref, ...), custom_call_target="tpu_custom_call" | custom-call | tf_op jit(solution)/shard_map/middle_levels/pallas_call | solution.py:394
  94.1 1.0 collective-permute-start.10
  95.2 1.9 %collective-permute-start.7 = (bf16[64,16,128]{2,1,0:T(8,128)(2,1)S(1)}, bf16[64,16,128]{2,1,0:T(8,128)(2,1)S(1)}, u32[]{:S(2)}, u32[]{:S(2)}) collective-permute-start(bf16[64,16,128]{2,1,0:T(8,128)(2,1)S(1)} %get-tuple-element.23), channel_id=1, source_target_pairs={{0,0},{1,4},{2,2},{3,6},{4,1},{5,5},{6,3},{7,7},{8,8},{9,12},{10,1... | collective-permute-start | bytes 786440 | tf_op jit(solution)/shard_map/ppermute | solution.py:407
  97.1 0.2 collective-permute-start.8
  97.4 0.0 copy-start.12
  97.4 3.6 %collective-permute-start.9 = (bf16[64,16,128]{2,1,0:T(8,128)(2,1)S(1)}, bf16[64,16,128]{2,1,0:T(8,128)(2,1)S(1)}, u32[]{:S(2)}, u32[]{:S(2)}) collective-permute-start(bf16[64,16,128]{2,1,0:T(8,128)(2,1)S(1)} %get-tuple-element.25), channel_id=1, source_target_pairs={{0,16},{1,20},{2,18},{3,22},{4,17},{5,21},{6,19},{7,23},{8,24},{9,... | collective-permute-start | bytes 786440 | tf_op jit(solution)/shard_map/ppermute | solution.py:407
  101.0 7.9 %middle_levels.2 = (bf16[64,16,128]{2,1,0:T(8,128)(2,1)}, bf16[64,16,128]{2,1,0:T(8,128)(2,1)}, bf16[64,16,128]{2,1,0:T(8,128)(2,1)}, bf16[64,16,128]{2,1,0:T(8,128)(2,1)}) custom-call(s32[3]{0:T(128)S(1)} %pad_add_fusion.me_ref, s32[4]{0:T(128)S(1)} %copy-done.11, bf16[512,16,128]{2,1,0:T(8,128)(2,1)S(1)} %all-to-all-done.g_ref, f32[4096,128]{1,0:T(8,128)} %copy-done.2, ...), custom_call_target="tpu_custom_call" | custom-call | tf_op jit(solution)/shard_map/middle_levels/pallas_call | solution.py:394
  108.9 1.9 %collective-permute-start.3 = (bf16[64,16,128]{2,1,0:T(8,128)(2,1)}, bf16[64,16,128]{2,1,0:T(8,128)(2,1)S(1)}, u32[]{:S(2)}, u32[]{:S(2)}) collective-permute-start(bf16[64,16,128]{2,1,0:T(8,128)(2,1)} %get-tuple-element.19), channel_id=1, source_target_pairs={{0,0},{1,4},{2,2},{3,6},{4,1},{5,5},{6,3},{7,7},{8,8},{9,12},{10,1... | collective-permute-start | bytes 786440 | tf_op jit(solution)/shard_map/ppermute | solution.py:407
  110.8 0.3 collective-permute-done.10.p3
  111.2 0.2 collective-permute-start.4
  111.4 8.0 %collective-permute-done.7.p0 = bf16[64,16,128]{2,1,0:T(8,128)(2,1)S(1)} collective-permute-done((bf16[64,16,128]{2,1,0:T(8,128)(2,1)S(1)}, bf16[64,16,128]{2,1,0:T(8,128)(2,1)S(1)}, u32[]{:S(2)}, u32[]{:S(2)}) %collective-permute-start.7) | collective-permute-done | bytes 262176 | tf_op jit(solution)/shard_map/ppermute | solution.py:407
  119.4 0.0 collective-permute-start.5
  119.4 3.1 %collective-permute-done.8.p1 = bf16[64,16,128]{2,1,0:T(8,128)(2,1)S(1)} collective-permute-done((bf16[64,16,128]{2,1,0:T(8,128)(2,1)S(1)}, bf16[64,16,128]{2,1,0:T(8,128)(2,1)S(1)}, u32[]{:S(2)}, u32[]{:S(2)}) %collective-permute-start.8) | collective-permute-done | bytes 262176 | tf_op jit(solution)/shard_map/ppermute | solution.py:407
  122.5 0.0 collective-permute-start.6
  122.5 0.7 fusion.5
  125.8 4.8 %collective-permute-done.9.p2 = bf16[64,16,128]{2,1,0:T(8,128)(2,1)S(1)} collective-permute-done((bf16[64,16,128]{2,1,0:T(8,128)(2,1)S(1)}, bf16[64,16,128]{2,1,0:T(8,128)(2,1)S(1)}, u32[]{:S(2)}, u32[]{:S(2)}) %collective-permute-start.9) | collective-permute-done | bytes 262176 | tf_op jit(solution)/shard_map/ppermute | solution.py:407
  130.6 1.6 %copy-done.1 = bf16[8192,128]{1,0:T(8,128)(2,1)S(1)} copy-done((bf16[8192,128]{1,0:T(8,128)(2,1)S(1)}, bf16[8192,128]{1,0:T(8,128)(2,1)}, u32[]{:S(2)}) %copy-start.1) | copy-done | bytes 2097176
  132.2 2.5 %first_receivers.1.done_ref = bf16[4096,128]{1,0:T(8,128)(2,1)S(1)} custom-call(s32[3]{0:T(128)S(1)} %pad_add_fusion.me_ref, s32[4]{0:T(128)S(1)} %copy-done.11, bf16[8192,128]{1,0:T(8,128)(2,1)S(1)} %copy-done.1, bf16[64,16,128]{2,1,0:T(8,128)(2,1)S(1)} %collective-permute-done.7.p0, bf16[64,16,128]{2,1,0:T(8,128)(2,1)S(1)} %collective-permute-done.8.p1, ...), custom_call_target="tpu_custom_call" | custom-call | tf_op jit(solution)/shard_map/first_receivers/pallas_call | solution.py:417
  134.7 1.5 %collective-permute-done.3.p0 = bf16[64,16,128]{2,1,0:T(8,128)(2,1)S(1)} collective-permute-done((bf16[64,16,128]{2,1,0:T(8,128)(2,1)}, bf16[64,16,128]{2,1,0:T(8,128)(2,1)S(1)}, u32[]{:S(2)}, u32[]{:S(2)}) %collective-permute-start.3) | collective-permute-done | bytes 262176 | tf_op jit(solution)/shard_map/ppermute | solution.py:407
  136.3 0.0 collective-permute-done.4.p1
  136.3 4.3 %collective-permute-done.5.p2 = bf16[64,16,128]{2,1,0:T(8,128)(2,1)S(1)} collective-permute-done((bf16[64,16,128]{2,1,0:T(8,128)(2,1)}, bf16[64,16,128]{2,1,0:T(8,128)(2,1)S(1)}, u32[]{:S(2)}, u32[]{:S(2)}) %collective-permute-start.5) | collective-permute-done | bytes 262176 | tf_op jit(solution)/shard_map/ppermute | solution.py:407
  140.6 0.0 collective-permute-done.6.p3
  140.6 12.0 %last_receivers.1 = bf16[8192,128]{1,0:T(8,128)(2,1)} custom-call(s32[3]{0:T(128)S(1)} %pad_add_fusion.me_ref, s32[4]{0:T(128)S(1)} %copy-done.11, s32[8192]{0:T(1024)S(1)} %fusion.slot_ref, bf16[8192,128]{1,0:T(8,128)(2,1)S(1)} %copy-done.1, bf16[64,16,128]{2,1,0:T(8,128)(2,1)S(1)} %collective-permute-done.3.p0, ...), custom_call_target="tpu_custom_call" | custom-call | tf_op jit(solution)/shard_map/last_receivers/pallas_call | solution.py:426
  (14 shorter events, 0.1 us)
Async XLA Ops:
  1.7 28.8 %all-to-all-start.1 = ((bf16[128,8,128]{2,1,0:T(8,128)(2,1)}), bf16[128,8,128]{2,1,0:T(8,128)(2,1)S(1)}, u32[]{:S(2)}, u32[]{:S(2)}) async-start(bf16[128,8,128]{2,1,0:T(8,128)(2,1)} %bitcast.7), calls=%async_computation.1 | async-start | bytes 524288 | tf_op jit(solution)/shard_map/all_to_all | solution.py:347
  8.8 1.0 copy-start.5
  9.8 1.6 %copy-start.7 = (bf16[8192,128]{1,0:T(8,128)(2,1)S(1)}, bf16[8192,128]{1,0:T(8,128)(2,1)}, u32[]{:S(2)}) copy-start(bf16[8192,128]{1,0:T(8,128)(2,1)} %ch_hbm.1) | copy-start | bytes 6291460
  11.4 0.9 copy-start.8
  12.4 0.8 copy-start.9
  13.1 0.7 copy-start.10
  29.2 1.3 copy-start
  30.5 38.4 %copy-start.6 = (bf16[8,2,2,64,128]{4,3,2,1,0:T(8,128)(2,1)S(1)}, bf16[8,2,2,64,128]{4,3,2,1,0:T(8,128)(2,1)}, u32[]{:S(2)}) copy-start(bf16[8,2,2,64,128]{4,3,2,1,0:T(8,128)(2,1)} %tr_ref.1) | copy-start | bytes 1572868
  30.5 55.4 %copy-start.11 = (s32[4]{0:T(128)S(1)}, s32[4]{0:T(128)}, u32[]{:S(2)}) copy-start(s32[4]{0:T(128)} %bits_ref.9) | copy-start | bytes 52
  30.5 55.4 %all-to-all-start = ((bf16[512,16,128]{2,1,0:T(8,128)(2,1)}), bf16[512,16,128]{2,1,0:T(8,128)(2,1)S(1)}, u32[]{:S(2)}, u32[]{:S(2)}) async-start(bf16[512,16,128]{2,1,0:T(8,128)(2,1)} %copy-done), calls=%async_computation | async-start | bytes 4194304 | tf_op jit(solution)/shard_map/all_to_all | solution.py:376
  36.4 2.3 %collective-permute-start = (bf16[1024,128]{1,0:T(8,128)(2,1)S(1)}, bf16[1024,128]{1,0:T(8,128)(2,1)S(1)}, u32[]{:S(2)}, u32[]{:S(2)}) collective-permute-start(bf16[1024,128]{1,0:T(8,128)(2,1)S(1)} %bitcast.12), channel_id=1, source_target_pairs={{0,1},{1,0},{2,3},{3,2},{4,5},{5,4},{6,7},{7,6},{8,9},{9,8},{10,11... | collective-permute-start | bytes 786440 | tf_op jit(solution)/shard_map/ppermute | solution.py:352
  36.7 22.3 %collective-permute-start.1 = (bf16[1024,128]{1,0:T(8,128)(2,1)S(1)}, bf16[1024,128]{1,0:T(8,128)(2,1)S(1)}, u32[]{:S(2)}, u32[]{:S(2)}) collective-permute-start(bf16[1024,128]{1,0:T(8,128)(2,1)S(1)} %bitcast.13), channel_id=1, source_target_pairs={{0,16},{1,17},{2,18},{3,19},{4,20},{5,21},{6,22},{7,23},{8,24},{9,... | collective-permute-start | bytes 786440 | tf_op jit(solution)/shard_map/ppermute | solution.py:352
  38.2 30.7 %collective-permute-start.2 = (bf16[1024,128]{1,0:T(8,128)(2,1)S(1)}, bf16[1024,128]{1,0:T(8,128)(2,1)}, u32[]{:S(2)}, u32[]{:S(2)}) collective-permute-start(bf16[1024,128]{1,0:T(8,128)(2,1)S(1)} %bitcast.14), channel_id=1, source_target_pairs={{0,17},{1,16},{2,19},{3,18},{4,21},{5,20},{6,23},{7,22},{8,25},{9,... | collective-permute-start | bytes 786440 | tf_op jit(solution)/shard_map/ppermute | solution.py:352
  73.3 1.3 copy-start.2
  74.6 1.2 copy-start.3
  85.9 1.4 copy-start.4
  94.1 17.0 %collective-permute-start.10 = (bf16[64,16,128]{2,1,0:T(8,128)(2,1)S(1)}, bf16[64,16,128]{2,1,0:T(8,128)(2,1)S(1)}, u32[]{:S(2)}, u32[]{:S(2)}) collective-permute-start(bf16[64,16,128]{2,1,0:T(8,128)(2,1)S(1)} %get-tuple-element.26), channel_id=1, source_target_pairs={{0,20},{1,16},{2,22},{3,18},{4,21},{5,17},{6,23},{7,19},{8,28},{9,... | collective-permute-start | bytes 786440 | tf_op jit(solution)/shard_map/ppermute | solution.py:407
  95.2 24.2 %collective-permute-start.7 = (bf16[64,16,128]{2,1,0:T(8,128)(2,1)S(1)}, bf16[64,16,128]{2,1,0:T(8,128)(2,1)S(1)}, u32[]{:S(2)}, u32[]{:S(2)}) collective-permute-start(bf16[64,16,128]{2,1,0:T(8,128)(2,1)S(1)} %get-tuple-element.23), channel_id=1, source_target_pairs={{0,0},{1,4},{2,2},{3,6},{4,1},{5,5},{6,3},{7,7},{8,8},{9,12},{10,1... | collective-permute-start | bytes 786440 | tf_op jit(solution)/shard_map/ppermute | solution.py:407
  97.1 25.4 %collective-permute-start.8 = (bf16[64,16,128]{2,1,0:T(8,128)(2,1)S(1)}, bf16[64,16,128]{2,1,0:T(8,128)(2,1)S(1)}, u32[]{:S(2)}, u32[]{:S(2)}) collective-permute-start(bf16[64,16,128]{2,1,0:T(8,128)(2,1)S(1)} %get-tuple-element.24), channel_id=1, source_target_pairs={{0,4},{1,0},{2,6},{3,2},{4,5},{5,1},{6,7},{7,3},{8,12},{9,8},{10,1... | collective-permute-start | bytes 786440 | tf_op jit(solution)/shard_map/ppermute | solution.py:407
  97.4 28.4 %copy-start.12 = (s32[8192]{0:T(1024)S(1)}, s32[8192]{0:T(1024)}, u32[]{:S(2)}) copy-start(s32[8192]{0:T(1024)} %param.15) | copy-start | bytes 98308
  97.4 33.3 %collective-permute-start.9 = (bf16[64,16,128]{2,1,0:T(8,128)(2,1)S(1)}, bf16[64,16,128]{2,1,0:T(8,128)(2,1)S(1)}, u32[]{:S(2)}, u32[]{:S(2)}) collective-permute-start(bf16[64,16,128]{2,1,0:T(8,128)(2,1)S(1)} %get-tuple-element.25), channel_id=1, source_target_pairs={{0,16},{1,20},{2,18},{3,22},{4,17},{5,21},{6,19},{7,23},{8,24},{9,... | collective-permute-start | bytes 786440 | tf_op jit(solution)/shard_map/ppermute | solution.py:407
  108.9 27.4 %collective-permute-start.3 = (bf16[64,16,128]{2,1,0:T(8,128)(2,1)}, bf16[64,16,128]{2,1,0:T(8,128)(2,1)S(1)}, u32[]{:S(2)}, u32[]{:S(2)}) collective-permute-start(bf16[64,16,128]{2,1,0:T(8,128)(2,1)} %get-tuple-element.19), channel_id=1, source_target_pairs={{0,0},{1,4},{2,2},{3,6},{4,1},{5,5},{6,3},{7,7},{8,8},{9,12},{10,1... | collective-permute-start | bytes 786440 | tf_op jit(solution)/shard_map/ppermute | solution.py:407
  111.2 25.1 %collective-permute-start.4 = (bf16[64,16,128]{2,1,0:T(8,128)(2,1)}, bf16[64,16,128]{2,1,0:T(8,128)(2,1)S(1)}, u32[]{:S(2)}, u32[]{:S(2)}) collective-permute-start(bf16[64,16,128]{2,1,0:T(8,128)(2,1)} %get-tuple-element.20), channel_id=1, source_target_pairs={{0,4},{1,0},{2,6},{3,2},{4,5},{5,1},{6,7},{7,3},{8,12},{9,8},{10,1... | collective-permute-start | bytes 786440 | tf_op jit(solution)/shard_map/ppermute | solution.py:407
  119.4 21.1 %collective-permute-start.5 = (bf16[64,16,128]{2,1,0:T(8,128)(2,1)}, bf16[64,16,128]{2,1,0:T(8,128)(2,1)S(1)}, u32[]{:S(2)}, u32[]{:S(2)}) collective-permute-start(bf16[64,16,128]{2,1,0:T(8,128)(2,1)} %get-tuple-element.21), channel_id=1, source_target_pairs={{0,16},{1,20},{2,18},{3,22},{4,17},{5,21},{6,19},{7,23},{8,24},{9,... | collective-permute-start | bytes 786440 | tf_op jit(solution)/shard_map/ppermute | solution.py:407
  122.5 18.0 %collective-permute-start.6 = (bf16[64,16,128]{2,1,0:T(8,128)(2,1)}, bf16[64,16,128]{2,1,0:T(8,128)(2,1)S(1)}, u32[]{:S(2)}, u32[]{:S(2)}) collective-permute-start(bf16[64,16,128]{2,1,0:T(8,128)(2,1)} %get-tuple-element.22), channel_id=1, source_target_pairs={{0,20},{1,16},{2,22},{3,18},{4,21},{5,17},{6,23},{7,19},{8,28},{9,... | collective-permute-start | bytes 786440 | tf_op jit(solution)/shard_map/ppermute | solution.py:407
  130.6 1.6 %copy-start.1 = (bf16[8192,128]{1,0:T(8,128)(2,1)S(1)}, bf16[8192,128]{1,0:T(8,128)(2,1)}, u32[]{:S(2)}) copy-start(bf16[8192,128]{1,0:T(8,128)(2,1)} %ri_ref.3) | copy-start | bytes 6291460

commit v3 on v2

--- a/solution.py
+++ b/solution.py
@@ -183,23 +183,31 @@
     return lax.shift_left(lax.shift_right_logical(i, bit), bit + 1) | low | (value << bit)
 
 
-def prepare_kernel(dims, me_ref, f0, f1, f2, f3, tr_ref, fa, fb, w_ref):
-    blocks = dims[3]
-    for j, f_ref in enumerate((f0, f1, f2, f3)):
-        split_factors(lambda at, f_ref=f_ref: f_ref[pl.ds(at, 16), :], fa, fb, j * blocks * 8, blocks * 8)
-    for index in range(4):
-        build_weights(w_ref, index, tr_ref, index + 2)
-    build_weights(w_ref, 4, tr_ref, 6, me_ref[1])
-    build_weights(w_ref, 5, tr_ref, 7, me_ref[0])
-
-
-def middle_kernel(dims, half, me_ref, bits_ref, g_ref, fa, fb, w_ref, o0, o1, o2, o3, x, x2):
+def middle_kernel(dims, half, me_ref, bits_ref, g_ref, f0, f1, f2, f3, tr_ref, o0, o1, o2, o3, x, x2, fa, fb, w_ref):
     n_hi, n_lo, share, blocks, rhs = dims
     quarter = rhs // 4
     st = log2(share)
     y, core = me_ref[0], me_ref[1]
     spare, inner, outer = spare_bit(bits_ref, dims)
     count = blocks // 2
+    for index in range(4):
+        build_weights(w_ref, index, tr_ref, index + 2)
+    build_weights(w_ref, 4, tr_ref, 6, core)
+    build_weights(w_ref, 5, tr_ref, 7, y)
+    low = lanes_low((8, 128))
+    for j, f_ref in enumerate((f0, f1, f2, f3)):
+
+        def split(step, carry, j=j, f_ref=f_ref):
+            for part in range(32):
+                i = step * 32 + part
+                fac = f_ref[with_bit(i, spare, half)].astype(F32)
+                turned = roll64(fac)
+                rows = pl.ds(pl.multiple_of((j * count + i) * 8, 8), 8)
+                fa[rows, :] = jnp.where(low, fac, turned)
+                fb[rows, :] = jnp.where(low, -turned, fac)
+            return carry
+
+        lax.fori_loop(0, count // 32, split, 0)
 
     def read_arrived(j, i):
         n = with_bit(i, spare, half)
@@ -220,20 +228,18 @@
     def level(index, bit, read, x):
         packed = bit - (bit > spare).astype(jnp.int32)
         ends = [pair_of(k, packed) for k in range(count // 2)]
-        homes = [tuple(with_bit(i, spare, half) * 8 + index for i in pair) for pair in ends]
         for j in range(4):
             lhs = jnp.concatenate([jnp.concatenate([read(j, a), read(j, b)], axis=1) for a, b in ends], axis=0)
             res = jnp.dot(lhs, w_ref[index - 2], preferred_element_type=F32)
             for p in range(count // 2):
                 for c in range(2):
-                    x[j * count + ends[p][c]] = finish(res, p, c, j * blocks * 8 + homes[p][c])
+                    n = j * count + ends[p][c]
+                    x[n] = finish(res, p, c, n * 8 + index)
 
     level(2, inner, read_arrived, x)
     level(3, outer, held(x), x2)
     level(4, bits_ref[2], held(x2), x)
     level(5, bits_ref[3], held(x), x2)
-
-    homes = [with_bit(i, spare, half) * 8 for i in range(count)]
 
     def across(index, x, pairs, outs):
         for (a, b), (out_a, out_b) in zip(pairs, outs):
@@ -243,7 +249,7 @@
             res = jnp.dot(lhs, w_ref[index - 2], preferred_element_type=F32)
             for p in range(count):
                 for c, (j, out) in enumerate(((a, out_a), (b, out_b))):
-                    out[p] = finish(res, p, c, j * blocks * 8 + homes[p] + index)
+                    out[p] = finish(res, p, c, (j * count + p) * 8 + index)
 
     rest = [x.at[pl.ds(j * count, count)] for j in range(4)]
     across(6, x2, ((0, 1), (2, 3)), ((rest[0], rest[1]), (rest[2], rest[3])))
@@ -270,15 +276,15 @@
             result = lax.dot_general(
                 ri_ref[rows, :], stack[part], (((1,), (1,)), ((), ())), preferred_element_type=F32
             )
-            store(pl.multiple_of(i * LEAF, LEAF), result)
+            store(i, rows, result)
         return carry
 
     lax.fori_loop(0, blocks // 2 // STACKS, values, 0)
 
 
 def first_receivers(dims, me_ref, bits_ref, ri_ref, p0, p1, p2, p3, out_ref, stack):
-    def store(at, result):
-        out_ref[pl.ds(at, LEAF), :] = result.astype(BF16)
+    def store(i, rows, result):
+        out_ref[pl.ds(pl.multiple_of(i * LEAF, LEAF), LEAF), :] = result.astype(BF16)
 
     receiver_values(dims, 0, me_ref, bits_ref, ri_ref, (p0, p1, p2, p3), stack, store)
 
@@ -287,15 +293,19 @@
     blocks = dims[3]
     points = blocks * LEAF
 
-    def store(at, result):
-        t32[pl.ds(points // 2 + at, LEAF), :] = result
+    spare, _, _ = spare_bit(bits_ref, dims)
+
+    def store(i, rows, result):
+        t32[rows, :] = result
 
     def widen(step, carry):
-        rows = pl.ds(pl.multiple_of(step * 512, 512), 512)
-        t32[rows, :] = done_ref[rows, :].astype(F32)
-        return carry
-
-    lax.fori_loop(0, points // 2 // 512, widen, 0)
+        for part in range(STACKS):
+            i = step * STACKS + part
+            held = done_ref[pl.ds(pl.multiple_of(i * LEAF, LEAF), LEAF), :]
+            t32[pl.ds(pl.multiple_of(with_bit(i, spare, 0) * LEAF, LEAF), LEAF), :] = held.astype(F32)
+        return carry
+
+    lax.fori_loop(0, blocks // 2 // STACKS, widen, 0)
     receiver_values(dims, 1, me_ref, bits_ref, ri_ref, (p0, p1, p2, p3), stack, store)
 
     def pick(step, carry):
@@ -319,8 +329,8 @@
     return pl.BlockSpec(memory_space=pltpu.SMEM)
 
 
-def params():
-    return pltpu.CompilerParams(vmem_limit_bytes=48 * 2**20)
+def params(mebibytes):
+    return pltpu.CompilerParams(vmem_limit_bytes=mebibytes * 2**20)
 
 
 def per_device(
@@ -335,7 +345,7 @@
     dims = (n_hi, n_lo, share, blocks, rhs)
     half_hi, half_lo = n_hi // 2 * n_lo, n_lo // 2
     hi, lo = lax.axis_index("hi"), lax.axis_index("lo")
-    me = jnp.stack([hi >> (log2(n_hi) - 1), lo & 1, lo >> (log2(n_lo) - 1)]).astype(jnp.int32)
+    me = jnp.stack([hi >> (log2(n_hi) - 1), lo & 1, lo >> (log2(n_lo) - 1), hi, lo]).astype(jnp.int32)
 
     def swapped(device, j):
         flipped = device ^ (half_hi if j >> 1 else 0)
@@ -345,7 +355,6 @@
 
     spread = factors.reshape(n_hi, 2, n_lo // 4, 2, share, 8, 128).transpose(0, 3, 2, 1, 4, 5, 6)
     spread = lax.all_to_all(spread.reshape(blocks, 8, 128), AXES, split_axis=0, concat_axis=0, tiled=True)
-    spread = spread.reshape(blocks * 8, 128)
     facs = [spread]
     for j in range(1, 4):
         mask = (half_hi if j >> 1 else 0) ^ (j & 1)
@@ -369,24 +378,11 @@
             pltpu.VMEM((blocks * 8, 128), F32),
             pltpu.VMEM((2, 256, 512), BF16),
         ],
-        compiler_params=params(),
+        compiler_params=params(60),
         name="source_side",
     )(source_order, level_bits, charges, source_interp, factors.reshape(blocks * 8, 128), transfers)
 
     arrived = lax.all_to_all(sent, AXES, split_axis=0, concat_axis=0, tiled=True)
-
-    prepared = pl.pallas_call(
-        functools.partial(prepare_kernel, dims),
-        out_shape=[
-            jax.ShapeDtypeStruct((4 * blocks * 8, 128), F32),
-            jax.ShapeDtypeStruct((4 * blocks * 8, 128), F32),
-            jax.ShapeDtypeStruct((6, 256, 512), BF16),
-        ],
-        in_specs=[on_smem()] + [on_vmem()] * 5,
-        out_specs=[on_vmem()] * 3,
-        compiler_params=params(),
-        name="factors_and_weights",
-    )(me, *facs, transfers)
 
     piece = jax.ShapeDtypeStruct((blocks // 2, quarter, 128), BF16)
     homes = []
@@ -394,25 +390,21 @@
         pieces = pl.pallas_call(
             functools.partial(middle_kernel, dims, half),
             out_shape=[piece] * 4,
-            in_specs=[on_smem(), on_smem()] + [on_vmem()] * 4,
+            in_specs=[on_smem(), on_smem()] + [on_vmem()] * 6,
             out_specs=[on_vmem()] * 4,
             scratch_shapes=[
                 pltpu.VMEM((2 * blocks, quarter, 128), BF16),
                 pltpu.VMEM((2 * blocks, quarter, 128), BF16),
+                pltpu.VMEM((2 * blocks * 8, 128), F32),
+                pltpu.VMEM((2 * blocks * 8, 128), F32),
+                pltpu.VMEM((6, 256, 512), BF16),
             ],
-            compiler_params=params(),
+            compiler_params=params(16),
             name="middle_levels",
-        )(me, level_bits, arrived, *prepared)
+        )(me, level_bits, arrived, *facs, transfers)
         homes.append(
             [lax.ppermute(pieces[j], AXES, [(s, swapped(s, j)) for s in range(devices)]) for j in range(4)]
         )
-
-    spare, _, _ = spare_bit(level_bits, dims)
-    leaf_of = receiver_slot // LEAF
-    low = leaf_of & (lax.shift_left(1, spare) - 1)
-    packed = ((leaf_of >> (spare + 1)) << spare) | low
-    half_of = (leaf_of >> spare) & 1
-    slots = half_of * (points // 2) + packed * LEAF + receiver_slot % LEAF
 
     done = pl.pallas_call(
         functools.partial(first_receivers, dims),
@@ -420,7 +412,7 @@
         in_specs=[on_smem(), on_smem()] + [on_vmem()] * 5,
         out_specs=on_vmem(),
         scratch_shapes=[pltpu.VMEM((STACKS, 2 * rhs, 128), BF16)],
-        compiler_params=params(),
+        compiler_params=params(16),
         name="first_receivers",
     )(me, level_bits, receiver_interp, *homes[0])
     return pl.pallas_call(
@@ -429,9 +421,9 @@
         in_specs=[on_smem(), on_smem(), on_smem()] + [on_vmem()] * 6,
         out_specs=on_vmem(),
         scratch_shapes=[pltpu.VMEM((points, 128), F32), pltpu.VMEM((STACKS, 2 * rhs, 128), BF16)],
-        compiler_params=params(),
+        compiler_params=params(20),
         name="last_receivers",
-    )(me, level_bits, slots, receiver_interp, *homes[1], done)
+    )(me, level_bits, receiver_slot, receiver_interp, *homes[1], done)
 
 
 def solution(mesh):

time: 153 us -> 151 us (0.987)
  waiting for transfers between devices: 62.5 us -> 75.2 us
  local copies, waits for them, and re-layouts: 14.1 us -> 1.79 us
  between operations: 2.66 us -> 0.14 us
  starting transfers between devices: 24.1 us -> 26.6 us
  Pallas kernels: 49 us -> 47.1 us
    unnamed x26 -> x8, local copies, waits for them, and re-layouts: 11.8 us -> 0.02 us
    all_to_all x1, waiting for transfers between devices: 10.1 us -> 17 us  [per_device(): lax.all_to_all(sent, AXES, split_axis=0, concat_axis=0, tiled=True)]
    ppermute x8, waiting for transfers between devices: 22.1 us -> 28 us  [per_device(): lax.ppermute(pieces[j], AXES, [(s, swapped(s, j)) for s in range(devices)])]
    pallas_call x1 -> x0, Pallas kernels: 4.4 us -> none  [per_device(): pl.pallas_call(functools.partial(prepare_kernel, dims), out_shape=[jax.Sh...]
    ppermute x8, starting transfers between devices: 8.98 us -> 11.4 us  [per_device(): lax.ppermute(pieces[j], AXES, [(s, swapped(s, j)) for s in range(devices)])]
    pallas_call x1, Pallas kernels: 15.4 us -> 17.2 us  [per_device(): pl.pallas_call(functools.partial(source_kernel, dims), out_shape=jax.Shap...]
    transpose x1 -> x0, local copies, waits for them, and re-layouts: 1.68 us -> none  [per_device(): factors.reshape(n_hi, 2, n_lo // 4, 2, share, 8, 128)]
    reshape x0 -> x1, local copies, waits for them, and re-layouts: none -> 1.68 us  [per_device(): factors.reshape(n_hi, 2, n_lo // 4, 2, share, 8, 128)]
  transfers between devices with their start and end apart: 13 -> 13, of which waited for: 9 -> 7; matrix products, arithmetic and copies ran while one was open for 1% -> 0% of each run, Pallas kernels for 20% -> 18%
where the time goes in v3:
time: 151 us
  waiting for transfers between devices  75.2 us (50%)
  Pallas kernels  47.1 us (31%)
  starting transfers between devices  26.6 us (18%)
  local copies, waits for them, and re-layouts  1.79 us (1%)
    ppermute x3, waiting for transfers between devices, per_device(): lax.ppermute(spread, AXES, [(s, s ^ mask) for s in range(devices)])  30.2 us
    ppermute x8, waiting for transfers between devices, per_device(): lax.ppermute(pieces[j], AXES, [(s, swapped(s, j)) for s in range(devices)])  28 us
    pallas_call x1, Pallas kernels, per_device(): pl.pallas_call(functools.partial(source_kernel, dims), out_shape=jax.Shap...  17.2 us
    all_to_all x1, waiting for transfers between devices, per_device(): lax.all_to_all(sent, AXES, split_axis=0, concat_axis=0, tiled=True)  17 us
    pallas_call x2, Pallas kernels, per_device(): pl.pallas_call(functools.partial(middle_kernel, dims, half), out_shape=[p...  15.2 us
    pallas_call x1, Pallas kernels, per_device(): pl.pallas_call(functools.partial(last_receivers, dims), out_shape=jax.Sha...  12.1 us
    ppermute x8, starting transfers between devices, per_device(): lax.ppermute(pieces[j], AXES, [(s, swapped(s, j)) for s in range(devices)])  11.4 us
    all_to_all x1, starting transfers between devices, per_device(): lax.all_to_all(spread.reshape(blocks, 8, 128), AXES, split_axis=0, concat...  7.1 us
  transfers between devices with their start and end apart: 13, of which 7 were waited for; matrix products, arithmetic and copies ran while one was open for 0% of the time, Pallas kernels for 18%

profile of v3, /device:TPU:1, one launch (start us, length us, event | category | flops | bytes accessed | tf_op | source)
XLA Modules:
  0.0 150.8 jit_solution(7227239547678188056)
XLA Ops:
  0.0 1.7 %copy.9 = bf16[4,2,2,2,4,8,128]{6,5,4,1,2,3,0:T(8,128)(2,1)} copy(bf16[4,2,2,2,4,8,128]{6,5,4,3,2,1,0:T(8,128)(2,1)} %bitcast.10) | data formatting | bytes 524288 | tf_op jit(solution)/shard_map/reshape | solution.py:356
  1.7 7.1 %all-to-all-start.1 = ((bf16[128,8,128]{2,1,0:T(8,128)(2,1)}), bf16[128,8,128]{2,1,0:T(8,128)(2,1)S(1)}, u32[]{:S(2)}, u32[]{:S(2)}) async-start(bf16[128,8,128]{2,1,0:T(8,128)(2,1)} %bitcast.8), calls=%async_computation.1 | async-start | bytes 524288 | tf_op jit(solution)/shard_map/all_to_all | solution.py:357
  8.8 17.2 %source_side.1 = bf16[512,16,128]{2,1,0:T(8,128)(2,1)} custom-call(s32[8192]{0:T(1024)} %order_ref.1, s32[4]{0:T(128)} %bits_ref.9, bf16[8192,128]{1,0:T(8,128)(2,1)} %ch_hbm.1, bf16[8192,128]{1,0:T(8,128)(2,1)} %si_hbm.1, bf16[1024,128]{1,0:T(8,128)(2,1)} %bitcast.11, bf16[8,2,2,64,128]{4,3,2,1,0:T(8,128)(2,1)} %tr_ref.3), custom_call_target="tpu_custom_call" | custom-call | tf_op jit(solution)/shard_map/source_side/pallas_call | solution.py:363
  26.0 0.0 copy-start.1
  26.0 0.0 copy-start.3
  26.1 0.0 all-to-all-done.1.f0
  26.1 5.8 %all-to-all-start = ((bf16[512,16,128]{2,1,0:T(8,128)(2,1)}), bf16[512,16,128]{2,1,0:T(8,128)(2,1)S(1)}, u32[]{:S(2)}, u32[]{:S(2)}) async-start(bf16[512,16,128]{2,1,0:T(8,128)(2,1)} %source_side.1), calls=%async_computation | async-start | bytes 4194304 | tf_op jit(solution)/shard_map/all_to_all | solution.py:385
  31.9 0.3 collective-permute-start
  32.2 1.5 collective-permute-start.1
  33.7 0.4 collective-permute-start.2
  34.1 0.1 stack.23.me_ref
  34.2 0.0 collective-permute-done.f1
  34.2 20.3 %collective-permute-done.1.f2 = bf16[128,8,128]{2,1,0:T(8,128)(2,1)S(1)} collective-permute-done((bf16[128,8,128]{2,1,0:T(8,128)(2,1)S(1)}, bf16[128,8,128]{2,1,0:T(8,128)(2,1)S(1)}, u32[]{:S(2)}, u32[]{:S(2)}) %collective-permute-start.1) | collective-permute-done | bytes 262176 | tf_op jit(solution)/shard_map/ppermute | solution.py:361
  54.5 9.9 %collective-permute-done.2.f3 = bf16[128,8,128]{2,1,0:T(8,128)(2,1)} collective-permute-done((bf16[128,8,128]{2,1,0:T(8,128)(2,1)S(1)}, bf16[128,8,128]{2,1,0:T(8,128)(2,1)}, u32[]{:S(2)}, u32[]{:S(2)}) %collective-permute-start.2) | collective-permute-done | bytes 262176 | tf_op jit(solution)/shard_map/ppermute | solution.py:361
  64.4 17.0 %all-to-all-done.g_ref = bf16[512,16,128]{2,1,0:T(8,128)(2,1)S(1)} async-done(((bf16[512,16,128]{2,1,0:T(8,128)(2,1)}), bf16[512,16,128]{2,1,0:T(8,128)(2,1)S(1)}, u32[]{:S(2)}, u32[]{:S(2)}) %all-to-all-start) | async-done | bytes 2097184 | tf_op jit(solution)/shard_map/all_to_all | solution.py:385
  81.4 0.0 copy-done.1
  81.4 0.0 copy-done.3
  81.4 7.6 %middle_levels.3 = (bf16[64,16,128]{2,1,0:T(8,128)(2,1)S(1)}, bf16[64,16,128]{2,1,0:T(8,128)(2,1)S(1)}, bf16[64,16,128]{2,1,0:T(8,128)(2,1)S(1)}, bf16[64,16,128]{2,1,0:T(8,128)(2,1)S(1)}) custom-call(s32[5]{0:T(128)S(1)} %stack.23.me_ref, s32[4]{0:T(128)S(1)} %copy-done.3, bf16[512,16,128]{2,1,0:T(8,128)(2,1)S(1)} %all-to-all-done.g_ref, ...), custom_call_target="tpu_custom_call" | custom-call | tf_op jit(solution)/shard_map/middle_levels/pallas_call | solution.py:390
  89.0 0.0 copy-start
  89.0 2.1 %collective-permute-start.7 = (bf16[64,16,128]{2,1,0:T(8,128)(2,1)S(1)}, bf16[64,16,128]{2,1,0:T(8,128)(2,1)S(1)}, u32[]{:S(2)}, u32[]{:S(2)}) collective-permute-start(bf16[64,16,128]{2,1,0:T(8,128)(2,1)S(1)} %get-tuple-element.17), channel_id=1, source_target_pairs={{0,0},{1,4},{2,2},{3,6},{4,1},{5,5},{6,3},{7,7},{8,8},{9,12},{10,1... | collective-permute-start | bytes 786440 | tf_op jit(solution)/shard_map/ppermute | solution.py:406
  91.1 0.2 collective-permute-start.8
  91.3 3.3 %collective-permute-start.9 = (bf16[64,16,128]{2,1,0:T(8,128)(2,1)S(1)}, bf16[64,16,128]{2,1,0:T(8,128)(2,1)S(1)}, u32[]{:S(2)}, u32[]{:S(2)}) collective-permute-start(bf16[64,16,128]{2,1,0:T(8,128)(2,1)S(1)} %get-tuple-element.19), channel_id=1, source_target_pairs={{0,16},{1,20},{2,18},{3,22},{4,17},{5,21},{6,19},{7,23},{8,24},{9,... | collective-permute-start | bytes 786440 | tf_op jit(solution)/shard_map/ppermute | solution.py:406
  94.7 7.6 %middle_levels.2 = (bf16[64,16,128]{2,1,0:T(8,128)(2,1)S(1)}, bf16[64,16,128]{2,1,0:T(8,128)(2,1)S(1)}, bf16[64,16,128]{2,1,0:T(8,128)(2,1)S(1)}, bf16[64,16,128]{2,1,0:T(8,128)(2,1)S(1)}) custom-call(s32[5]{0:T(128)S(1)} %stack.23.me_ref, s32[4]{0:T(128)S(1)} %copy-done.3, bf16[512,16,128]{2,1,0:T(8,128)(2,1)S(1)} %all-to-all-done.g_ref, ...), custom_call_target="tpu_custom_call" | custom-call | tf_op jit(solution)/shard_map/middle_levels/pallas_call | solution.py:390
  102.3 1.9 %collective-permute-start.3 = (bf16[64,16,128]{2,1,0:T(8,128)(2,1)S(1)}, bf16[64,16,128]{2,1,0:T(8,128)(2,1)S(1)}, u32[]{:S(2)}, u32[]{:S(2)}) collective-permute-start(bf16[64,16,128]{2,1,0:T(8,128)(2,1)S(1)} %get-tuple-element.13), channel_id=1, source_target_pairs={{0,0},{1,4},{2,2},{3,6},{4,1},{5,5},{6,3},{7,7},{8,8},{9,12},{10,1... | collective-permute-start | bytes 786440 | tf_op jit(solution)/shard_map/ppermute | solution.py:406
  104.2 0.1 collective-permute-start.4
  104.3 8.0 %collective-permute-done.7.p0 = bf16[64,16,128]{2,1,0:T(8,128)(2,1)S(1)} collective-permute-done((bf16[64,16,128]{2,1,0:T(8,128)(2,1)S(1)}, bf16[64,16,128]{2,1,0:T(8,128)(2,1)S(1)}, u32[]{:S(2)}, u32[]{:S(2)}) %collective-permute-start.7) | collective-permute-done | bytes 262176 | tf_op jit(solution)/shard_map/ppermute | solution.py:406
  112.3 0.0 collective-permute-start.10
  112.3 0.0 collective-permute-done.8.p1
  112.3 3.8 %collective-permute-start.5 = (bf16[64,16,128]{2,1,0:T(8,128)(2,1)S(1)}, bf16[64,16,128]{2,1,0:T(8,128)(2,1)S(1)}, u32[]{:S(2)}, u32[]{:S(2)}) collective-permute-start(bf16[64,16,128]{2,1,0:T(8,128)(2,1)S(1)} %get-tuple-element.15), channel_id=1, source_target_pairs={{0,16},{1,20},{2,18},{3,22},{4,17},{5,21},{6,19},{7,23},{8,24},{9,... | collective-permute-start | bytes 786440 | tf_op jit(solution)/shard_map/ppermute | solution.py:406
  116.1 11.5 %collective-permute-done.9.p2 = bf16[64,16,128]{2,1,0:T(8,128)(2,1)S(1)} collective-permute-done((bf16[64,16,128]{2,1,0:T(8,128)(2,1)S(1)}, bf16[64,16,128]{2,1,0:T(8,128)(2,1)S(1)}, u32[]{:S(2)}, u32[]{:S(2)}) %collective-permute-start.9) | collective-permute-done | bytes 262176 | tf_op jit(solution)/shard_map/ppermute | solution.py:406
  127.5 0.0 copy-start.2
  127.5 0.0 collective-permute-start.6
  127.5 5.5 %collective-permute-done.10.p3 = bf16[64,16,128]{2,1,0:T(8,128)(2,1)S(1)} collective-permute-done((bf16[64,16,128]{2,1,0:T(8,128)(2,1)S(1)}, bf16[64,16,128]{2,1,0:T(8,128)(2,1)S(1)}, u32[]{:S(2)}, u32[]{:S(2)}) %collective-permute-start.10) | collective-permute-done | bytes 262176 | tf_op jit(solution)/shard_map/ppermute | solution.py:406
  133.0 0.0 copy-done
  133.0 2.5 %first_receivers.1.done_ref = bf16[4096,128]{1,0:T(8,128)(2,1)S(1)} custom-call(s32[5]{0:T(128)S(1)} %stack.23.me_ref, s32[4]{0:T(128)S(1)} %copy-done.3, bf16[8192,128]{1,0:T(8,128)(2,1)S(1)} %copy-done, bf16[64,16,128]{2,1,0:T(8,128)(2,1)S(1)} %collective-permute-done.7.p0, bf16[64,16,128]{2,1,0:T(8,128)(2,1)S(1)} %collective-permute-done.8.p1, ...), custom_call_target="tpu_custom_call" | custom-call | tf_op jit(solution)/shard_map/first_receivers/pallas_call | solution.py:409
  135.5 0.0 collective-permute-done.3.p0
  135.5 0.0 collective-permute-done.4.p1
  135.5 3.1 %collective-permute-done.5.p2 = bf16[64,16,128]{2,1,0:T(8,128)(2,1)S(1)} collective-permute-done((bf16[64,16,128]{2,1,0:T(8,128)(2,1)S(1)}, bf16[64,16,128]{2,1,0:T(8,128)(2,1)S(1)}, u32[]{:S(2)}, u32[]{:S(2)}) %collective-permute-start.5) | collective-permute-done | bytes 262176 | tf_op jit(solution)/shard_map/ppermute | solution.py:406
  138.6 0.0 collective-permute-done.6.p3
  138.6 0.0 copy-done.2
  138.7 12.1 %last_receivers.1 = bf16[8192,128]{1,0:T(8,128)(2,1)} custom-call(s32[5]{0:T(128)S(1)} %stack.23.me_ref, s32[4]{0:T(128)S(1)} %copy-done.3, s32[8192]{0:T(1024)S(1)} %copy-done.2, bf16[8192,128]{1,0:T(8,128)(2,1)S(1)} %copy-done, bf16[64,16,128]{2,1,0:T(8,128)(2,1)S(1)} %collective-permute-done.3.p0, bf16[64,16,128]{2,1,0:T(8,128)(2,1)S(1)} %collective-permute-done.4.p1, ...), custom_call_target="tpu_custom_call" | custom-call | tf_op jit(solution)/shard_map/last_receivers/pallas_call | solution.py:418
Async XLA Ops:
  1.7 24.4 %all-to-all-start.1 = ((bf16[128,8,128]{2,1,0:T(8,128)(2,1)}), bf16[128,8,128]{2,1,0:T(8,128)(2,1)S(1)}, u32[]{:S(2)}, u32[]{:S(2)}) async-start(bf16[128,8,128]{2,1,0:T(8,128)(2,1)} %bitcast.8), calls=%async_computation.1 | async-start | bytes 524288 | tf_op jit(solution)/shard_map/all_to_all | solution.py:357
  26.0 55.4 %copy-start.1 = (bf16[8,2,2,64,128]{4,3,2,1,0:T(8,128)(2,1)S(1)}, bf16[8,2,2,64,128]{4,3,2,1,0:T(8,128)(2,1)}, u32[]{:S(2)}) copy-start(bf16[8,2,2,64,128]{4,3,2,1,0:T(8,128)(2,1)} %tr_ref.3) | copy-start | bytes 1572868
  26.0 55.4 %copy-start.3 = (s32[4]{0:T(128)S(1)}, s32[4]{0:T(128)}, u32[]{:S(2)}) copy-start(s32[4]{0:T(128)} %bits_ref.9) | copy-start | bytes 52
  26.1 55.4 %all-to-all-start = ((bf16[512,16,128]{2,1,0:T(8,128)(2,1)}), bf16[512,16,128]{2,1,0:T(8,128)(2,1)S(1)}, u32[]{:S(2)}, u32[]{:S(2)}) async-start(bf16[512,16,128]{2,1,0:T(8,128)(2,1)} %source_side.1), calls=%async_computation | async-start | bytes 4194304 | tf_op jit(solution)/shard_map/all_to_all | solution.py:385
  31.9 2.3 %collective-permute-start = (bf16[128,8,128]{2,1,0:T(8,128)(2,1)S(1)}, bf16[128,8,128]{2,1,0:T(8,128)(2,1)S(1)}, u32[]{:S(2)}, u32[]{:S(2)}) collective-permute-start(bf16[128,8,128]{2,1,0:T(8,128)(2,1)S(1)} %all-to-all-done.1.f0), channel_id=1, source_target_pairs={{0,1},{1,0},{2,3},{3,2},{4,5},{5,4},{6,7},{7,6},{8,9},{9,8},{10,11... | collective-permute-start | bytes 786440 | tf_op jit(solution)/shard_map/ppermute | solution.py:361
  32.2 22.3 %collective-permute-start.1 = (bf16[128,8,128]{2,1,0:T(8,128)(2,1)S(1)}, bf16[128,8,128]{2,1,0:T(8,128)(2,1)S(1)}, u32[]{:S(2)}, u32[]{:S(2)}) collective-permute-start(bf16[128,8,128]{2,1,0:T(8,128)(2,1)S(1)} %all-to-all-done.1.f0), channel_id=1, source_target_pairs={{0,16},{1,17},{2,18},{3,19},{4,20},{5,21},{6,22},{7,23},{8,24},{9,... | collective-permute-start | bytes 786440 | tf_op jit(solution)/shard_map/ppermute | solution.py:361
  33.7 30.7 %collective-permute-start.2 = (bf16[128,8,128]{2,1,0:T(8,128)(2,1)S(1)}, bf16[128,8,128]{2,1,0:T(8,128)(2,1)}, u32[]{:S(2)}, u32[]{:S(2)}) collective-permute-start(bf16[128,8,128]{2,1,0:T(8,128)(2,1)S(1)} %all-to-all-done.1.f0), channel_id=1, source_target_pairs={{0,17},{1,16},{2,19},{3,18},{4,21},{5,20},{6,23},{7,22},{8,25},{9,... | collective-permute-start | bytes 786440 | tf_op jit(solution)/shard_map/ppermute | solution.py:361
  89.0 44.0 %copy-start = (bf16[8192,128]{1,0:T(8,128)(2,1)S(1)}, bf16[8192,128]{1,0:T(8,128)(2,1)}, u32[]{:S(2)}) copy-start(bf16[8192,128]{1,0:T(8,128)(2,1)} %ri_ref.3) | copy-start | bytes 6291460
  89.0 23.3 %collective-permute-start.7 = (bf16[64,16,128]{2,1,0:T(8,128)(2,1)S(1)}, bf16[64,16,128]{2,1,0:T(8,128)(2,1)S(1)}, u32[]{:S(2)}, u32[]{:S(2)}) collective-permute-start(bf16[64,16,128]{2,1,0:T(8,128)(2,1)S(1)} %get-tuple-element.17), channel_id=1, source_target_pairs={{0,0},{1,4},{2,2},{3,6},{4,1},{5,5},{6,3},{7,7},{8,8},{9,12},{10,1... | collective-permute-start | bytes 786440 | tf_op jit(solution)/shard_map/ppermute | solution.py:406
  91.1 21.2 %collective-permute-start.8 = (bf16[64,16,128]{2,1,0:T(8,128)(2,1)S(1)}, bf16[64,16,128]{2,1,0:T(8,128)(2,1)S(1)}, u32[]{:S(2)}, u32[]{:S(2)}) collective-permute-start(bf16[64,16,128]{2,1,0:T(8,128)(2,1)S(1)} %get-tuple-element.18), channel_id=1, source_target_pairs={{0,4},{1,0},{2,6},{3,2},{4,5},{5,1},{6,7},{7,3},{8,12},{9,8},{10,1... | collective-permute-start | bytes 786440 | tf_op jit(solution)/shard_map/ppermute | solution.py:406
  91.3 36.2 %collective-permute-start.9 = (bf16[64,16,128]{2,1,0:T(8,128)(2,1)S(1)}, bf16[64,16,128]{2,1,0:T(8,128)(2,1)S(1)}, u32[]{:S(2)}, u32[]{:S(2)}) collective-permute-start(bf16[64,16,128]{2,1,0:T(8,128)(2,1)S(1)} %get-tuple-element.19), channel_id=1, source_target_pairs={{0,16},{1,20},{2,18},{3,22},{4,17},{5,21},{6,19},{7,23},{8,24},{9,... | collective-permute-start | bytes 786440 | tf_op jit(solution)/shard_map/ppermute | solution.py:406
  102.3 33.2 %collective-permute-start.3 = (bf16[64,16,128]{2,1,0:T(8,128)(2,1)S(1)}, bf16[64,16,128]{2,1,0:T(8,128)(2,1)S(1)}, u32[]{:S(2)}, u32[]{:S(2)}) collective-permute-start(bf16[64,16,128]{2,1,0:T(8,128)(2,1)S(1)} %get-tuple-element.13), channel_id=1, source_target_pairs={{0,0},{1,4},{2,2},{3,6},{4,1},{5,5},{6,3},{7,7},{8,8},{9,12},{10,1... | collective-permute-start | bytes 786440 | tf_op jit(solution)/shard_map/ppermute | solution.py:406
  104.2 31.3 %collective-permute-start.4 = (bf16[64,16,128]{2,1,0:T(8,128)(2,1)S(1)}, bf16[64,16,128]{2,1,0:T(8,128)(2,1)S(1)}, u32[]{:S(2)}, u32[]{:S(2)}) collective-permute-start(bf16[64,16,128]{2,1,0:T(8,128)(2,1)S(1)} %get-tuple-element.14), channel_id=1, source_target_pairs={{0,4},{1,0},{2,6},{3,2},{4,5},{5,1},{6,7},{7,3},{8,12},{9,8},{10,1... | collective-permute-start | bytes 786440 | tf_op jit(solution)/shard_map/ppermute | solution.py:406
  112.3 20.7 %collective-permute-start.10 = (bf16[64,16,128]{2,1,0:T(8,128)(2,1)S(1)}, bf16[64,16,128]{2,1,0:T(8,128)(2,1)S(1)}, u32[]{:S(2)}, u32[]{:S(2)}) collective-permute-start(bf16[64,16,128]{2,1,0:T(8,128)(2,1)S(1)} %get-tuple-element.20), channel_id=1, source_target_pairs={{0,20},{1,16},{2,22},{3,18},{4,21},{5,17},{6,23},{7,19},{8,28},{9,... | collective-permute-start | bytes 786440 | tf_op jit(solution)/shard_map/ppermute | solution.py:406
  112.3 26.4 %collective-permute-start.5 = (bf16[64,16,128]{2,1,0:T(8,128)(2,1)S(1)}, bf16[64,16,128]{2,1,0:T(8,128)(2,1)S(1)}, u32[]{:S(2)}, u32[]{:S(2)}) collective-permute-start(bf16[64,16,128]{2,1,0:T(8,128)(2,1)S(1)} %get-tuple-element.15), channel_id=1, source_target_pairs={{0,16},{1,20},{2,18},{3,22},{4,17},{5,21},{6,19},{7,23},{8,24},{9,... | collective-permute-start | bytes 786440 | tf_op jit(solution)/shard_map/ppermute | solution.py:406
  127.5 11.1 %copy-start.2 = (s32[8192]{0:T(1024)S(1)}, s32[8192]{0:T(1024)}, u32[]{:S(2)}) copy-start(s32[8192]{0:T(1024)} %slot_ref.1) | copy-start | bytes 98308
  127.5 11.1 %collective-permute-start.6 = (bf16[64,16,128]{2,1,0:T(8,128)(2,1)S(1)}, bf16[64,16,128]{2,1,0:T(8,128)(2,1)S(1)}, u32[]{:S(2)}, u32[]{:S(2)}) collective-permute-start(bf16[64,16,128]{2,1,0:T(8,128)(2,1)S(1)} %get-tuple-element.16), channel_id=1, source_target_pairs={{0,20},{1,16},{2,22},{3,18},{4,21},{5,17},{6,23},{7,19},{8,28},{9,... | collective-permute-start | bytes 786440 | tf_op jit(solution)/shard_map/ppermute | solution.py:406

commit v4 on v3

v4 whole, which is shorter than its diff:
```python
import functools

import jax
import jax.numpy as jnp
from jax import lax
from jax.experimental import pallas as pl
from jax.experimental.pallas import tpu as pltpu
from jax.sharding import PartitionSpec as P

LEAF = 64
AXES = ("hi", "lo")
SPLIT = 16
STACKS = 16
QUARTERS = ((0,), (1, 2), (3,))
LEAVES = 32
SPAIRS = 32
F32 = jnp.float32
BF16 = jnp.bfloat16


def log2(value):
    return value.bit_length() - 1


def lanes_low(shape):
    return lax.broadcasted_iota(jnp.int32, shape, len(shape) - 1) < 64


def roll64(value):
    return pltpu.roll(value, 64, 1)


def build_weights(w_ref, slot, tr_ref, level, flip=0):
    for i in range(2):
        for c in range(2):
            piece = tr_ref[level, c ^ flip, i ^ flip].astype(F32)
            turned = roll64(piece)
            turned = jnp.where(lanes_low(piece.shape), -turned, turned)
            block = jnp.concatenate([piece, turned], axis=0).astype(BF16)
            w_ref[slot, i * 128 : (i + 1) * 128, c * 128 : (c + 1) * 128] = block
            across = roll64(jnp.concatenate([piece, turned], axis=0)).astype(BF16)
            w_ref[slot, i * 128 : (i + 1) * 128, 256 + c * 128 : 256 + (c + 1) * 128] = across


def split_factors(read16, fa_ref, fb_ref, first, rows):
    def body(step, carry):
        for part in range(SPLIT):
            at = pl.multiple_of(step * (16 * SPLIT) + part * 16, 16)
            fac = read16(at).astype(F32)
            turned = roll64(fac)
            low = lanes_low(fac.shape)
            fa_ref[pl.ds(first + at, 16), :] = jnp.where(low, fac, turned)
            fb_ref[pl.ds(first + at, 16), :] = jnp.where(low, -turned, fac)
        return carry

    lax.fori_loop(0, rows // (16 * SPLIT), body, 0)


def scaled(value, other, fa_ref, fb_ref, row):
    fa = fa_ref[pl.ds(row, 1), :]
    fb = fb_ref[pl.ds(row, 1), :]
    return (value * fa + other * fb).astype(BF16)


def gather16(rows_ref, index_ref, first):
    iota = lax.broadcasted_iota(jnp.int32, (8, 128), 0)
    halves = []
    for half in range(2):
        acc = None
        for i in range(8):
            at = index_ref[first + half * 8 + i]
            row = jnp.broadcast_to(rows_ref[pl.ds(at, 1), :], (8, 128))
            acc = row if acc is None else jnp.where(iota == i, row, acc)
        halves.append(acc)
    return jnp.concatenate(halves, axis=0).astype(BF16)


def pair_of(k, bit):
    low = k & (lax.shift_left(1, bit) - 1)
    first = lax.shift_left(lax.shift_right_logical(k, bit), bit + 1) | low
    return first, first + lax.shift_left(1, bit)


def source_kernel(
    dims, order_ref, bits_ref, ch_hbm, si_hbm, fac_hbm, tr_hbm, out_ref,
    ch_ref, si_ref, fac_ref, tr_ref, sems, x32, mid_ref, fa, fb, w_ref,
):
    n_hi, n_lo, share, blocks, rhs = dims
    quarter = rhs // 4
    points = blocks * LEAF
    part = points // 4
    copies = [
        pltpu.make_async_copy(ch_hbm.at[pl.ds(i * part, part)], ch_ref.at[pl.ds(i * part, part)], sems.at[i])
        for i in range(4)
    ]
    copies.append(pltpu.make_async_copy(fac_hbm, fac_ref, sems.at[4]))
    copies.append(pltpu.make_async_copy(tr_hbm.at[pl.ds(0, 2)], tr_ref, sems.at[5]))
    copies.append(pltpu.make_async_copy(si_hbm, si_ref, sems.at[6]))
    for copy in copies[4:6] + copies[:4] + copies[6:]:
        copy.start()
    copies[5].wait()
    build_weights(w_ref, 0, tr_ref, 0)
    build_weights(w_ref, 1, tr_ref, 1)
    copies[4].wait()
    split_factors(lambda at: fac_ref[pl.ds(at, 16), :], fa, fb, 0, blocks * 8)

    def widen(step, carry):
        rows = pl.ds(pl.multiple_of(step * 512, 512), 512)
        x32[rows, :] = ch_ref[rows, :].astype(F32)
        return carry

    for i in range(4):
        copies[i].wait()
        lax.fori_loop(i * (part // 512), (i + 1) * (part // 512), widen, 0)
    copies[6].wait()

    def leaf(b):
        first = pl.multiple_of(b * LEAF, LEAF)
        rows = jnp.concatenate([gather16(x32, order_ref, first + g * 16) for g in range(LEAF // 16)], axis=0)
        product = lax.dot_general(
            rows, si_ref[pl.ds(first, LEAF), :], (((0,), (0,)), ((), ())), preferred_element_type=F32
        )
        lower = roll64(product[rhs:])
        lower = jnp.where(lanes_low(lower.shape), -lower, lower)
        return (product[:rhs] + lower).astype(BF16)

    def level(index, pairs, read, store):
        bit = bits_ref[index]

        def body(step, carry):
            ends = [pair_of(step * pairs + p, bit) for p in range(pairs)]
            lhs = jnp.concatenate([jnp.concatenate([read(a), read(b)], axis=1) for a, b in ends], axis=0)
            res = jnp.dot(lhs, w_ref[index], preferred_element_type=F32)
            for p in range(pairs):
                for c in range(2):
                    n = ends[p][c]
                    value = res[p * rhs : (p + 1) * rhs, c * 128 : (c + 1) * 128]
                    other = res[p * rhs : (p + 1) * rhs, 256 + c * 128 : 256 + (c + 1) * 128]
                    store(n, scaled(value, other, fa, fb, n * 8 + index))
            return carry

        lax.fori_loop(0, blocks // 2 // pairs, body, 0)

    st, lm, hh = log2(share), log2(n_lo // 4), log2(n_hi // 2)

    def store_first(n, value):
        mid_ref[n] = value

    def store_second(n, value):
        t = n & (share - 1)
        core = (n >> st) & 1
        lmid = (n >> (st + 1)) & (n_lo // 4 - 1)
        z1 = (n >> (st + 1 + lm)) & 1
        rest = (n >> (st + 2 + lm)) & (n_hi // 2 - 1)
        y = n >> (st + 2 + lm + hh)
        target = rest * n_lo + core * (n_lo // 2) + lmid * 2
        m = (y * 2 + z1) * share + t
        for r in range(4):
            d = target + (r // 2) * (n_hi // 2) * n_lo + r % 2
            out_ref[d * (4 * share) + m] = value[r * quarter : (r + 1) * quarter]

    level(0, LEAVES // 2, leaf, store_first)
    level(1, SPAIRS, lambda n: mid_ref[n], store_second)


def spare_bits(bits_ref, dims):
    n_hi, n_lo, share, blocks, rhs = dims
    inner = log2(share) + log2(n_lo) - 1
    outer = log2(share) + log2(n_lo) + log2(n_hi) - 1
    free = [bit for bit in range(outer) if bit != inner]

    def first_free(after):
        found = jnp.int32(free[-1])
        for bit in reversed(free[:-1]):
            usable = (bits_ref[2] != bit) & (bits_ref[3] != bit) & (bit > after)
            found = jnp.where(usable, bit, found)
        return found

    first = first_free(-1)
    return (first, first_free(first)), inner, outer


def with_bit(i, bit, value):
    low = i & (lax.shift_left(1, bit) - 1)
    return lax.shift_left(lax.shift_right_logical(i, bit), bit + 1) | low | (value << bit)


def in_quarter(i, spare, quarter):
    return with_bit(with_bit(i, spare[0], quarter & 1), spare[1], quarter >> 1)


def inverse_kernel(dims, slot_ref, after_ref, inverse_ref):
    def invert(step, carry):
        for part in range(32):
            at = step * 32 + part
            inverse_ref[slot_ref[at]] = at
        return carry

    lax.fori_loop(0, dims[3] * LEAF // 32, invert, 0)


def middle_kernel(
    dims, quarters, me_ref, bits_ref, g_ref, f0, f1, f2, f3, tr_ref, o0, o1, o2, o3, x, x2, fa, fb, w_ref
):
    n_hi, n_lo, share, blocks, rhs = dims
    rows = rhs // 4
    st = log2(share)
    y, core = me_ref[0], me_ref[1]
    spare, inner, outer = spare_bits(bits_ref, dims)
    count = blocks // 4
    low = lanes_low((8, 128))
    for index in range(4):
        build_weights(w_ref, index, tr_ref, index + 2)
    build_weights(w_ref, 4, tr_ref, 6, core)
    build_weights(w_ref, 5, tr_ref, 7, y)

    def finish(res, p, c, row):
        value = res[p * rows : (p + 1) * rows, c * 128 : (c + 1) * 128]
        other = res[p * rows : (p + 1) * rows, 256 + c * 128 : 256 + (c + 1) * 128]
        return scaled(value, other, fa, fb, row)

    def held(x):
        def read(j, i):
            return x[j * count + i]

        return read

    def level(index, bit, read, x):
        packed = bit - (bit > spare[0]).astype(jnp.int32) - (bit > spare[1]).astype(jnp.int32)
        ends = [pair_of(k, packed) for k in range(count // 2)]
        for j in range(4):
            lhs = jnp.concatenate([jnp.concatenate([read(j, a), read(j, b)], axis=1) for a, b in ends], axis=0)
            res = jnp.dot(lhs, w_ref[index - 2], preferred_element_type=F32)
            for p in range(count // 2):
                for c in range(2):
                    n = j * count + ends[p][c]
                    x[n] = finish(res, p, c, n * 8 + index)

    def across(index, x, pairs, outs):
        for (a, b), (out_a, out_b) in zip(pairs, outs):
            lhs = jnp.concatenate([x[pl.ds(j * count, count)].reshape(count * rows, 128) for j in (a, b)], axis=1)
            res = jnp.dot(lhs, w_ref[index - 2], preferred_element_type=F32)
            for p in range(count):
                for c, (j, out) in enumerate(((a, out_a), (b, out_b))):
                    out[p] = finish(res, p, c, (j * count + p) * 8 + index)

    for place, quarter in enumerate(quarters):
        for j, f_ref in enumerate((f0, f1, f2, f3)):
            for i in range(count):
                fac = f_ref[in_quarter(i, spare, quarter)].astype(F32)
                turned = roll64(fac)
                at = pl.ds((j * count + i) * 8, 8)
                fa[at, :] = jnp.where(low, fac, turned)
                fb[at, :] = jnp.where(low, -turned, fac)

        def read_arrived(j, i):
            n = in_quarter(i, spare, quarter)
            first = (((j >> 1) ^ y) * 2 + ((j & 1) ^ core)) * share
            return g_ref[(n >> st) * (4 * share) + first + (n & (share - 1))]

        level(2, inner, read_arrived, x)
        level(3, outer, held(x), x2)
        level(4, bits_ref[2], held(x2), x)
        level(5, bits_ref[3], held(x), x2)
        rest = [x.at[pl.ds(j * count, count)] for j in range(4)]
        done = [o.at[pl.ds(place * count, count)] for o in (o0, o1, o2, o3)]
        across(6, x2, ((0, 1), (2, 3)), ((rest[0], rest[1]), (rest[2], rest[3])))
        across(7, x, ((0, 2), (1, 3)), ((done[0], done[2]), (done[1], done[3])))


def receive(dims, quarters, me_ref, bits_ref, inverse_ref, ri_ref, pieces, out32, stack, t32):
    n_hi, n_lo, share, blocks, rhs = dims
    part_rows = rhs // 4
    y, z1 = me_ref[0], me_ref[2]
    spare, _, _ = spare_bits(bits_ref, dims)
    count = blocks // 4
    lows = lanes_low((part_rows, 128))

    for place, quarter in enumerate(quarters):

        def body(step, carry):
            for part in range(STACKS):
                i = step * STACKS + part
                n = in_quarter(i, spare, quarter)
                for j, p_ref in enumerate(pieces):
                    group = ((j >> 1) ^ y) * 2 + ((j & 1) ^ z1)
                    at = pl.multiple_of(group * part_rows, part_rows)
                    piece = p_ref[place * count + i].astype(F32)
                    stack[part, pl.ds(at, part_rows), :] = jnp.where(lows, piece, -piece).astype(BF16)
                    stack[part, pl.ds(at + rhs, part_rows), :] = roll64(piece).astype(BF16)
                first = pl.multiple_of(n * LEAF, LEAF)
                t32[part * LEAF : (part + 1) * LEAF, :] = lax.dot_general(
                    ri_ref[pl.ds(first, LEAF), :],
                    stack[part],
                    (((1,), (1,)), ((), ())),
                    preferred_element_type=F32,
                )
                for r in range(LEAF):
                    out32[pl.ds(inverse_ref[first + r], 1), :] = t32[part * LEAF + r : part * LEAF + r + 1, :]
            return carry

        lax.fori_loop(0, count // STACKS, body, 0)


def first_receivers(dims, me_ref, bits_ref, inverse_ref, ri_ref, *refs):
    pieces, (out_ref, stack, t32) = refs[:-3], refs[-3:]
    for at, quarters in enumerate(QUARTERS[:-1]):
        receive(
            dims, quarters, me_ref, bits_ref, inverse_ref, ri_ref, pieces[4 * at : 4 * at + 4], out_ref, stack, t32
        )


def last_receivers(dims, me_ref, bits_ref, inverse_ref, ri_ref, p0, p1, p2, p3, done_ref, out_hbm, whole, narrow, sems, stack, t32):
    points = dims[3] * LEAF
    part = points // 4

    def take(step, carry):
        rows = pl.ds(pl.multiple_of(step * 512, 512), 512)
        whole[rows, :] = done_ref[rows, :]
        return carry

    lax.fori_loop(0, points // 512, take, 0)
    receive(dims, QUARTERS[-1], me_ref, bits_ref, inverse_ref, ri_ref, (p0, p1, p2, p3), whole, stack, t32)
    copies = []
    for i in range(4):

        def round_off(step, carry):
            rows = pl.ds(pl.multiple_of(step * 512, 512), 512)
            narrow[rows, :] = whole[rows, :].astype(BF16)
            return carry

        lax.fori_loop(i * (part // 512), (i + 1) * (part // 512), round_off, 0)
        rows = pl.ds(i * part, part)
        copies.append(pltpu.make_async_copy(narrow.at[rows], out_hbm.at[rows], sems.at[i]))
        copies[-1].start()
    for copy in copies:
        copy.wait()


def on_vmem():
    return pl.BlockSpec(memory_space=pltpu.VMEM)


def on_any():
    return pl.BlockSpec(memory_space=pl.ANY)


def on_smem():
    return pl.BlockSpec(memory_space=pltpu.SMEM)


def params(mebibytes):
    return pltpu.CompilerParams(vmem_limit_bytes=mebibytes * 2**20)


def per_device(
    n_hi, n_lo, charges, source_order, source_interp, factors, transfers, level_bits, receiver_interp, receiver_slot
):
    points, twice_rhs = charges.shape
    rhs = twice_rhs // 2
    blocks = points // LEAF
    devices = n_hi * n_lo
    share = blocks // devices
    quarter = rhs // 4
    dims = (n_hi, n_lo, share, blocks, rhs)
    half_hi, half_lo = n_hi // 2 * n_lo, n_lo // 2
    hi, lo = lax.axis_index("hi"), lax.axis_index("lo")
    me = jnp.stack([hi >> (log2(n_hi) - 1), lo & 1, lo >> (log2(n_lo) - 1), hi, lo]).astype(jnp.int32)

    def swapped(device, j):
        flipped = device ^ (half_hi if j >> 1 else 0)
        core, top = flipped & 1, (flipped // half_lo) & 1
        base = flipped - core - top * half_lo
        return base + (core ^ (j & 1)) * half_lo + top

    spread = factors.reshape(n_hi, 2, n_lo // 4, 2, share, 8, 128).transpose(0, 3, 2, 1, 4, 5, 6)
    spread = lax.all_to_all(spread.reshape(blocks, 8, 128), AXES, split_axis=0, concat_axis=0, tiled=True)
    facs = [spread]
    for j in range(1, 4):
        mask = (half_hi if j >> 1 else 0) ^ (j & 1)
        facs.append(lax.ppermute(spread, AXES, [(s, s ^ mask) for s in range(devices)]))

    sent = pl.pallas_call(
        functools.partial(source_kernel, dims),
        out_shape=jax.ShapeDtypeStruct((devices * 4 * share, quarter, 128), BF16),
        in_specs=[on_smem(), on_smem()] + [on_any()] * 4,
        out_specs=on_vmem(),
        scratch_shapes=[
            pltpu.VMEM((points, 128), BF16),
            pltpu.VMEM((points, 128), BF16),
            pltpu.VMEM((blocks * 8, 128), BF16),
            pltpu.VMEM((2,) + transfers.shape[1:], BF16),
            pltpu.SemaphoreType.DMA((7,)),
            pltpu.VMEM((points, 128), F32),
            pltpu.VMEM((blocks, rhs, 128), BF16),
            pltpu.VMEM((blocks * 8, 128), F32),
            pltpu.VMEM((blocks * 8, 128), F32),
            pltpu.VMEM((2, 256, 512), BF16),
        ],
        compiler_params=params(60),
        name="source_side",
    )(source_order, level_bits, charges, source_interp, factors.reshape(blocks * 8, 128), transfers)

    arrived = lax.all_to_all(sent, AXES, split_axis=0, concat_axis=0, tiled=True)

    inverse = pl.pallas_call(
        functools.partial(inverse_kernel, dims),
        out_shape=jax.ShapeDtypeStruct((points,), jnp.int32),
        in_specs=[on_smem(), on_any()],
        out_specs=on_smem(),
        compiler_params=params(12),
        cost_estimate=pl.CostEstimate(flops=10**10, bytes_accessed=2**25, transcendentals=0),
        name="inverse_slots",
    )(receiver_slot, facs[3])
    facs[1], inverse = lax.optimization_barrier((facs[1], inverse))

    homes = []
    for quarters in QUARTERS:
        count = len(quarters) * blocks // 4
        pieces = pl.pallas_call(
            functools.partial(middle_kernel, dims, quarters),
            out_shape=[jax.ShapeDtypeStruct((count, quarter, 128), BF16)] * 4,
            in_specs=[on_smem(), on_smem()] + [on_vmem()] * 6,
            out_specs=[on_vmem()] * 4,
            scratch_shapes=[
                pltpu.VMEM((blocks, quarter, 128), BF16),
                pltpu.VMEM((blocks, quarter, 128), BF16),
                pltpu.VMEM((blocks * 8, 128), F32),
                pltpu.VMEM((blocks * 8, 128), F32),
                pltpu.VMEM((6, 256, 512), BF16),
            ],
            compiler_params=params(16),
            name="middle_levels",
        )(me, level_bits, arrived, *facs, transfers)
        homes.append(
            [lax.ppermute(pieces[j], AXES, [(s, swapped(s, j)) for s in range(devices)]) for j in range(4)]
        )

    work = [pltpu.VMEM((STACKS, 2 * rhs, 128), BF16), pltpu.VMEM((STACKS * LEAF, 128), F32)]
    done = pl.pallas_call(
        functools.partial(first_receivers, dims),
        out_shape=jax.ShapeDtypeStruct((points, twice_rhs), F32),
        in_specs=[on_smem(), on_smem(), on_smem()] + [on_vmem()] * (4 * len(QUARTERS) - 3),
        out_specs=on_vmem(),
        scratch_shapes=work,
        compiler_params=params(16),
        name="first_receivers",
    )(me, level_bits, inverse, receiver_interp, *[piece for home in homes[:-1] for piece in home])
    return pl.pallas_call(
        functools.partial(last_receivers, dims),
        out_shape=jax.ShapeDtypeStruct((points, twice_rhs), BF16),
        in_specs=[on_smem(), on_smem(), on_smem()] + [on_vmem()] * 6,
        out_specs=on_any(),
        scratch_shapes=[
            pltpu.VMEM((points, 128), F32),
            pltpu.VMEM((points, 128), BF16),
            pltpu.SemaphoreType.DMA((4,)),
        ]
        + work,
        compiler_params=params(24),
        name="last_receivers",
    )(me, level_bits, inverse, receiver_interp, *homes[-1], done)


def solution(mesh):
    body = functools.partial(per_device, mesh.shape["hi"], mesh.shape["lo"])
    return jax.shard_map(
        body,
        mesh=mesh,
        in_specs=(
            P(AXES, None),
            P(AXES),
            P(AXES, None),
            P(AXES, None, None),
            P(),
            P(),
            P(AXES, None),
            P(AXES),
        ),
        out_specs=P(AXES, None),
        check_vma=False,
    )
```

time: 151 us -> 144 us (0.954)
  waiting for transfers between devices: 75.2 us -> 50.5 us
  Pallas kernels: 47.1 us -> 55.3 us
  starting transfers between devices: 26.6 us -> 34.1 us
  local copies, waits for them, and re-layouts: 1.79 us -> 3.42 us
    ppermute x8 -> x12, waiting for transfers between devices: 28 us -> 15.7 us  [per_device(): lax.ppermute(pieces[j], AXES, [(s, swapped(s, j)) for s in range(devices)])]
    pallas_call x2 -> x4, Pallas kernels: 15.2 us -> 24.4 us  [the longest x3 12.7 us: per_device(): pl.pallas_call(functools.partial(middle_kernel, dims, quarters), out_shap...]
    ppermute x3, waiting for transfers between devices: 30.2 us -> 21.2 us  [per_device(): lax.ppermute(spread, AXES, [(s, s ^ mask) for s in range(devices)])]
    ppermute x8 -> x12, starting transfers between devices: 11.4 us -> 18.9 us  [per_device(): lax.ppermute(pieces[j], AXES, [(s, swapped(s, j)) for s in range(devices)])]
    pallas_call x1, Pallas kernels: 2.51 us -> 9.89 us  [per_device(): pl.pallas_call(functools.partial(first_receivers, dims), out_shape=jax.Sh...]
    pallas_call x1, Pallas kernels: 12.1 us -> 5.71 us  [per_device(): pl.pallas_call(functools.partial(last_receivers, dims), out_shape=jax.Sha...]
    all_to_all x1, waiting for transfers between devices: 17 us -> 13.6 us  [per_device(): lax.all_to_all(sent, AXES, split_axis=0, concat_axis=0, tiled=True)]
    pallas_call x1, Pallas kernels: 17.2 us -> 15.4 us  [per_device(): pl.pallas_call(functools.partial(source_kernel, dims), out_shape=jax.Shap...]
  transfers between devices with their start and end apart: 13 -> 17, of which waited for: 7 -> 4; matrix products, arithmetic and copies ran while one was open for 0% -> 0% of each run, Pallas kernels for 18% -> 32%
where the time goes in v4:
time: 144 us
  Pallas kernels  55.3 us (38%)
  waiting for transfers between devices  50.5 us (35%)
  starting transfers between devices  34.1 us (24%)
  local copies, waits for them, and re-layouts  3.42 us (2%)
    ppermute x3, waiting for transfers between devices, per_device(): lax.ppermute(spread, AXES, [(s, s ^ mask) for s in range(devices)])  21.2 us
    ppermute x12, starting transfers between devices, per_device(): lax.ppermute(pieces[j], AXES, [(s, swapped(s, j)) for s in range(devices)])  18.9 us
    ppermute x12, waiting for transfers between devices, per_device(): lax.ppermute(pieces[j], AXES, [(s, swapped(s, j)) for s in range(devices)])  15.7 us
    pallas_call x1, Pallas kernels, per_device(): pl.pallas_call(functools.partial(source_kernel, dims), out_shape=jax.Shap...  15.4 us
    all_to_all x1, waiting for transfers between devices, per_device(): lax.all_to_all(sent, AXES, split_axis=0, concat_axis=0, tiled=True)  13.6 us
    pallas_call x3, Pallas kernels, per_device(): pl.pallas_call(functools.partial(middle_kernel, dims, quarters), out_shap...  12.7 us
    pallas_call x1, Pallas kernels, per_device(): pl.pallas_call(functools.partial(inverse_kernel, dims), out_shape=jax.Sha...  11.6 us
    pallas_call x1, Pallas kernels, per_device(): pl.pallas_call(functools.partial(first_receivers, dims), out_shape=jax.Sh...  9.89 us
  transfers between devices with their start and end apart: 17, of which 4 were waited for; matrix products, arithmetic and copies ran while one was open for 0% of the time, Pallas kernels for 32%

profile of v4, /device:TPU:1, one launch (start us, length us, event | category | flops | bytes accessed | tf_op | source)
XLA Modules:
  0.0 143.8 jit_solution(12896334331558090319)
XLA Ops:
  0.0 1.7 %copy.9 = bf16[4,2,2,2,4,8,128]{6,5,4,1,2,3,0:T(8,128)(2,1)} copy(bf16[4,2,2,2,4,8,128]{6,5,4,3,2,1,0:T(8,128)(2,1)} %bitcast.10) | data formatting | bytes 524288 | tf_op jit(solution)/shard_map/reshape | solution.py:376
  1.7 7.1 %all-to-all-start = ((bf16[128,8,128]{2,1,0:T(8,128)(2,1)}), bf16[128,8,128]{2,1,0:T(8,128)(2,1)S(1)}, u32[]{:S(2)}, u32[]{:S(2)}) async-start(bf16[128,8,128]{2,1,0:T(8,128)(2,1)} %bitcast.7), calls=%async_computation | async-start | bytes 524288 | tf_op jit(solution)/shard_map/all_to_all | solution.py:377
  8.8 15.4 %source_side.1 = bf16[512,16,128]{2,1,0:T(8,128)(2,1)} custom-call(s32[8192]{0:T(1024)} %order_ref.1, s32[4]{0:T(128)} %bits_ref.11, bf16[8192,128]{1,0:T(8,128)(2,1)} %ch_hbm.1, bf16[8192,128]{1,0:T(8,128)(2,1)} %si_hbm.1, bf16[1024,128]{1,0:T(8,128)(2,1)} %bitcast.11, bf16[8,2,2,64,128]{4,3,2,1,0:T(8,128)(2,1)} %tr_ref.5), custom_call_target="tpu_custom_call" | custom-call | tf_op jit(solution)/shard_map/source_side/pallas_call | solution.py:383
  24.2 0.0 copy-start.5
  24.2 0.0 all-to-all-done.f0
  24.2 5.8 %all-to-all-start.1 = ((bf16[512,16,128]{2,1,0:T(8,128)(2,1)}), bf16[512,16,128]{2,1,0:T(8,128)(2,1)S(1)}, u32[]{:S(2)}, u32[]{:S(2)}) async-start(bf16[512,16,128]{2,1,0:T(8,128)(2,1)} %source_side.1), calls=%async_computation.1 | async-start | bytes 4194304 | tf_op jit(solution)/shard_map/all_to_all | solution.py:404
  30.1 1.7 %collective-permute-start.1 = (bf16[128,8,128]{2,1,0:T(8,128)(2,1)S(1)}, bf16[128,8,128]{2,1,0:T(8,128)(2,1)S(1)}, u32[]{:S(2)}, u32[]{:S(2)}) collective-permute-start(bf16[128,8,128]{2,1,0:T(8,128)(2,1)S(1)} %all-to-all-done.f0), channel_id=1, source_target_pairs={{0,17},{1,16},{2,19},{3,18},{4,21},{5,20},{6,23},{7,22},{8,25},{9,... | collective-permute-start | bytes 786440 | tf_op jit(solution)/shard_map/ppermute | solution.py:381
  31.8 0.1 stack.23.me_ref
  31.8 0.0 collective-permute-start.2
  31.9 0.5 collective-permute-start
  32.4 21.2 %collective-permute-done.1.after_ref.f3 = bf16[128,8,128]{2,1,0:T(8,128)(2,1)S(1)} collective-permute-done((bf16[128,8,128]{2,1,0:T(8,128)(2,1)S(1)}, bf16[128,8,128]{2,1,0:T(8,128)(2,1)S(1)}, u32[]{:S(2)}, u32[]{:S(2)}) %collective-permute-start.1) | collective-permute-done | bytes 262176 | tf_op jit(solution)/shard_map/ppermute | solution.py:381
  53.6 11.6 %inverse_slots.1.inverse_ref = s32[8192]{0:T(1024)S(1)} custom-call(s32[8192]{0:T(1024)S(1)} %copy-done.5, bf16[128,8,128]{2,1,0:T(8,128)(2,1)S(1)} %collective-permute-done.1.after_ref.f3), custom_call_target="tpu_custom_call" | custom-call | flops 10000000000 | bytes 33554432 | tf_op jit(solution)/shard_map/inverse_slots/pallas_call | solution.py:406
  65.3 0.0 collective-permute-done.f1
  65.3 0.7 copy-done.2
  66.0 0.0 collective-permute-done.2.f2
  66.0 13.6 %all-to-all-done.1.g_ref = bf16[512,16,128]{2,1,0:T(8,128)(2,1)S(1)} async-done(((bf16[512,16,128]{2,1,0:T(8,128)(2,1)}), bf16[512,16,128]{2,1,0:T(8,128)(2,1)S(1)}, u32[]{:S(2)}, u32[]{:S(2)}) %all-to-all-start.1) | async-done | bytes 2097184 | tf_op jit(solution)/shard_map/all_to_all | solution.py:404
  79.6 0.0 copy-done.4
  79.6 0.9 copy-done.3
  80.5 3.4 %middle_levels.4 = (bf16[32,16,128]{2,1,0:T(8,128)(2,1)S(1)}, bf16[32,16,128]{2,1,0:T(8,128)(2,1)S(1)}, bf16[32,16,128]{2,1,0:T(8,128)(2,1)S(1)}, bf16[32,16,128]{2,1,0:T(8,128)(2,1)S(1)}) custom-call(s32[5]{0:T(128)S(1)} %stack.23.me_ref, s32[4]{0:T(128)S(1)} %copy-done.4, bf16[512,16,128]{2,1,0:T(8,128)(2,1)S(1)} %all-to-all-done.1.g_ref, ...), custom_call_target="tpu_custom_call" | custom-call | tf_op jit(solution)/shard_map/middle_levels/pallas_call | solution.py:420
  83.9 1.9 %collective-permute-start.7 = (bf16[32,16,128]{2,1,0:T(8,128)(2,1)S(1)}, bf16[32,16,128]{2,1,0:T(8,128)(2,1)S(1)}, u32[]{:S(2)}, u32[]{:S(2)}) collective-permute-start(bf16[32,16,128]{2,1,0:T(8,128)(2,1)S(1)} %get-tuple-element.25), channel_id=1, source_target_pairs={{0,0},{1,4},{2,2},{3,6},{4,1},{5,5},{6,3},{7,7},{8,8},{9,12},{10,1... | collective-permute-start | bytes 393224 | tf_op jit(solution)/shard_map/ppermute | solution.py:436
  85.9 0.2 collective-permute-start.8
  86.1 3.3 %collective-permute-start.9 = (bf16[32,16,128]{2,1,0:T(8,128)(2,1)S(1)}, bf16[32,16,128]{2,1,0:T(8,128)(2,1)S(1)}, u32[]{:S(2)}, u32[]{:S(2)}) collective-permute-start(bf16[32,16,128]{2,1,0:T(8,128)(2,1)S(1)} %get-tuple-element.27), channel_id=1, source_target_pairs={{0,16},{1,20},{2,18},{3,22},{4,17},{5,21},{6,19},{7,23},{8,24},{9,... | collective-permute-start | bytes 393224 | tf_op jit(solution)/shard_map/ppermute | solution.py:436
  89.5 5.9 %middle_levels.5 = (bf16[64,16,128]{2,1,0:T(8,128)(2,1)S(1)}, bf16[64,16,128]{2,1,0:T(8,128)(2,1)S(1)}, bf16[64,16,128]{2,1,0:T(8,128)(2,1)S(1)}, bf16[64,16,128]{2,1,0:T(8,128)(2,1)S(1)}) custom-call(s32[5]{0:T(128)S(1)} %stack.23.me_ref, s32[4]{0:T(128)S(1)} %copy-done.4, bf16[512,16,128]{2,1,0:T(8,128)(2,1)S(1)} %all-to-all-done.1.g_ref, ...), custom_call_target="tpu_custom_call" | custom-call | tf_op jit(solution)/shard_map/middle_levels/pallas_call | solution.py:420
  95.4 0.0 copy-start.1
  95.4 2.1 %collective-permute-start.11 = (bf16[64,16,128]{2,1,0:T(8,128)(2,1)S(1)}, bf16[64,16,128]{2,1,0:T(8,128)(2,1)S(1)}, u32[]{:S(2)}, u32[]{:S(2)}) collective-permute-start(bf16[64,16,128]{2,1,0:T(8,128)(2,1)S(1)} %get-tuple-element.29), channel_id=1, source_target_pairs={{0,0},{1,4},{2,2},{3,6},{4,1},{5,5},{6,3},{7,7},{8,8},{9,12},{10,1... | collective-permute-start | bytes 786440 | tf_op jit(solution)/shard_map/ppermute | solution.py:436
  97.4 0.1 collective-permute-start.12
  97.5 0.0 collective-permute-done.7.refs_0_
  97.5 3.0 %collective-permute-start.13 = (bf16[64,16,128]{2,1,0:T(8,128)(2,1)S(1)}, bf16[64,16,128]{2,1,0:T(8,128)(2,1)S(1)}, u32[]{:S(2)}, u32[]{:S(2)}) collective-permute-start(bf16[64,16,128]{2,1,0:T(8,128)(2,1)S(1)} %get-tuple-element.31), channel_id=1, source_target_pairs={{0,16},{1,20},{2,18},{3,22},{4,17},{5,21},{6,19},{7,23},{8,24},{9,... | collective-permute-start | bytes 786440 | tf_op jit(solution)/shard_map/ppermute | solution.py:436
  100.5 0.0 collective-permute-done.8.refs_1_
  100.5 1.7 %collective-permute-start.10 = (bf16[32,16,128]{2,1,0:T(8,128)(2,1)S(1)}, bf16[32,16,128]{2,1,0:T(8,128)(2,1)S(1)}, u32[]{:S(2)}, u32[]{:S(2)}) collective-permute-start(bf16[32,16,128]{2,1,0:T(8,128)(2,1)S(1)} %get-tuple-element.28), channel_id=1, source_target_pairs={{0,20},{1,16},{2,22},{3,18},{4,21},{5,17},{6,23},{7,19},{8,28},{9,... | collective-permute-start | bytes 393224 | tf_op jit(solution)/shard_map/ppermute | solution.py:436
  102.2 0.0 collective-permute-done.9.refs_2_
  102.2 0.1 collective-permute-start.14
  102.2 3.4 %middle_levels.3 = (bf16[32,16,128]{2,1,0:T(8,128)(2,1)S(1)}, bf16[32,16,128]{2,1,0:T(8,128)(2,1)S(1)}, bf16[32,16,128]{2,1,0:T(8,128)(2,1)S(1)}, bf16[32,16,128]{2,1,0:T(8,128)(2,1)S(1)}) custom-call(s32[5]{0:T(128)S(1)} %stack.23.me_ref, s32[4]{0:T(128)S(1)} %copy-done.4, bf16[512,16,128]{2,1,0:T(8,128)(2,1)S(1)} %all-to-all-done.1.g_ref, ...), custom_call_target="tpu_custom_call" | custom-call | tf_op jit(solution)/shard_map/middle_levels/pallas_call | solution.py:420
  105.7 14.8 %collective-permute-done.10.refs_3_ = bf16[32,16,128]{2,1,0:T(8,128)(2,1)S(1)} collective-permute-done((bf16[32,16,128]{2,1,0:T(8,128)(2,1)S(1)}, bf16[32,16,128]{2,1,0:T(8,128)(2,1)S(1)}, u32[]{:S(2)}, u32[]{:S(2)}) %collective-permute-start.10) | collective-permute-done | bytes 131104 | tf_op jit(solution)/shard_map/ppermute | solution.py:436
  120.4 1.9 %collective-permute-start.3 = (bf16[32,16,128]{2,1,0:T(8,128)(2,1)S(1)}, bf16[32,16,128]{2,1,0:T(8,128)(2,1)S(1)}, u32[]{:S(2)}, u32[]{:S(2)}) collective-permute-start(bf16[32,16,128]{2,1,0:T(8,128)(2,1)S(1)} %get-tuple-element.21), channel_id=1, source_target_pairs={{0,0},{1,4},{2,2},{3,6},{4,1},{5,5},{6,3},{7,7},{8,8},{9,12},{10,1... | collective-permute-start | bytes 393224 | tf_op jit(solution)/shard_map/ppermute | solution.py:436
  122.3 0.0 collective-permute-done.11.refs_4_
  122.4 0.1 collective-permute-start.4
  122.4 0.0 collective-permute-done.12.refs_5_
  122.4 3.6 %collective-permute-start.5 = (bf16[32,16,128]{2,1,0:T(8,128)(2,1)S(1)}, bf16[32,16,128]{2,1,0:T(8,128)(2,1)S(1)}, u32[]{:S(2)}, u32[]{:S(2)}) collective-permute-start(bf16[32,16,128]{2,1,0:T(8,128)(2,1)S(1)} %get-tuple-element.23), channel_id=1, source_target_pairs={{0,16},{1,20},{2,18},{3,22},{4,17},{5,21},{6,19},{7,23},{8,24},{9,... | collective-permute-start | bytes 393224 | tf_op jit(solution)/shard_map/ppermute | solution.py:436
  126.1 0.0 collective-permute-done.13.refs_6_
  126.1 1.0 collective-permute-start.6
  127.1 0.0 collective-permute-done.14.refs_7_
  127.1 9.9 %first_receivers.1.done_ref = f32[8192,128]{1,0:T(8,128)S(1)} custom-call(s32[5]{0:T(128)S(1)} %stack.23.me_ref, s32[4]{0:T(128)S(1)} %copy-done.4, s32[8192]{0:T(1024)S(1)} %inverse_slots.1.inverse_ref, bf16[8192,128]{1,0:T(8,128)(2,1)S(1)} %copy-done.1, bf16[32,16,128]{2,1,0:T(8,128)(2,1)S(1)} %collective-permute-done.7.refs_0_, ...), custom_call_target="tpu_custom_call" | custom-call | tf_op jit(solution)/shard_map/first_receivers/pallas_call | solution.py:440
  137.0 0.0 collective-permute-done.3.p0
  137.0 0.0 collective-permute-done.4.p1
  137.0 0.9 collective-permute-done.5.p2
  137.9 0.0 collective-permute-done.6.p3
  137.9 5.7 %last_receivers.1 = bf16[8192,128]{1,0:T(8,128)(2,1)} custom-call(s32[5]{0:T(128)S(1)} %stack.23.me_ref, s32[4]{0:T(128)S(1)} %copy-done.4, s32[8192]{0:T(1024)S(1)} %inverse_slots.1.inverse_ref, bf16[8192,128]{1,0:T(8,128)(2,1)S(1)} %copy-done.1, bf16[32,16,128]{2,1,0:T(8,128)(2,1)S(1)} %collective-permute-done.3.p0, ...), custom_call_target="tpu_custom_call" | custom-call | tf_op jit(solution)/shard_map/last_receivers/pallas_call | solution.py:449
  (7 shorter events, 0.0 us)
Async XLA Ops:
  1.7 22.5 %all-to-all-start = ((bf16[128,8,128]{2,1,0:T(8,128)(2,1)}), bf16[128,8,128]{2,1,0:T(8,128)(2,1)S(1)}, u32[]{:S(2)}, u32[]{:S(2)}) async-start(bf16[128,8,128]{2,1,0:T(8,128)(2,1)} %bitcast.7), calls=%async_computation | async-start | bytes 524288 | tf_op jit(solution)/shard_map/all_to_all | solution.py:377
  24.2 29.4 %copy-start.5 = (s32[8192]{0:T(1024)S(1)}, s32[8192]{0:T(1024)}, u32[]{:S(2)}) copy-start(s32[8192]{0:T(1024)} %slot_ref.1) | copy-start | bytes 98308
  24.2 55.4 %all-to-all-start.1 = ((bf16[512,16,128]{2,1,0:T(8,128)(2,1)}), bf16[512,16,128]{2,1,0:T(8,128)(2,1)S(1)}, u32[]{:S(2)}, u32[]{:S(2)}) async-start(bf16[512,16,128]{2,1,0:T(8,128)(2,1)} %source_side.1), calls=%async_computation.1 | async-start | bytes 4194304 | tf_op jit(solution)/shard_map/all_to_all | solution.py:404
  30.1 23.6 %collective-permute-start.1 = (bf16[128,8,128]{2,1,0:T(8,128)(2,1)S(1)}, bf16[128,8,128]{2,1,0:T(8,128)(2,1)S(1)}, u32[]{:S(2)}, u32[]{:S(2)}) collective-permute-start(bf16[128,8,128]{2,1,0:T(8,128)(2,1)S(1)} %all-to-all-done.f0), channel_id=1, source_target_pairs={{0,17},{1,16},{2,19},{3,18},{4,21},{5,20},{6,23},{7,22},{8,25},{9,... | collective-permute-start | bytes 786440 | tf_op jit(solution)/shard_map/ppermute | solution.py:381
  31.8 47.7 %copy-start = (bf16[8,2,2,64,128]{4,3,2,1,0:T(8,128)(2,1)S(1)}, bf16[8,2,2,64,128]{4,3,2,1,0:T(8,128)(2,1)}, u32[]{:S(2)}) copy-start(bf16[8,2,2,64,128]{4,3,2,1,0:T(8,128)(2,1)} %tr_ref.5) | copy-start | bytes 1572868
  31.8 47.7 %copy-start.4 = (s32[4]{0:T(128)S(1)}, s32[4]{0:T(128)}, u32[]{:S(2)}) copy-start(s32[4]{0:T(128)} %bits_ref.11) | copy-start | bytes 52
  31.8 34.1 %collective-permute-start.2 = (bf16[128,8,128]{2,1,0:T(8,128)(2,1)S(1)}, bf16[128,8,128]{2,1,0:T(8,128)(2,1)S(1)}, u32[]{:S(2)}, u32[]{:S(2)}) collective-permute-start(bf16[128,8,128]{2,1,0:T(8,128)(2,1)S(1)} %all-to-all-done.f0), channel_id=1, source_target_pairs={{0,16},{1,17},{2,18},{3,19},{4,20},{5,21},{6,22},{7,23},{8,24},{9,... | collective-permute-start | bytes 786440 | tf_op jit(solution)/shard_map/ppermute | solution.py:381
  31.9 33.4 %collective-permute-start = (bf16[128,8,128]{2,1,0:T(8,128)(2,1)S(1)}, bf16[128,8,128]{2,1,0:T(8,128)(2,1)S(1)}, u32[]{:S(2)}, u32[]{:S(2)}) collective-permute-start(bf16[128,8,128]{2,1,0:T(8,128)(2,1)S(1)} %all-to-all-done.f0), channel_id=1, source_target_pairs={{0,1},{1,0},{2,3},{3,2},{4,5},{5,4},{6,7},{7,6},{8,9},{9,8},{10,11... | collective-permute-start | bytes 786440 | tf_op jit(solution)/shard_map/ppermute | solution.py:381
  65.3 0.7 copy-start.2
  79.6 1.0 copy-start.3
  83.9 13.6 %collective-permute-start.7 = (bf16[32,16,128]{2,1,0:T(8,128)(2,1)S(1)}, bf16[32,16,128]{2,1,0:T(8,128)(2,1)S(1)}, u32[]{:S(2)}, u32[]{:S(2)}) collective-permute-start(bf16[32,16,128]{2,1,0:T(8,128)(2,1)S(1)} %get-tuple-element.25), channel_id=1, source_target_pairs={{0,0},{1,4},{2,2},{3,6},{4,1},{5,5},{6,3},{7,7},{8,8},{9,12},{10,1... | collective-permute-start | bytes 393224 | tf_op jit(solution)/shard_map/ppermute | solution.py:436
  85.9 14.6 %collective-permute-start.8 = (bf16[32,16,128]{2,1,0:T(8,128)(2,1)S(1)}, bf16[32,16,128]{2,1,0:T(8,128)(2,1)S(1)}, u32[]{:S(2)}, u32[]{:S(2)}) collective-permute-start(bf16[32,16,128]{2,1,0:T(8,128)(2,1)S(1)} %get-tuple-element.26), channel_id=1, source_target_pairs={{0,4},{1,0},{2,6},{3,2},{4,5},{5,1},{6,7},{7,3},{8,12},{9,8},{10,1... | collective-permute-start | bytes 393224 | tf_op jit(solution)/shard_map/ppermute | solution.py:436
  86.1 16.0 %collective-permute-start.9 = (bf16[32,16,128]{2,1,0:T(8,128)(2,1)S(1)}, bf16[32,16,128]{2,1,0:T(8,128)(2,1)S(1)}, u32[]{:S(2)}, u32[]{:S(2)}) collective-permute-start(bf16[32,16,128]{2,1,0:T(8,128)(2,1)S(1)} %get-tuple-element.27), channel_id=1, source_target_pairs={{0,16},{1,20},{2,18},{3,22},{4,17},{5,21},{6,19},{7,23},{8,24},{9,... | collective-permute-start | bytes 393224 | tf_op jit(solution)/shard_map/ppermute | solution.py:436
  95.4 31.7 %copy-start.1 = (bf16[8192,128]{1,0:T(8,128)(2,1)S(1)}, bf16[8192,128]{1,0:T(8,128)(2,1)}, u32[]{:S(2)}) copy-start(bf16[8192,128]{1,0:T(8,128)(2,1)} %ri_ref.3) | copy-start | bytes 6291460
  95.4 27.0 %collective-permute-start.11 = (bf16[64,16,128]{2,1,0:T(8,128)(2,1)S(1)}, bf16[64,16,128]{2,1,0:T(8,128)(2,1)S(1)}, u32[]{:S(2)}, u32[]{:S(2)}) collective-permute-start(bf16[64,16,128]{2,1,0:T(8,128)(2,1)S(1)} %get-tuple-element.29), channel_id=1, source_target_pairs={{0,0},{1,4},{2,2},{3,6},{4,1},{5,5},{6,3},{7,7},{8,8},{9,12},{10,1... | collective-permute-start | bytes 786440 | tf_op jit(solution)/shard_map/ppermute | solution.py:436
  97.4 25.0 %collective-permute-start.12 = (bf16[64,16,128]{2,1,0:T(8,128)(2,1)S(1)}, bf16[64,16,128]{2,1,0:T(8,128)(2,1)S(1)}, u32[]{:S(2)}, u32[]{:S(2)}) collective-permute-start(bf16[64,16,128]{2,1,0:T(8,128)(2,1)S(1)} %get-tuple-element.30), channel_id=1, source_target_pairs={{0,4},{1,0},{2,6},{3,2},{4,5},{5,1},{6,7},{7,3},{8,12},{9,8},{10,1... | collective-permute-start | bytes 786440 | tf_op jit(solution)/shard_map/ppermute | solution.py:436
  97.5 28.5 %collective-permute-start.13 = (bf16[64,16,128]{2,1,0:T(8,128)(2,1)S(1)}, bf16[64,16,128]{2,1,0:T(8,128)(2,1)S(1)}, u32[]{:S(2)}, u32[]{:S(2)}) collective-permute-start(bf16[64,16,128]{2,1,0:T(8,128)(2,1)S(1)} %get-tuple-element.31), channel_id=1, source_target_pairs={{0,16},{1,20},{2,18},{3,22},{4,17},{5,21},{6,19},{7,23},{8,24},{9,... | collective-permute-start | bytes 786440 | tf_op jit(solution)/shard_map/ppermute | solution.py:436
  100.5 19.9 %collective-permute-start.10 = (bf16[32,16,128]{2,1,0:T(8,128)(2,1)S(1)}, bf16[32,16,128]{2,1,0:T(8,128)(2,1)S(1)}, u32[]{:S(2)}, u32[]{:S(2)}) collective-permute-start(bf16[32,16,128]{2,1,0:T(8,128)(2,1)S(1)} %get-tuple-element.28), channel_id=1, source_target_pairs={{0,20},{1,16},{2,22},{3,18},{4,21},{5,17},{6,23},{7,19},{8,28},{9,... | collective-permute-start | bytes 393224 | tf_op jit(solution)/shard_map/ppermute | solution.py:436
  102.2 24.9 %collective-permute-start.14 = (bf16[64,16,128]{2,1,0:T(8,128)(2,1)S(1)}, bf16[64,16,128]{2,1,0:T(8,128)(2,1)S(1)}, u32[]{:S(2)}, u32[]{:S(2)}) collective-permute-start(bf16[64,16,128]{2,1,0:T(8,128)(2,1)S(1)} %get-tuple-element.32), channel_id=1, source_target_pairs={{0,20},{1,16},{2,22},{3,18},{4,21},{5,17},{6,23},{7,19},{8,28},{9,... | collective-permute-start | bytes 786440 | tf_op jit(solution)/shard_map/ppermute | solution.py:436
  120.4 16.6 %collective-permute-start.3 = (bf16[32,16,128]{2,1,0:T(8,128)(2,1)S(1)}, bf16[32,16,128]{2,1,0:T(8,128)(2,1)S(1)}, u32[]{:S(2)}, u32[]{:S(2)}) collective-permute-start(bf16[32,16,128]{2,1,0:T(8,128)(2,1)S(1)} %get-tuple-element.21), channel_id=1, source_target_pairs={{0,0},{1,4},{2,2},{3,6},{4,1},{5,5},{6,3},{7,7},{8,8},{9,12},{10,1... | collective-permute-start | bytes 393224 | tf_op jit(solution)/shard_map/ppermute | solution.py:436
  122.4 14.6 %collective-permute-start.4 = (bf16[32,16,128]{2,1,0:T(8,128)(2,1)S(1)}, bf16[32,16,128]{2,1,0:T(8,128)(2,1)S(1)}, u32[]{:S(2)}, u32[]{:S(2)}) collective-permute-start(bf16[32,16,128]{2,1,0:T(8,128)(2,1)S(1)} %get-tuple-element.22), channel_id=1, source_target_pairs={{0,4},{1,0},{2,6},{3,2},{4,5},{5,1},{6,7},{7,3},{8,12},{9,8},{10,1... | collective-permute-start | bytes 393224 | tf_op jit(solution)/shard_map/ppermute | solution.py:436
  122.4 15.4 %collective-permute-start.5 = (bf16[32,16,128]{2,1,0:T(8,128)(2,1)S(1)}, bf16[32,16,128]{2,1,0:T(8,128)(2,1)S(1)}, u32[]{:S(2)}, u32[]{:S(2)}) collective-permute-start(bf16[32,16,128]{2,1,0:T(8,128)(2,1)S(1)} %get-tuple-element.23), channel_id=1, source_target_pairs={{0,16},{1,20},{2,18},{3,22},{4,17},{5,21},{6,19},{7,23},{8,24},{9,... | collective-permute-start | bytes 393224 | tf_op jit(solution)/shard_map/ppermute | solution.py:436
  126.1 11.8 %collective-permute-start.6 = (bf16[32,16,128]{2,1,0:T(8,128)(2,1)S(1)}, bf16[32,16,128]{2,1,0:T(8,128)(2,1)S(1)}, u32[]{:S(2)}, u32[]{:S(2)}) collective-permute-start(bf16[32,16,128]{2,1,0:T(8,128)(2,1)S(1)} %get-tuple-element.24), channel_id=1, source_target_pairs={{0,20},{1,16},{2,22},{3,18},{4,21},{5,17},{6,23},{7,19},{8,28},{9,... | collective-permute-start | bytes 393224 | tf_op jit(solution)/shard_map/ppermute | solution.py:436

commit v5 on v4

--- a/solution.py
+++ b/solution.py
@@ -11,7 +11,7 @@
 AXES = ("hi", "lo")
 SPLIT = 16
 STACKS = 16
-QUARTERS = ((0,), (1, 2), (3,))
+QUARTERS = ((0,), (1,), (2,), (3,))
 LEAVES = 32
 SPAIRS = 32
 F32 = jnp.float32
@@ -82,8 +82,8 @@
 
 
 def source_kernel(
-    dims, order_ref, bits_ref, ch_hbm, si_hbm, fac_hbm, tr_hbm, out_ref,
-    ch_ref, si_ref, fac_ref, tr_ref, sems, x32, mid_ref, fa, fb, w_ref,
+    dims, order_hbm, bits_ref, ch_hbm, si_hbm, fac_hbm, tr_hbm, out_ref,
+    order_ref, ch_ref, si_ref, fac_ref, tr_ref, sems, x32, mid_ref, fa, fb, w_ref,
 ):
     n_hi, n_lo, share, blocks, rhs = dims
     quarter = rhs // 4
@@ -96,6 +96,7 @@
     copies.append(pltpu.make_async_copy(fac_hbm, fac_ref, sems.at[4]))
     copies.append(pltpu.make_async_copy(tr_hbm.at[pl.ds(0, 2)], tr_ref, sems.at[5]))
     copies.append(pltpu.make_async_copy(si_hbm, si_ref, sems.at[6]))
+    copies.append(pltpu.make_async_copy(order_hbm, order_ref, sems.at[7]))
     for copy in copies[4:6] + copies[:4] + copies[6:]:
         copy.start()
     copies[5].wait()
@@ -113,6 +114,7 @@
         copies[i].wait()
         lax.fori_loop(i * (part // 512), (i + 1) * (part // 512), widen, 0)
     copies[6].wait()
+    copies[7].wait()
 
     def leaf(b):
         first = pl.multiple_of(b * LEAF, LEAF)
@@ -200,7 +202,7 @@
 
 
 def middle_kernel(
-    dims, quarters, me_ref, bits_ref, g_ref, f0, f1, f2, f3, tr_ref, o0, o1, o2, o3, x, x2, fa, fb, w_ref
+    dims, quarters, me_ref, bits_ref, g_ref, f0, f1, f2, f3, tr_ref, after_ref, o0, o1, o2, o3, x, x2, fa, fb, w_ref
 ):
     n_hi, n_lo, share, blocks, rhs = dims
     rows = rhs // 4
@@ -383,14 +385,15 @@
     sent = pl.pallas_call(
         functools.partial(source_kernel, dims),
         out_shape=jax.ShapeDtypeStruct((devices * 4 * share, quarter, 128), BF16),
-        in_specs=[on_smem(), on_smem()] + [on_any()] * 4,
+        in_specs=[on_any(), on_smem()] + [on_any()] * 4,
         out_specs=on_vmem(),
         scratch_shapes=[
+            pltpu.SMEM((points,), jnp.int32),
             pltpu.VMEM((points, 128), BF16),
             pltpu.VMEM((points, 128), BF16),
             pltpu.VMEM((blocks * 8, 128), BF16),
             pltpu.VMEM((2,) + transfers.shape[1:], BF16),
-            pltpu.SemaphoreType.DMA((7,)),
+            pltpu.SemaphoreType.DMA((8,)),
             pltpu.VMEM((points, 128), F32),
             pltpu.VMEM((blocks, rhs, 128), BF16),
             pltpu.VMEM((blocks * 8, 128), F32),
@@ -412,15 +415,15 @@
         cost_estimate=pl.CostEstimate(flops=10**10, bytes_accessed=2**25, transcendentals=0),
         name="inverse_slots",
     )(receiver_slot, facs[3])
-    facs[1], inverse = lax.optimization_barrier((facs[1], inverse))
 
     homes = []
+    after = inverse
     for quarters in QUARTERS:
         count = len(quarters) * blocks // 4
         pieces = pl.pallas_call(
             functools.partial(middle_kernel, dims, quarters),
             out_shape=[jax.ShapeDtypeStruct((count, quarter, 128), BF16)] * 4,
-            in_specs=[on_smem(), on_smem()] + [on_vmem()] * 6,
+            in_specs=[on_smem(), on_smem()] + [on_vmem()] * 6 + [on_any()],
             out_specs=[on_vmem()] * 4,
             scratch_shapes=[
                 pltpu.VMEM((blocks, quarter, 128), BF16),
@@ -431,7 +434,8 @@
             ],
             compiler_params=params(16),
             name="middle_levels",
-        )(me, level_bits, arrived, *facs, transfers)
+        )(me, level_bits, arrived, *facs, transfers, after)
+        after = pieces[0]
         homes.append(
             [lax.ppermute(pieces[j], AXES, [(s, swapped(s, j)) for s in range(devices)]) for j in range(4)]
         )

time: 144 us -> 139 us (0.965)
  waiting for transfers between devices: 50.5 us -> 40.2 us
  starting transfers between devices: 34.1 us -> 38 us
    ppermute x12 -> x16, waiting for transfers between devices: 15.7 us -> 5.35 us  [per_device(): lax.ppermute(pieces[j], AXES, [(s, swapped(s, j)) for s in range(devices)])]
    ppermute x12 -> x16, starting transfers between devices: 18.9 us -> 22.8 us  [per_device(): lax.ppermute(pieces[j], AXES, [(s, swapped(s, j)) for s in range(devices)])]
    pallas_call x3 -> x4, Pallas kernels: 12.7 us -> 13.7 us  [per_device(): pl.pallas_call(functools.partial(middle_kernel, dims, quarters), out_shap...]
  transfers between devices with their start and end apart: 17 -> 21, of which waited for: 4 -> 7; matrix products, arithmetic and copies ran while one was open for 0% -> 0% of each run, Pallas kernels for 32% -> 34%
where the time goes in v5:
time: 139 us; the launch traced here: 138 us
  Pallas kernels  55.8 us (40%)
  waiting for transfers between devices  40.2 us (29%)
  starting transfers between devices  38 us (27%)
  local copies, waits for them, and re-layouts  3.42 us (2%)
    ppermute x16, starting transfers between devices, per_device(): lax.ppermute(pieces[j], AXES, [(s, swapped(s, j)) for s in range(devices)])  22.8 us
    ppermute x3, waiting for transfers between devices, per_device(): lax.ppermute(spread, AXES, [(s, s ^ mask) for s in range(devices)])  21.2 us
    pallas_call x1, Pallas kernels, per_device(): pl.pallas_call(functools.partial(source_kernel, dims), out_shape=jax.Shap...  14.9 us
    pallas_call x4, Pallas kernels, per_device(): pl.pallas_call(functools.partial(middle_kernel, dims, quarters), out_shap...  13.7 us
    all_to_all x1, waiting for transfers between devices, per_device(): lax.all_to_all(sent, AXES, split_axis=0, concat_axis=0, tiled=True)  13.6 us
    pallas_call x1, Pallas kernels, per_device(): pl.pallas_call(functools.partial(inverse_kernel, dims), out_shape=jax.Sha...  11.6 us
    pallas_call x1, Pallas kernels, per_device(): pl.pallas_call(functools.partial(first_receivers, dims), out_shape=jax.Sh...  9.93 us
    all_to_all x1, starting transfers between devices, per_device(): lax.all_to_all(spread.reshape(blocks, 8, 128), AXES, split_axis=0, concat...  7.1 us
  transfers between devices with their start and end apart: 21, of which 7 were waited for; matrix products, arithmetic and copies ran while one was open for 0% of the time, Pallas kernels for 34%

profile of v5, /device:TPU:1, one launch (start us, length us, event | category | flops | bytes accessed | tf_op | source)
XLA Modules:
  0.0 137.9 jit_solution(13923351479180640562)
XLA Ops:
  0.0 1.7 %copy.9 = bf16[4,2,2,2,4,8,128]{6,5,4,1,2,3,0:T(8,128)(2,1)} copy(bf16[4,2,2,2,4,8,128]{6,5,4,3,2,1,0:T(8,128)(2,1)} %bitcast.10) | data formatting | bytes 524288 | tf_op jit(solution)/shard_map/reshape | solution.py:378
  1.7 7.1 %all-to-all-start = ((bf16[128,8,128]{2,1,0:T(8,128)(2,1)}), bf16[128,8,128]{2,1,0:T(8,128)(2,1)S(1)}, u32[]{:S(2)}, u32[]{:S(2)}) async-start(bf16[128,8,128]{2,1,0:T(8,128)(2,1)} %bitcast.7), calls=%async_computation | async-start | bytes 524288 | tf_op jit(solution)/shard_map/all_to_all | solution.py:379
  8.8 14.9 %source_side.1 = bf16[512,16,128]{2,1,0:T(8,128)(2,1)} custom-call(s32[8192]{0:T(1024)} %order_hbm.1, s32[4]{0:T(128)} %bits_ref.13, bf16[8192,128]{1,0:T(8,128)(2,1)} %ch_hbm.1, bf16[8192,128]{1,0:T(8,128)(2,1)} %si_hbm.1, bf16[1024,128]{1,0:T(8,128)(2,1)} %bitcast.11, bf16[8,2,2,64,128]{4,3,2,1,0:T(8,128)(2,1)} %tr_ref.7), custom_call_target="tpu_custom_call" | custom-call | tf_op jit(solution)/shard_map/source_side/pallas_call | solution.py:385
  23.7 0.0 copy-start.5
  23.7 5.8 %all-to-all-start.1 = ((bf16[512,16,128]{2,1,0:T(8,128)(2,1)}), bf16[512,16,128]{2,1,0:T(8,128)(2,1)S(1)}, u32[]{:S(2)}, u32[]{:S(2)}) async-start(bf16[512,16,128]{2,1,0:T(8,128)(2,1)} %source_side.1), calls=%async_computation.1 | async-start | bytes 4194304 | tf_op jit(solution)/shard_map/all_to_all | solution.py:407
  29.5 1.7 %collective-permute-start = (bf16[128,8,128]{2,1,0:T(8,128)(2,1)S(1)}, bf16[128,8,128]{2,1,0:T(8,128)(2,1)S(1)}, u32[]{:S(2)}, u32[]{:S(2)}) collective-permute-start(bf16[128,8,128]{2,1,0:T(8,128)(2,1)S(1)} %all-to-all-done.f0), channel_id=1, source_target_pairs={{0,17},{1,16},{2,19},{3,18},{4,21},{5,20},{6,23},{7,22},{8,25},{9,... | collective-permute-start | bytes 786440 | tf_op jit(solution)/shard_map/ppermute | solution.py:383
  31.2 0.1 stack.23.me_ref
  31.3 0.0 collective-permute-start.2
  31.4 0.5 collective-permute-start.1
  31.9 21.2 %collective-permute-done.after_ref.f3 = bf16[128,8,128]{2,1,0:T(8,128)(2,1)S(1)} collective-permute-done((bf16[128,8,128]{2,1,0:T(8,128)(2,1)S(1)}, bf16[128,8,128]{2,1,0:T(8,128)(2,1)S(1)}, u32[]{:S(2)}, u32[]{:S(2)}) %collective-permute-start) | collective-permute-done | bytes 262176 | tf_op jit(solution)/shard_map/ppermute | solution.py:383
  53.1 11.6 %inverse_slots.1.after_ref.inverse_ref = s32[8192]{0:T(1024)S(1)} custom-call(s32[8192]{0:T(1024)S(1)} %copy-done.5, bf16[128,8,128]{2,1,0:T(8,128)(2,1)S(1)} %collective-permute-done.after_ref.f3), custom_call_target="tpu_custom_call" | custom-call | flops 10000000000 | bytes 33554432 | tf_op jit(solution)/shard_map/inverse_slots/pallas_call | solution.py:409
  64.7 0.0 collective-permute-done.2.f2
  64.7 0.0 collective-permute-done.1.f1
  64.8 0.7 copy-done.2
  65.5 13.6 %all-to-all-done.1.g_ref = bf16[512,16,128]{2,1,0:T(8,128)(2,1)S(1)} async-done(((bf16[512,16,128]{2,1,0:T(8,128)(2,1)}), bf16[512,16,128]{2,1,0:T(8,128)(2,1)S(1)}, u32[]{:S(2)}, u32[]{:S(2)}) %all-to-all-start.1) | async-done | bytes 2097184 | tf_op jit(solution)/shard_map/all_to_all | solution.py:407
  79.1 0.9 copy-done.3
  80.0 3.4 %middle_levels.4 = (bf16[32,16,128]{2,1,0:T(8,128)(2,1)S(1)}, bf16[32,16,128]{2,1,0:T(8,128)(2,1)S(1)}, bf16[32,16,128]{2,1,0:T(8,128)(2,1)S(1)}, bf16[32,16,128]{2,1,0:T(8,128)(2,1)S(1)}) custom-call(s32[5]{0:T(128)S(1)} %stack.23.me_ref, s32[4]{0:T(128)S(1)} %copy-done.4, bf16[512,16,128]{2,1,0:T(8,128)(2,1)S(1)} %all-to-all-done.1.g_ref, ...), custom_call_target="tpu_custom_call" | custom-call | tf_op jit(solution)/shard_map/middle_levels/pallas_call | solution.py:423
  83.4 0.9 collective-permute-start.8
  84.3 1.7 %collective-permute-start.10 = (bf16[32,16,128]{2,1,0:T(8,128)(2,1)S(1)}, bf16[32,16,128]{2,1,0:T(8,128)(2,1)S(1)}, u32[]{:S(2)}, u32[]{:S(2)}) collective-permute-start(bf16[32,16,128]{2,1,0:T(8,128)(2,1)S(1)} %get-tuple-element.30), channel_id=1, source_target_pairs={{0,20},{1,16},{2,22},{3,18},{4,21},{5,17},{6,23},{7,19},{8,28},{9,... | collective-permute-start | bytes 393224 | tf_op jit(solution)/shard_map/ppermute | solution.py:440
  86.0 3.5 %collective-permute-start.7 = (bf16[32,16,128]{2,1,0:T(8,128)(2,1)S(1)}, bf16[32,16,128]{2,1,0:T(8,128)(2,1)S(1)}, u32[]{:S(2)}, u32[]{:S(2)}) collective-permute-start(bf16[32,16,128]{2,1,0:T(8,128)(2,1)S(1)} %get-tuple-element.21.after_ref), channel_id=1, source_target_pairs={{0,0},{1,4},{2,2},{3,6},{4,1},{5,5},{6,3},{7,7},{8,8},{9,12},{10,1... | collective-permute-start | bytes 393224 | tf_op jit(solution)/shard_map/ppermute | solution.py:440
  89.5 3.4 %middle_levels.5 = (bf16[32,16,128]{2,1,0:T(8,128)(2,1)S(1)}, bf16[32,16,128]{2,1,0:T(8,128)(2,1)S(1)}, bf16[32,16,128]{2,1,0:T(8,128)(2,1)S(1)}, bf16[32,16,128]{2,1,0:T(8,128)(2,1)S(1)}) custom-call(s32[5]{0:T(128)S(1)} %stack.23.me_ref, s32[4]{0:T(128)S(1)} %copy-done.4, bf16[512,16,128]{2,1,0:T(8,128)(2,1)S(1)} %all-to-all-done.1.g_ref, ...), custom_call_target="tpu_custom_call" | custom-call | tf_op jit(solution)/shard_map/middle_levels/pallas_call | solution.py:423
  92.9 0.2 collective-permute-start.12
  93.2 0.5 collective-permute-done.8.refs_1_
  93.7 0.6 collective-permute-start.13
  94.3 3.4 %middle_levels.6 = (bf16[32,16,128]{2,1,0:T(8,128)(2,1)S(1)}, bf16[32,16,128]{2,1,0:T(8,128)(2,1)S(1)}, bf16[32,16,128]{2,1,0:T(8,128)(2,1)S(1)}, bf16[32,16,128]{2,1,0:T(8,128)(2,1)S(1)}) custom-call(s32[5]{0:T(128)S(1)} %stack.23.me_ref, s32[4]{0:T(128)S(1)} %copy-done.4, bf16[512,16,128]{2,1,0:T(8,128)(2,1)S(1)} %all-to-all-done.1.g_ref, ...), custom_call_target="tpu_custom_call" | custom-call | tf_op jit(solution)/shard_map/middle_levels/pallas_call | solution.py:423
  97.8 0.0 copy-start.1
  97.8 0.0 collective-permute-done.9.refs_2_
  97.8 2.0 %collective-permute-start.14 = (bf16[32,16,128]{2,1,0:T(8,128)(2,1)S(1)}, bf16[32,16,128]{2,1,0:T(8,128)(2,1)S(1)}, u32[]{:S(2)}, u32[]{:S(2)}) collective-permute-start(bf16[32,16,128]{2,1,0:T(8,128)(2,1)S(1)} %get-tuple-element.33), channel_id=1, source_target_pairs={{0,20},{1,16},{2,22},{3,18},{4,21},{5,17},{6,23},{7,19},{8,28},{9,... | collective-permute-start | bytes 393224 | tf_op jit(solution)/shard_map/ppermute | solution.py:440
  99.8 2.9 %collective-permute-start.11 = (bf16[32,16,128]{2,1,0:T(8,128)(2,1)S(1)}, bf16[32,16,128]{2,1,0:T(8,128)(2,1)S(1)}, u32[]{:S(2)}, u32[]{:S(2)}) collective-permute-start(bf16[32,16,128]{2,1,0:T(8,128)(2,1)S(1)} %get-tuple-element.22.after_ref), channel_id=1, source_target_pairs={{0,0},{1,4},{2,2},{3,6},{4,1},{5,5},{6,3},{7,7},{8,8},{9,12},{10,1... | collective-permute-start | bytes 393224 | tf_op jit(solution)/shard_map/ppermute | solution.py:440
  102.7 0.0 collective-permute-done.7.refs_0_
  102.7 0.1 collective-permute-start.16
  102.8 0.7 collective-permute-done.12.refs_5_
  103.5 1.4 %collective-permute-start.17 = (bf16[32,16,128]{2,1,0:T(8,128)(2,1)S(1)}, bf16[32,16,128]{2,1,0:T(8,128)(2,1)S(1)}, u32[]{:S(2)}, u32[]{:S(2)}) collective-permute-start(bf16[32,16,128]{2,1,0:T(8,128)(2,1)S(1)} %get-tuple-element.35), channel_id=1, source_target_pairs={{0,16},{1,20},{2,18},{3,22},{4,17},{5,21},{6,19},{7,23},{8,24},{9,... | collective-permute-start | bytes 393224 | tf_op jit(solution)/shard_map/ppermute | solution.py:440
  104.9 0.0 collective-permute-done.13.refs_6_
  104.9 1.6 %collective-permute-start.18 = (bf16[32,16,128]{2,1,0:T(8,128)(2,1)S(1)}, bf16[32,16,128]{2,1,0:T(8,128)(2,1)S(1)}, u32[]{:S(2)}, u32[]{:S(2)}) collective-permute-start(bf16[32,16,128]{2,1,0:T(8,128)(2,1)S(1)} %get-tuple-element.36), channel_id=1, source_target_pairs={{0,20},{1,16},{2,22},{3,18},{4,21},{5,17},{6,23},{7,19},{8,28},{9,... | collective-permute-start | bytes 393224 | tf_op jit(solution)/shard_map/ppermute | solution.py:440
  106.5 3.4 %middle_levels.7 = (bf16[32,16,128]{2,1,0:T(8,128)(2,1)S(1)}, bf16[32,16,128]{2,1,0:T(8,128)(2,1)S(1)}, bf16[32,16,128]{2,1,0:T(8,128)(2,1)S(1)}, bf16[32,16,128]{2,1,0:T(8,128)(2,1)S(1)}) custom-call(s32[5]{0:T(128)S(1)} %stack.23.me_ref, s32[4]{0:T(128)S(1)} %copy-done.4, bf16[512,16,128]{2,1,0:T(8,128)(2,1)S(1)} %all-to-all-done.1.g_ref, ...), custom_call_target="tpu_custom_call" | custom-call | tf_op jit(solution)/shard_map/middle_levels/pallas_call | solution.py:423
  109.9 0.0 collective-permute-done.14.refs_7_
  109.9 2.3 %collective-permute-start.15 = (bf16[32,16,128]{2,1,0:T(8,128)(2,1)S(1)}, bf16[32,16,128]{2,1,0:T(8,128)(2,1)S(1)}, u32[]{:S(2)}, u32[]{:S(2)}) collective-permute-start(bf16[32,16,128]{2,1,0:T(8,128)(2,1)S(1)} %get-tuple-element.23.after_ref), channel_id=1, source_target_pairs={{0,0},{1,4},{2,2},{3,6},{4,1},{5,5},{6,3},{7,7},{8,8},{9,12},{10,1... | collective-permute-start | bytes 393224 | tf_op jit(solution)/shard_map/ppermute | solution.py:440
  112.3 1.3 collective-permute-done.11.refs_4_
  113.6 2.8 %collective-permute-start.3 = (bf16[32,16,128]{2,1,0:T(8,128)(2,1)S(1)}, bf16[32,16,128]{2,1,0:T(8,128)(2,1)S(1)}, u32[]{:S(2)}, u32[]{:S(2)}) collective-permute-start(bf16[32,16,128]{2,1,0:T(8,128)(2,1)S(1)} %get-tuple-element.24), channel_id=1, source_target_pairs={{0,0},{1,4},{2,2},{3,6},{4,1},{5,5},{6,3},{7,7},{8,8},{9,12},{10,1... | collective-permute-start | bytes 393224 | tf_op jit(solution)/shard_map/ppermute | solution.py:440
  116.4 0.0 collective-permute-done.16.refs_9_
  116.4 0.1 collective-permute-start.4
  116.5 1.4 collective-permute-done.17.refs_10_
  117.8 1.9 %collective-permute-start.5 = (bf16[32,16,128]{2,1,0:T(8,128)(2,1)S(1)}, bf16[32,16,128]{2,1,0:T(8,128)(2,1)S(1)}, u32[]{:S(2)}, u32[]{:S(2)}) collective-permute-start(bf16[32,16,128]{2,1,0:T(8,128)(2,1)S(1)} %get-tuple-element.26), channel_id=1, source_target_pairs={{0,16},{1,20},{2,18},{3,22},{4,17},{5,21},{6,19},{7,23},{8,24},{9,... | collective-permute-start | bytes 393224 | tf_op jit(solution)/shard_map/ppermute | solution.py:440
  119.8 0.8 collective-permute-start.6
  120.5 9.9 %first_receivers.1.done_ref = f32[8192,128]{1,0:T(8,128)S(1)} custom-call(s32[5]{0:T(128)S(1)} %stack.23.me_ref, s32[4]{0:T(128)S(1)} %copy-done.4, s32[8192]{0:T(1024)S(1)} %inverse_slots.1.after_ref.inverse_ref, bf16[8192,128]{1,0:T(8,128)(2,1)S(1)} %copy-done.1, bf16[32,16,128]{2,1,0:T(8,128)(2,1)S(1)} %collective-permute-done.7.refs_0_, ...), custom_call_target="tpu_custom_call" | custom-call | tf_op jit(solution)/shard_map/first_receivers/pallas_call | solution.py:444
  130.5 1.5 %collective-permute-done.5.p2 = bf16[32,16,128]{2,1,0:T(8,128)(2,1)S(1)} collective-permute-done((bf16[32,16,128]{2,1,0:T(8,128)(2,1)S(1)}, bf16[32,16,128]{2,1,0:T(8,128)(2,1)S(1)}, u32[]{:S(2)}, u32[]{:S(2)}) %collective-permute-start.5) | collective-permute-done | bytes 131104 | tf_op jit(solution)/shard_map/ppermute | solution.py:440
  132.0 5.7 %last_receivers.1 = bf16[8192,128]{1,0:T(8,128)(2,1)} custom-call(s32[5]{0:T(128)S(1)} %stack.23.me_ref, s32[4]{0:T(128)S(1)} %copy-done.4, s32[8192]{0:T(1024)S(1)} %inverse_slots.1.after_ref.inverse_ref, bf16[8192,128]{1,0:T(8,128)(2,1)S(1)} %copy-done.1, bf16[32,16,128]{2,1,0:T(8,128)(2,1)S(1)} %collective-permute-done.3.p0, ...), custom_call_target="tpu_custom_call" | custom-call | tf_op jit(solution)/shard_map/last_receivers/pallas_call | solution.py:453
  (16 shorter events, 0.0 us)
Async XLA Ops:
  1.7 22.0 %all-to-all-start = ((bf16[128,8,128]{2,1,0:T(8,128)(2,1)}), bf16[128,8,128]{2,1,0:T(8,128)(2,1)S(1)}, u32[]{:S(2)}, u32[]{:S(2)}) async-start(bf16[128,8,128]{2,1,0:T(8,128)(2,1)} %bitcast.7), calls=%async_computation | async-start | bytes 524288 | tf_op jit(solution)/shard_map/all_to_all | solution.py:379
  23.7 29.4 %copy-start.5 = (s32[8192]{0:T(1024)S(1)}, s32[8192]{0:T(1024)}, u32[]{:S(2)}) copy-start(s32[8192]{0:T(1024)} %slot_ref.1) | copy-start | bytes 98308
  23.7 55.4 %all-to-all-start.1 = ((bf16[512,16,128]{2,1,0:T(8,128)(2,1)}), bf16[512,16,128]{2,1,0:T(8,128)(2,1)S(1)}, u32[]{:S(2)}, u32[]{:S(2)}) async-start(bf16[512,16,128]{2,1,0:T(8,128)(2,1)} %source_side.1), calls=%async_computation.1 | async-start | bytes 4194304 | tf_op jit(solution)/shard_map/all_to_all | solution.py:407
  29.5 23.6 %collective-permute-start = (bf16[128,8,128]{2,1,0:T(8,128)(2,1)S(1)}, bf16[128,8,128]{2,1,0:T(8,128)(2,1)S(1)}, u32[]{:S(2)}, u32[]{:S(2)}) collective-permute-start(bf16[128,8,128]{2,1,0:T(8,128)(2,1)S(1)} %all-to-all-done.f0), channel_id=1, source_target_pairs={{0,17},{1,16},{2,19},{3,18},{4,21},{5,20},{6,23},{7,22},{8,25},{9,... | collective-permute-start | bytes 786440 | tf_op jit(solution)/shard_map/ppermute | solution.py:383
  31.3 47.7 %copy-start = (bf16[8,2,2,64,128]{4,3,2,1,0:T(8,128)(2,1)S(1)}, bf16[8,2,2,64,128]{4,3,2,1,0:T(8,128)(2,1)}, u32[]{:S(2)}) copy-start(bf16[8,2,2,64,128]{4,3,2,1,0:T(8,128)(2,1)} %tr_ref.7) | copy-start | bytes 1572868
  31.3 47.7 %copy-start.4 = (s32[4]{0:T(128)S(1)}, s32[4]{0:T(128)}, u32[]{:S(2)}) copy-start(s32[4]{0:T(128)} %bits_ref.13) | copy-start | bytes 52
  31.3 33.4 %collective-permute-start.2 = (bf16[128,8,128]{2,1,0:T(8,128)(2,1)S(1)}, bf16[128,8,128]{2,1,0:T(8,128)(2,1)S(1)}, u32[]{:S(2)}, u32[]{:S(2)}) collective-permute-start(bf16[128,8,128]{2,1,0:T(8,128)(2,1)S(1)} %all-to-all-done.f0), channel_id=1, source_target_pairs={{0,16},{1,17},{2,18},{3,19},{4,20},{5,21},{6,22},{7,23},{8,24},{9,... | collective-permute-start | bytes 786440 | tf_op jit(solution)/shard_map/ppermute | solution.py:383
  31.4 33.4 %collective-permute-start.1 = (bf16[128,8,128]{2,1,0:T(8,128)(2,1)S(1)}, bf16[128,8,128]{2,1,0:T(8,128)(2,1)S(1)}, u32[]{:S(2)}, u32[]{:S(2)}) collective-permute-start(bf16[128,8,128]{2,1,0:T(8,128)(2,1)S(1)} %all-to-all-done.f0), channel_id=1, source_target_pairs={{0,1},{1,0},{2,3},{3,2},{4,5},{5,4},{6,7},{7,6},{8,9},{9,8},{10,11... | collective-permute-start | bytes 786440 | tf_op jit(solution)/shard_map/ppermute | solution.py:383
  64.8 0.7 copy-start.2
  79.1 1.0 copy-start.3
  83.4 10.3 %collective-permute-start.8 = (bf16[32,16,128]{2,1,0:T(8,128)(2,1)S(1)}, bf16[32,16,128]{2,1,0:T(8,128)(2,1)S(1)}, u32[]{:S(2)}, u32[]{:S(2)}) collective-permute-start(bf16[32,16,128]{2,1,0:T(8,128)(2,1)S(1)} %get-tuple-element.28), channel_id=1, source_target_pairs={{0,4},{1,0},{2,6},{3,2},{4,5},{5,1},{6,7},{7,3},{8,12},{9,8},{10,1... | collective-permute-start | bytes 393224 | tf_op jit(solution)/shard_map/ppermute | solution.py:440
  84.3 13.5 %collective-permute-start.9 = (bf16[32,16,128]{2,1,0:T(8,128)(2,1)S(1)}, bf16[32,16,128]{2,1,0:T(8,128)(2,1)S(1)}, u32[]{:S(2)}, u32[]{:S(2)}) collective-permute-start(bf16[32,16,128]{2,1,0:T(8,128)(2,1)S(1)} %get-tuple-element.29), channel_id=1, source_target_pairs={{0,16},{1,20},{2,18},{3,22},{4,17},{5,21},{6,19},{7,23},{8,24},{9,... | collective-permute-start | bytes 393224 | tf_op jit(solution)/shard_map/ppermute | solution.py:440
  84.3 15.5 %collective-permute-start.10 = (bf16[32,16,128]{2,1,0:T(8,128)(2,1)S(1)}, bf16[32,16,128]{2,1,0:T(8,128)(2,1)S(1)}, u32[]{:S(2)}, u32[]{:S(2)}) collective-permute-start(bf16[32,16,128]{2,1,0:T(8,128)(2,1)S(1)} %get-tuple-element.30), channel_id=1, source_target_pairs={{0,20},{1,16},{2,22},{3,18},{4,21},{5,17},{6,23},{7,19},{8,28},{9,... | collective-permute-start | bytes 393224 | tf_op jit(solution)/shard_map/ppermute | solution.py:440
  86.0 16.7 %collective-permute-start.7 = (bf16[32,16,128]{2,1,0:T(8,128)(2,1)S(1)}, bf16[32,16,128]{2,1,0:T(8,128)(2,1)S(1)}, u32[]{:S(2)}, u32[]{:S(2)}) collective-permute-start(bf16[32,16,128]{2,1,0:T(8,128)(2,1)S(1)} %get-tuple-element.21.after_ref), channel_id=1, source_target_pairs={{0,0},{1,4},{2,2},{3,6},{4,1},{5,5},{6,3},{7,7},{8,8},{9,12},{10,1... | collective-permute-start | bytes 393224 | tf_op jit(solution)/shard_map/ppermute | solution.py:440
  92.9 10.6 %collective-permute-start.12 = (bf16[32,16,128]{2,1,0:T(8,128)(2,1)S(1)}, bf16[32,16,128]{2,1,0:T(8,128)(2,1)S(1)}, u32[]{:S(2)}, u32[]{:S(2)}) collective-permute-start(bf16[32,16,128]{2,1,0:T(8,128)(2,1)S(1)} %get-tuple-element.31), channel_id=1, source_target_pairs={{0,4},{1,0},{2,6},{3,2},{4,5},{5,1},{6,7},{7,3},{8,12},{9,8},{10,1... | collective-permute-start | bytes 393224 | tf_op jit(solution)/shard_map/ppermute | solution.py:440
  93.7 11.2 %collective-permute-start.13 = (bf16[32,16,128]{2,1,0:T(8,128)(2,1)S(1)}, bf16[32,16,128]{2,1,0:T(8,128)(2,1)S(1)}, u32[]{:S(2)}, u32[]{:S(2)}) collective-permute-start(bf16[32,16,128]{2,1,0:T(8,128)(2,1)S(1)} %get-tuple-element.32), channel_id=1, source_target_pairs={{0,16},{1,20},{2,18},{3,22},{4,17},{5,21},{6,19},{7,23},{8,24},{9,... | collective-permute-start | bytes 393224 | tf_op jit(solution)/shard_map/ppermute | solution.py:440
  97.8 22.8 %copy-start.1 = (bf16[8192,128]{1,0:T(8,128)(2,1)S(1)}, bf16[8192,128]{1,0:T(8,128)(2,1)}, u32[]{:S(2)}) copy-start(bf16[8192,128]{1,0:T(8,128)(2,1)} %ri_ref.3) | copy-start | bytes 6291460
  97.8 12.1 %collective-permute-start.14 = (bf16[32,16,128]{2,1,0:T(8,128)(2,1)S(1)}, bf16[32,16,128]{2,1,0:T(8,128)(2,1)S(1)}, u32[]{:S(2)}, u32[]{:S(2)}) collective-permute-start(bf16[32,16,128]{2,1,0:T(8,128)(2,1)S(1)} %get-tuple-element.33), channel_id=1, source_target_pairs={{0,20},{1,16},{2,22},{3,18},{4,21},{5,17},{6,23},{7,19},{8,28},{9,... | collective-permute-start | bytes 393224 | tf_op jit(solution)/shard_map/ppermute | solution.py:440
  99.8 13.7 %collective-permute-start.11 = (bf16[32,16,128]{2,1,0:T(8,128)(2,1)S(1)}, bf16[32,16,128]{2,1,0:T(8,128)(2,1)S(1)}, u32[]{:S(2)}, u32[]{:S(2)}) collective-permute-start(bf16[32,16,128]{2,1,0:T(8,128)(2,1)S(1)} %get-tuple-element.22.after_ref), channel_id=1, source_target_pairs={{0,0},{1,4},{2,2},{3,6},{4,1},{5,5},{6,3},{7,7},{8,8},{9,12},{10,1... | collective-permute-start | bytes 393224 | tf_op jit(solution)/shard_map/ppermute | solution.py:440
  102.7 13.7 %collective-permute-start.16 = (bf16[32,16,128]{2,1,0:T(8,128)(2,1)S(1)}, bf16[32,16,128]{2,1,0:T(8,128)(2,1)S(1)}, u32[]{:S(2)}, u32[]{:S(2)}) collective-permute-start(bf16[32,16,128]{2,1,0:T(8,128)(2,1)S(1)} %get-tuple-element.34), channel_id=1, source_target_pairs={{0,4},{1,0},{2,6},{3,2},{4,5},{5,1},{6,7},{7,3},{8,12},{9,8},{10,1... | collective-permute-start | bytes 393224 | tf_op jit(solution)/shard_map/ppermute | solution.py:440
  103.5 14.4 %collective-permute-start.17 = (bf16[32,16,128]{2,1,0:T(8,128)(2,1)S(1)}, bf16[32,16,128]{2,1,0:T(8,128)(2,1)S(1)}, u32[]{:S(2)}, u32[]{:S(2)}) collective-permute-start(bf16[32,16,128]{2,1,0:T(8,128)(2,1)S(1)} %get-tuple-element.35), channel_id=1, source_target_pairs={{0,16},{1,20},{2,18},{3,22},{4,17},{5,21},{6,19},{7,23},{8,24},{9,... | collective-permute-start | bytes 393224 | tf_op jit(solution)/shard_map/ppermute | solution.py:440
  104.9 14.9 %collective-permute-start.18 = (bf16[32,16,128]{2,1,0:T(8,128)(2,1)S(1)}, bf16[32,16,128]{2,1,0:T(8,128)(2,1)S(1)}, u32[]{:S(2)}, u32[]{:S(2)}) collective-permute-start(bf16[32,16,128]{2,1,0:T(8,128)(2,1)S(1)} %get-tuple-element.36), channel_id=1, source_target_pairs={{0,20},{1,16},{2,22},{3,18},{4,21},{5,17},{6,23},{7,19},{8,28},{9,... | collective-permute-start | bytes 393224 | tf_op jit(solution)/shard_map/ppermute | solution.py:440
  109.9 10.6 %collective-permute-start.15 = (bf16[32,16,128]{2,1,0:T(8,128)(2,1)S(1)}, bf16[32,16,128]{2,1,0:T(8,128)(2,1)S(1)}, u32[]{:S(2)}, u32[]{:S(2)}) collective-permute-start(bf16[32,16,128]{2,1,0:T(8,128)(2,1)S(1)} %get-tuple-element.23.after_ref), channel_id=1, source_target_pairs={{0,0},{1,4},{2,2},{3,6},{4,1},{5,5},{6,3},{7,7},{8,8},{9,12},{10,1... | collective-permute-start | bytes 393224 | tf_op jit(solution)/shard_map/ppermute | solution.py:440
  113.6 16.9 %collective-permute-start.3 = (bf16[32,16,128]{2,1,0:T(8,128)(2,1)S(1)}, bf16[32,16,128]{2,1,0:T(8,128)(2,1)S(1)}, u32[]{:S(2)}, u32[]{:S(2)}) collective-permute-start(bf16[32,16,128]{2,1,0:T(8,128)(2,1)S(1)} %get-tuple-element.24), channel_id=1, source_target_pairs={{0,0},{1,4},{2,2},{3,6},{4,1},{5,5},{6,3},{7,7},{8,8},{9,12},{10,1... | collective-permute-start | bytes 393224 | tf_op jit(solution)/shard_map/ppermute | solution.py:440
  116.4 14.1 %collective-permute-start.4 = (bf16[32,16,128]{2,1,0:T(8,128)(2,1)S(1)}, bf16[32,16,128]{2,1,0:T(8,128)(2,1)S(1)}, u32[]{:S(2)}, u32[]{:S(2)}) collective-permute-start(bf16[32,16,128]{2,1,0:T(8,128)(2,1)S(1)} %get-tuple-element.25), channel_id=1, source_target_pairs={{0,4},{1,0},{2,6},{3,2},{4,5},{5,1},{6,7},{7,3},{8,12},{9,8},{10,1... | collective-permute-start | bytes 393224 | tf_op jit(solution)/shard_map/ppermute | solution.py:440
  117.8 14.1 %collective-permute-start.5 = (bf16[32,16,128]{2,1,0:T(8,128)(2,1)S(1)}, bf16[32,16,128]{2,1,0:T(8,128)(2,1)S(1)}, u32[]{:S(2)}, u32[]{:S(2)}) collective-permute-start(bf16[32,16,128]{2,1,0:T(8,128)(2,1)S(1)} %get-tuple-element.26), channel_id=1, source_target_pairs={{0,16},{1,20},{2,18},{3,22},{4,17},{5,21},{6,19},{7,23},{8,24},{9,... | collective-permute-start | bytes 393224 | tf_op jit(solution)/shard_map/ppermute | solution.py:440
  119.8 12.2 %collective-permute-start.6 = (bf16[32,16,128]{2,1,0:T(8,128)(2,1)S(1)}, bf16[32,16,128]{2,1,0:T(8,128)(2,1)S(1)}, u32[]{:S(2)}, u32[]{:S(2)}) collective-permute-start(bf16[32,16,128]{2,1,0:T(8,128)(2,1)S(1)} %get-tuple-element.27), channel_id=1, source_target_pairs={{0,20},{1,16},{2,22},{3,18},{4,21},{5,17},{6,23},{7,19},{8,28},{9,... | collective-permute-start | bytes 393224 | tf_op jit(solution)/shard_map/ppermute | solution.py:440

commit v6 on v5

--- a/solution.py
+++ b/solution.py
@@ -306,13 +306,14 @@
 
 def first_receivers(dims, me_ref, bits_ref, inverse_ref, ri_ref, *refs):
     pieces, (out_ref, stack, t32) = refs[:-3], refs[-3:]
-    for at, quarters in enumerate(QUARTERS[:-1]):
+    for at, quarters in enumerate(QUARTERS[:-2]):
         receive(
             dims, quarters, me_ref, bits_ref, inverse_ref, ri_ref, pieces[4 * at : 4 * at + 4], out_ref, stack, t32
         )
 
 
-def last_receivers(dims, me_ref, bits_ref, inverse_ref, ri_ref, p0, p1, p2, p3, done_ref, out_hbm, whole, narrow, sems, stack, t32):
+def last_receivers(dims, me_ref, bits_ref, inverse_ref, ri_ref, *refs):
+    early, late, (done_ref, out_hbm, whole, narrow, sems, stack, t32) = refs[:4], refs[4:8], refs[8:]
     points = dims[3] * LEAF
     part = points // 4
 
@@ -322,7 +323,8 @@
         return carry
 
     lax.fori_loop(0, points // 512, take, 0)
-    receive(dims, QUARTERS[-1], me_ref, bits_ref, inverse_ref, ri_ref, (p0, p1, p2, p3), whole, stack, t32)
+    receive(dims, QUARTERS[-2], me_ref, bits_ref, inverse_ref, ri_ref, early, whole, stack, t32)
+    receive(dims, QUARTERS[-1], me_ref, bits_ref, inverse_ref, ri_ref, late, whole, stack, t32)
     copies = []
     for i in range(4):
 
@@ -444,16 +446,16 @@
     done = pl.pallas_call(
         functools.partial(first_receivers, dims),
         out_shape=jax.ShapeDtypeStruct((points, twice_rhs), F32),
-        in_specs=[on_smem(), on_smem(), on_smem()] + [on_vmem()] * (4 * len(QUARTERS) - 3),
+        in_specs=[on_smem(), on_smem(), on_smem()] + [on_vmem()] * (4 * len(QUARTERS) - 7),
         out_specs=on_vmem(),
         scratch_shapes=work,
         compiler_params=params(16),
         name="first_receivers",
-    )(me, level_bits, inverse, receiver_interp, *[piece for home in homes[:-1] for piece in home])
+    )(me, level_bits, inverse, receiver_interp, *[piece for home in homes[:-2] for piece in home])
     return pl.pallas_call(
         functools.partial(last_receivers, dims),
         out_shape=jax.ShapeDtypeStruct((points, twice_rhs), BF16),
-        in_specs=[on_smem(), on_smem(), on_smem()] + [on_vmem()] * 6,
+        in_specs=[on_smem(), on_smem(), on_smem()] + [on_vmem()] * 10,
         out_specs=on_any(),
         scratch_shapes=[
             pltpu.VMEM((points, 128), F32),
@@ -463,7 +465,7 @@
         + work,
         compiler_params=params(24),
         name="last_receivers",
-    )(me, level_bits, inverse, receiver_interp, *homes[-1], done)
+    )(me, level_bits, inverse, receiver_interp, *homes[-2], *homes[-1], done)
 
 
 def solution(mesh):

time: 139 us -> 144 us (1.036)
  the two profiles are of different devices: /device:TPU:1 before, /device:TPU:11 now
where the time goes in v6:
time: 144 us; the launch traced here: 143 us
  Pallas kernels  55.8 us (39%)
  starting transfers between devices  51 us (35%)
  waiting for transfers between devices  32.7 us (23%)
  local copies, waits for them, and re-layouts  3.42 us (2%)
    ppermute x16, starting transfers between devices, per_device(): lax.ppermute(pieces[j], AXES, [(s, swapped(s, j)) for s in range(devices)])  36.6 us
    ppermute x3, waiting for transfers between devices, per_device(): lax.ppermute(spread, AXES, [(s, s ^ mask) for s in range(devices)])  17.8 us
    pallas_call x1, Pallas kernels, per_device(): pl.pallas_call(functools.partial(source_kernel, dims), out_shape=jax.Shap...  14.9 us
    pallas_call x4, Pallas kernels, per_device(): pl.pallas_call(functools.partial(middle_kernel, dims, quarters), out_shap...  13.7 us
    all_to_all x1, waiting for transfers between devices, per_device(): lax.all_to_all(sent, AXES, split_axis=0, concat_axis=0, tiled=True)  13.2 us
    pallas_call x1, Pallas kernels, per_device(): pl.pallas_call(functools.partial(inverse_kernel, dims), out_shape=jax.Sha...  11.6 us
    pallas_call x1, Pallas kernels, per_device(): pl.pallas_call(functools.partial(last_receivers, dims), out_shape=jax.Sha...  8.64 us
    pallas_call x1, Pallas kernels, per_device(): pl.pallas_call(functools.partial(first_receivers, dims), out_shape=jax.Sh...  6.98 us
  transfers between devices with their start and end apart: 21, of which 3 were waited for; matrix products, arithmetic and copies ran while one was open for 0% of the time, Pallas kernels for 31%

profile of v6, /device:TPU:11, one launch (start us, length us, event | category | flops | bytes accessed | tf_op | source)
XLA Modules:
  0.0 143.4 jit_solution(2006157326682122994)
XLA Ops:
  0.0 1.7 %copy.9 = bf16[4,2,2,2,4,8,128]{6,5,4,1,2,3,0:T(8,128)(2,1)} copy(bf16[4,2,2,2,4,8,128]{6,5,4,3,2,1,0:T(8,128)(2,1)} %bitcast.10) | data formatting | bytes 524288 | tf_op jit(solution)/shard_map/reshape | solution.py:380
  1.7 6.3 %all-to-all-start = ((bf16[128,8,128]{2,1,0:T(8,128)(2,1)}), bf16[128,8,128]{2,1,0:T(8,128)(2,1)S(1)}, u32[]{:S(2)}, u32[]{:S(2)}) async-start(bf16[128,8,128]{2,1,0:T(8,128)(2,1)} %bitcast.7), calls=%async_computation | async-start | bytes 524288 | tf_op jit(solution)/shard_map/all_to_all | solution.py:381
  8.0 14.9 %source_side.1 = bf16[512,16,128]{2,1,0:T(8,128)(2,1)} custom-call(s32[8192]{0:T(1024)} %order_hbm.1, s32[4]{0:T(128)} %bits_ref.13, bf16[8192,128]{1,0:T(8,128)(2,1)} %ch_hbm.1, bf16[8192,128]{1,0:T(8,128)(2,1)} %si_hbm.1, bf16[1024,128]{1,0:T(8,128)(2,1)} %bitcast.11, bf16[8,2,2,64,128]{4,3,2,1,0:T(8,128)(2,1)} %tr_ref.7), custom_call_target="tpu_custom_call" | custom-call | tf_op jit(solution)/shard_map/source_side/pallas_call | solution.py:387
  22.9 0.0 copy-start.5
  22.9 0.0 all-to-all-done.f0
  22.9 5.8 %all-to-all-start.1 = ((bf16[512,16,128]{2,1,0:T(8,128)(2,1)}), bf16[512,16,128]{2,1,0:T(8,128)(2,1)S(1)}, u32[]{:S(2)}, u32[]{:S(2)}) async-start(bf16[512,16,128]{2,1,0:T(8,128)(2,1)} %source_side.1), calls=%async_computation.1 | async-start | bytes 4194304 | tf_op jit(solution)/shard_map/all_to_all | solution.py:409
  28.8 1.5 %collective-permute-start = (bf16[128,8,128]{2,1,0:T(8,128)(2,1)S(1)}, bf16[128,8,128]{2,1,0:T(8,128)(2,1)S(1)}, u32[]{:S(2)}, u32[]{:S(2)}) collective-permute-start(bf16[128,8,128]{2,1,0:T(8,128)(2,1)S(1)} %all-to-all-done.f0), channel_id=1, source_target_pairs={{0,17},{1,16},{2,19},{3,18},{4,21},{5,20},{6,23},{7,22},{8,25},{9,... | collective-permute-start | bytes 786440 | tf_op jit(solution)/shard_map/ppermute | solution.py:385
  30.3 0.1 stack.23.me_ref
  30.4 0.3 collective-permute-start.2
  30.7 0.4 collective-permute-start.1
  31.1 17.8 %collective-permute-done.after_ref.f3 = bf16[128,8,128]{2,1,0:T(8,128)(2,1)S(1)} collective-permute-done((bf16[128,8,128]{2,1,0:T(8,128)(2,1)S(1)}, bf16[128,8,128]{2,1,0:T(8,128)(2,1)S(1)}, u32[]{:S(2)}, u32[]{:S(2)}) %collective-permute-start) | collective-permute-done | bytes 262176 | tf_op jit(solution)/shard_map/ppermute | solution.py:385
  48.9 11.6 %inverse_slots.1.after_ref.inverse_ref = s32[8192]{0:T(1024)S(1)} custom-call(s32[8192]{0:T(1024)S(1)} %copy-done.5, bf16[128,8,128]{2,1,0:T(8,128)(2,1)S(1)} %collective-permute-done.after_ref.f3), custom_call_target="tpu_custom_call" | custom-call | flops 10000000000 | bytes 33554432 | tf_op jit(solution)/shard_map/inverse_slots/pallas_call | solution.py:411
  60.5 0.0 collective-permute-done.2.f2
  60.6 0.0 collective-permute-done.1.f1
  60.6 0.7 copy-done.2
  61.3 13.2 %all-to-all-done.1.g_ref = bf16[512,16,128]{2,1,0:T(8,128)(2,1)S(1)} async-done(((bf16[512,16,128]{2,1,0:T(8,128)(2,1)}), bf16[512,16,128]{2,1,0:T(8,128)(2,1)S(1)}, u32[]{:S(2)}, u32[]{:S(2)}) %all-to-all-start.1) | async-done | bytes 2097184 | tf_op jit(solution)/shard_map/all_to_all | solution.py:409
  74.4 0.9 copy-done.3
  75.4 3.4 %middle_levels.4 = (bf16[32,16,128]{2,1,0:T(8,128)(2,1)S(1)}, bf16[32,16,128]{2,1,0:T(8,128)(2,1)S(1)}, bf16[32,16,128]{2,1,0:T(8,128)(2,1)S(1)}, bf16[32,16,128]{2,1,0:T(8,128)(2,1)S(1)}) custom-call(s32[5]{0:T(128)S(1)} %stack.23.me_ref, s32[4]{0:T(128)S(1)} %copy-done.4, bf16[512,16,128]{2,1,0:T(8,128)(2,1)S(1)} %all-to-all-done.1.g_ref, ...), custom_call_target="tpu_custom_call" | custom-call | tf_op jit(solution)/shard_map/middle_levels/pallas_call | solution.py:425
  78.8 1.4 collective-permute-start.12
  80.1 3.0 %collective-permute-start.13 = (bf16[32,16,128]{2,1,0:T(8,128)(2,1)S(1)}, bf16[32,16,128]{2,1,0:T(8,128)(2,1)S(1)}, u32[]{:S(2)}, u32[]{:S(2)}) collective-permute-start(bf16[32,16,128]{2,1,0:T(8,128)(2,1)S(1)} %get-tuple-element.32), channel_id=1, source_target_pairs={{0,16},{1,20},{2,18},{3,22},{4,17},{5,21},{6,19},{7,23},{8,24},{9,... | collective-permute-start | bytes 393224 | tf_op jit(solution)/shard_map/ppermute | solution.py:442
  83.1 1.0 collective-permute-start.14
  84.1 1.9 %collective-permute-start.11 = (bf16[32,16,128]{2,1,0:T(8,128)(2,1)S(1)}, bf16[32,16,128]{2,1,0:T(8,128)(2,1)S(1)}, u32[]{:S(2)}, u32[]{:S(2)}) collective-permute-start(bf16[32,16,128]{2,1,0:T(8,128)(2,1)S(1)} %get-tuple-element.21.after_ref), channel_id=1, source_target_pairs={{0,0},{1,4},{2,2},{3,6},{4,1},{5,5},{6,3},{7,7},{8,8},{9,12},{10,1... | collective-permute-start | bytes 393224 | tf_op jit(solution)/shard_map/ppermute | solution.py:442
  86.1 3.4 %middle_levels.5 = (bf16[32,16,128]{2,1,0:T(8,128)(2,1)S(1)}, bf16[32,16,128]{2,1,0:T(8,128)(2,1)S(1)}, bf16[32,16,128]{2,1,0:T(8,128)(2,1)S(1)}, bf16[32,16,128]{2,1,0:T(8,128)(2,1)S(1)}) custom-call(s32[5]{0:T(128)S(1)} %stack.23.me_ref, s32[4]{0:T(128)S(1)} %copy-done.4, bf16[512,16,128]{2,1,0:T(8,128)(2,1)S(1)} %all-to-all-done.1.g_ref, ...), custom_call_target="tpu_custom_call" | custom-call | tf_op jit(solution)/shard_map/middle_levels/pallas_call | solution.py:425
  89.5 0.1 collective-permute-start.16
  89.6 0.0 collective-permute-done.12.refs_1_
  89.6 5.5 %collective-permute-start.17 = (bf16[32,16,128]{2,1,0:T(8,128)(2,1)S(1)}, bf16[32,16,128]{2,1,0:T(8,128)(2,1)S(1)}, u32[]{:S(2)}, u32[]{:S(2)}) collective-permute-start(bf16[32,16,128]{2,1,0:T(8,128)(2,1)S(1)} %get-tuple-element.35), channel_id=1, source_target_pairs={{0,16},{1,20},{2,18},{3,22},{4,17},{5,21},{6,19},{7,23},{8,24},{9,... | collective-permute-start | bytes 393224 | tf_op jit(solution)/shard_map/ppermute | solution.py:442
  95.1 0.0 collective-permute-done.13.refs_2_
  95.1 0.0 collective-permute-start.18
  95.1 3.4 %middle_levels.6 = (bf16[32,16,128]{2,1,0:T(8,128)(2,1)S(1)}, bf16[32,16,128]{2,1,0:T(8,128)(2,1)S(1)}, bf16[32,16,128]{2,1,0:T(8,128)(2,1)S(1)}, bf16[32,16,128]{2,1,0:T(8,128)(2,1)S(1)}) custom-call(s32[5]{0:T(128)S(1)} %stack.23.me_ref, s32[4]{0:T(128)S(1)} %copy-done.4, bf16[512,16,128]{2,1,0:T(8,128)(2,1)S(1)} %all-to-all-done.1.g_ref, ...), custom_call_target="tpu_custom_call" | custom-call | tf_op jit(solution)/shard_map/middle_levels/pallas_call | solution.py:425
  98.6 0.0 copy-start.1
  98.6 0.0 collective-permute-done.14.refs_3_
  98.6 5.5 %collective-permute-start.15 = (bf16[32,16,128]{2,1,0:T(8,128)(2,1)S(1)}, bf16[32,16,128]{2,1,0:T(8,128)(2,1)S(1)}, u32[]{:S(2)}, u32[]{:S(2)}) collective-permute-start(bf16[32,16,128]{2,1,0:T(8,128)(2,1)S(1)} %get-tuple-element.22.after_ref), channel_id=1, source_target_pairs={{0,0},{1,4},{2,2},{3,6},{4,1},{5,5},{6,3},{7,7},{8,8},{9,12},{10,1... | collective-permute-start | bytes 393224 | tf_op jit(solution)/shard_map/ppermute | solution.py:442
  104.1 0.1 collective-permute-start.4
  104.1 0.8 collective-permute-start.5
  104.9 0.0 collective-permute-done.17.refs_6_
  104.9 1.3 collective-permute-start.6
  106.2 3.4 %middle_levels.7 = (bf16[32,16,128]{2,1,0:T(8,128)(2,1)S(1)}, bf16[32,16,128]{2,1,0:T(8,128)(2,1)S(1)}, bf16[32,16,128]{2,1,0:T(8,128)(2,1)S(1)}, bf16[32,16,128]{2,1,0:T(8,128)(2,1)S(1)}) custom-call(s32[5]{0:T(128)S(1)} %stack.23.me_ref, s32[4]{0:T(128)S(1)} %copy-done.4, bf16[512,16,128]{2,1,0:T(8,128)(2,1)S(1)} %all-to-all-done.1.g_ref, ...), custom_call_target="tpu_custom_call" | custom-call | tf_op jit(solution)/shard_map/middle_levels/pallas_call | solution.py:425
  109.6 5.1 %collective-permute-start.7 = (bf16[32,16,128]{2,1,0:T(8,128)(2,1)S(1)}, bf16[32,16,128]{2,1,0:T(8,128)(2,1)S(1)}, u32[]{:S(2)}, u32[]{:S(2)}) collective-permute-start(bf16[32,16,128]{2,1,0:T(8,128)(2,1)S(1)} %get-tuple-element.27), channel_id=1, source_target_pairs={{0,0},{1,4},{2,2},{3,6},{4,1},{5,5},{6,3},{7,7},{8,8},{9,12},{10,1... | collective-permute-start | bytes 393224 | tf_op jit(solution)/shard_map/ppermute | solution.py:442
  114.7 0.0 collective-permute-done.15.refs_4_
  114.7 0.1 collective-permute-start.8
  114.8 0.0 collective-permute-done.4.refs_1_
  114.8 2.2 %collective-permute-start.9 = (bf16[32,16,128]{2,1,0:T(8,128)(2,1)S(1)}, bf16[32,16,128]{2,1,0:T(8,128)(2,1)S(1)}, u32[]{:S(2)}, u32[]{:S(2)}) collective-permute-start(bf16[32,16,128]{2,1,0:T(8,128)(2,1)S(1)} %get-tuple-element.29), channel_id=1, source_target_pairs={{0,16},{1,20},{2,18},{3,22},{4,17},{5,21},{6,19},{7,23},{8,24},{9,... | collective-permute-start | bytes 393224 | tf_op jit(solution)/shard_map/ppermute | solution.py:442
  117.0 1.7 %collective-permute-done.5.refs_2_ = bf16[32,16,128]{2,1,0:T(8,128)(2,1)S(1)} collective-permute-done((bf16[32,16,128]{2,1,0:T(8,128)(2,1)S(1)}, bf16[32,16,128]{2,1,0:T(8,128)(2,1)S(1)}, u32[]{:S(2)}, u32[]{:S(2)}) %collective-permute-start.5) | collective-permute-done | bytes 131104 | tf_op jit(solution)/shard_map/ppermute | solution.py:442
  118.7 0.0 collective-permute-start.10
  118.7 0.0 collective-permute-done.6.refs_3_
  118.7 8.8 %collective-permute-start.3 = (bf16[32,16,128]{2,1,0:T(8,128)(2,1)S(1)}, bf16[32,16,128]{2,1,0:T(8,128)(2,1)S(1)}, u32[]{:S(2)}, u32[]{:S(2)}) collective-permute-start(bf16[32,16,128]{2,1,0:T(8,128)(2,1)S(1)} %get-tuple-element.23.after_ref), channel_id=1, source_target_pairs={{0,0},{1,4},{2,2},{3,6},{4,1},{5,5},{6,3},{7,7},{8,8},{9,12},{10,1... | collective-permute-start | bytes 393224 | tf_op jit(solution)/shard_map/ppermute | solution.py:442
  127.6 7.0 %first_receivers.1.refs_8_ = f32[8192,128]{1,0:T(8,128)S(1)} custom-call(s32[5]{0:T(128)S(1)} %stack.23.me_ref, s32[4]{0:T(128)S(1)} %copy-done.4, s32[8192]{0:T(1024)S(1)} %inverse_slots.1.after_ref.inverse_ref, bf16[8192,128]{1,0:T(8,128)(2,1)S(1)} %copy-done.1, bf16[32,16,128]{2,1,0:T(8,128)(2,1)S(1)} %collective-permute-done.11.refs_0_, ...), custom_call_target="tpu_custom_call" | custom-call | tf_op jit(solution)/shard_map/first_receivers/pallas_call | solution.py:446
  134.6 8.6 %last_receivers.1 = bf16[8192,128]{1,0:T(8,128)(2,1)} custom-call(s32[5]{0:T(128)S(1)} %stack.23.me_ref, s32[4]{0:T(128)S(1)} %copy-done.4, s32[8192]{0:T(1024)S(1)} %inverse_slots.1.after_ref.inverse_ref, bf16[8192,128]{1,0:T(8,128)(2,1)S(1)} %copy-done.1, bf16[32,16,128]{2,1,0:T(8,128)(2,1)S(1)} %collective-permute-done.3.refs_0_, ...), custom_call_target="tpu_custom_call" | custom-call | tf_op jit(solution)/shard_map/last_receivers/pallas_call | solution.py:455
  (16 shorter events, 0.0 us)
Async XLA Ops:
  1.7 21.2 %all-to-all-start = ((bf16[128,8,128]{2,1,0:T(8,128)(2,1)}), bf16[128,8,128]{2,1,0:T(8,128)(2,1)S(1)}, u32[]{:S(2)}, u32[]{:S(2)}) async-start(bf16[128,8,128]{2,1,0:T(8,128)(2,1)} %bitcast.7), calls=%async_computation | async-start | bytes 524288 | tf_op jit(solution)/shard_map/all_to_all | solution.py:381
  22.9 26.0 %copy-start.5 = (s32[8192]{0:T(1024)S(1)}, s32[8192]{0:T(1024)}, u32[]{:S(2)}) copy-start(s32[8192]{0:T(1024)} %slot_ref.1) | copy-start | bytes 98308
  22.9 51.5 %all-to-all-start.1 = ((bf16[512,16,128]{2,1,0:T(8,128)(2,1)}), bf16[512,16,128]{2,1,0:T(8,128)(2,1)S(1)}, u32[]{:S(2)}, u32[]{:S(2)}) async-start(bf16[512,16,128]{2,1,0:T(8,128)(2,1)} %source_side.1), calls=%async_computation.1 | async-start | bytes 4194304 | tf_op jit(solution)/shard_map/all_to_all | solution.py:409
  28.8 20.1 %collective-permute-start = (bf16[128,8,128]{2,1,0:T(8,128)(2,1)S(1)}, bf16[128,8,128]{2,1,0:T(8,128)(2,1)S(1)}, u32[]{:S(2)}, u32[]{:S(2)}) collective-permute-start(bf16[128,8,128]{2,1,0:T(8,128)(2,1)S(1)} %all-to-all-done.f0), channel_id=1, source_target_pairs={{0,17},{1,16},{2,19},{3,18},{4,21},{5,20},{6,23},{7,22},{8,25},{9,... | collective-permute-start | bytes 786440 | tf_op jit(solution)/shard_map/ppermute | solution.py:385
  30.4 44.1 %copy-start = (bf16[8,2,2,64,128]{4,3,2,1,0:T(8,128)(2,1)S(1)}, bf16[8,2,2,64,128]{4,3,2,1,0:T(8,128)(2,1)}, u32[]{:S(2)}) copy-start(bf16[8,2,2,64,128]{4,3,2,1,0:T(8,128)(2,1)} %tr_ref.7) | copy-start | bytes 1572868
  30.4 44.1 %copy-start.4 = (s32[4]{0:T(128)S(1)}, s32[4]{0:T(128)}, u32[]{:S(2)}) copy-start(s32[4]{0:T(128)} %bits_ref.13) | copy-start | bytes 52
  30.4 30.2 %collective-permute-start.2 = (bf16[128,8,128]{2,1,0:T(8,128)(2,1)S(1)}, bf16[128,8,128]{2,1,0:T(8,128)(2,1)S(1)}, u32[]{:S(2)}, u32[]{:S(2)}) collective-permute-start(bf16[128,8,128]{2,1,0:T(8,128)(2,1)S(1)} %all-to-all-done.f0), channel_id=1, source_target_pairs={{0,16},{1,17},{2,18},{3,19},{4,20},{5,21},{6,22},{7,23},{8,24},{9,... | collective-permute-start | bytes 786440 | tf_op jit(solution)/shard_map/ppermute | solution.py:385
  30.7 29.9 %collective-permute-start.1 = (bf16[128,8,128]{2,1,0:T(8,128)(2,1)S(1)}, bf16[128,8,128]{2,1,0:T(8,128)(2,1)S(1)}, u32[]{:S(2)}, u32[]{:S(2)}) collective-permute-start(bf16[128,8,128]{2,1,0:T(8,128)(2,1)S(1)} %all-to-all-done.f0), channel_id=1, source_target_pairs={{0,1},{1,0},{2,3},{3,2},{4,5},{5,4},{6,7},{7,6},{8,9},{9,8},{10,11... | collective-permute-start | bytes 786440 | tf_op jit(solution)/shard_map/ppermute | solution.py:385
  60.6 0.7 copy-start.2
  74.4 1.0 copy-start.3
  78.8 10.8 %collective-permute-start.12 = (bf16[32,16,128]{2,1,0:T(8,128)(2,1)S(1)}, bf16[32,16,128]{2,1,0:T(8,128)(2,1)S(1)}, u32[]{:S(2)}, u32[]{:S(2)}) collective-permute-start(bf16[32,16,128]{2,1,0:T(8,128)(2,1)S(1)} %get-tuple-element.31), channel_id=1, source_target_pairs={{0,4},{1,0},{2,6},{3,2},{4,5},{5,1},{6,7},{7,3},{8,12},{9,8},{10,1... | collective-permute-start | bytes 393224 | tf_op jit(solution)/shard_map/ppermute | solution.py:442
  80.1 15.0 %collective-permute-start.13 = (bf16[32,16,128]{2,1,0:T(8,128)(2,1)S(1)}, bf16[32,16,128]{2,1,0:T(8,128)(2,1)S(1)}, u32[]{:S(2)}, u32[]{:S(2)}) collective-permute-start(bf16[32,16,128]{2,1,0:T(8,128)(2,1)S(1)} %get-tuple-element.32), channel_id=1, source_target_pairs={{0,16},{1,20},{2,18},{3,22},{4,17},{5,21},{6,19},{7,23},{8,24},{9,... | collective-permute-start | bytes 393224 | tf_op jit(solution)/shard_map/ppermute | solution.py:442
  83.1 15.5 %collective-permute-start.14 = (bf16[32,16,128]{2,1,0:T(8,128)(2,1)S(1)}, bf16[32,16,128]{2,1,0:T(8,128)(2,1)S(1)}, u32[]{:S(2)}, u32[]{:S(2)}) collective-permute-start(bf16[32,16,128]{2,1,0:T(8,128)(2,1)S(1)} %get-tuple-element.33), channel_id=1, source_target_pairs={{0,20},{1,16},{2,22},{3,18},{4,21},{5,17},{6,23},{7,19},{8,28},{9,... | collective-permute-start | bytes 393224 | tf_op jit(solution)/shard_map/ppermute | solution.py:442
  84.1 19.9 %collective-permute-start.11 = (bf16[32,16,128]{2,1,0:T(8,128)(2,1)S(1)}, bf16[32,16,128]{2,1,0:T(8,128)(2,1)S(1)}, u32[]{:S(2)}, u32[]{:S(2)}) collective-permute-start(bf16[32,16,128]{2,1,0:T(8,128)(2,1)S(1)} %get-tuple-element.21.after_ref), channel_id=1, source_target_pairs={{0,0},{1,4},{2,2},{3,6},{4,1},{5,5},{6,3},{7,7},{8,8},{9,12},{10,1... | collective-permute-start | bytes 393224 | tf_op jit(solution)/shard_map/ppermute | solution.py:442
  89.5 14.6 %collective-permute-start.16 = (bf16[32,16,128]{2,1,0:T(8,128)(2,1)S(1)}, bf16[32,16,128]{2,1,0:T(8,128)(2,1)S(1)}, u32[]{:S(2)}, u32[]{:S(2)}) collective-permute-start(bf16[32,16,128]{2,1,0:T(8,128)(2,1)S(1)} %get-tuple-element.34), channel_id=1, source_target_pairs={{0,4},{1,0},{2,6},{3,2},{4,5},{5,1},{6,7},{7,3},{8,12},{9,8},{10,1... | collective-permute-start | bytes 393224 | tf_op jit(solution)/shard_map/ppermute | solution.py:442
  89.6 15.3 %collective-permute-start.17 = (bf16[32,16,128]{2,1,0:T(8,128)(2,1)S(1)}, bf16[32,16,128]{2,1,0:T(8,128)(2,1)S(1)}, u32[]{:S(2)}, u32[]{:S(2)}) collective-permute-start(bf16[32,16,128]{2,1,0:T(8,128)(2,1)S(1)} %get-tuple-element.35), channel_id=1, source_target_pairs={{0,16},{1,20},{2,18},{3,22},{4,17},{5,21},{6,19},{7,23},{8,24},{9,... | collective-permute-start | bytes 393224 | tf_op jit(solution)/shard_map/ppermute | solution.py:442
  95.1 14.5 %collective-permute-start.18 = (bf16[32,16,128]{2,1,0:T(8,128)(2,1)S(1)}, bf16[32,16,128]{2,1,0:T(8,128)(2,1)S(1)}, u32[]{:S(2)}, u32[]{:S(2)}) collective-permute-start(bf16[32,16,128]{2,1,0:T(8,128)(2,1)S(1)} %get-tuple-element.36), channel_id=1, source_target_pairs={{0,20},{1,16},{2,22},{3,18},{4,21},{5,17},{6,23},{7,19},{8,28},{9,... | collective-permute-start | bytes 393224 | tf_op jit(solution)/shard_map/ppermute | solution.py:442
  98.6 29.0 %copy-start.1 = (bf16[8192,128]{1,0:T(8,128)(2,1)S(1)}, bf16[8192,128]{1,0:T(8,128)(2,1)}, u32[]{:S(2)}) copy-start(bf16[8192,128]{1,0:T(8,128)(2,1)} %ri_ref.3) | copy-start | bytes 6291460
  98.6 16.1 %collective-permute-start.15 = (bf16[32,16,128]{2,1,0:T(8,128)(2,1)S(1)}, bf16[32,16,128]{2,1,0:T(8,128)(2,1)S(1)}, u32[]{:S(2)}, u32[]{:S(2)}) collective-permute-start(bf16[32,16,128]{2,1,0:T(8,128)(2,1)S(1)} %get-tuple-element.22.after_ref), channel_id=1, source_target_pairs={{0,0},{1,4},{2,2},{3,6},{4,1},{5,5},{6,3},{7,7},{8,8},{9,12},{10,1... | collective-permute-start | bytes 393224 | tf_op jit(solution)/shard_map/ppermute | solution.py:442
  104.1 10.7 %collective-permute-start.4 = (bf16[32,16,128]{2,1,0:T(8,128)(2,1)S(1)}, bf16[32,16,128]{2,1,0:T(8,128)(2,1)S(1)}, u32[]{:S(2)}, u32[]{:S(2)}) collective-permute-start(bf16[32,16,128]{2,1,0:T(8,128)(2,1)S(1)} %get-tuple-element.24), channel_id=1, source_target_pairs={{0,4},{1,0},{2,6},{3,2},{4,5},{5,1},{6,7},{7,3},{8,12},{9,8},{10,1... | collective-permute-start | bytes 393224 | tf_op jit(solution)/shard_map/ppermute | solution.py:442
  104.1 14.6 %collective-permute-start.5 = (bf16[32,16,128]{2,1,0:T(8,128)(2,1)S(1)}, bf16[32,16,128]{2,1,0:T(8,128)(2,1)S(1)}, u32[]{:S(2)}, u32[]{:S(2)}) collective-permute-start(bf16[32,16,128]{2,1,0:T(8,128)(2,1)S(1)} %get-tuple-element.25), channel_id=1, source_target_pairs={{0,16},{1,20},{2,18},{3,22},{4,17},{5,21},{6,19},{7,23},{8,24},{9,... | collective-permute-start | bytes 393224 | tf_op jit(solution)/shard_map/ppermute | solution.py:442
  104.9 13.8 %collective-permute-start.6 = (bf16[32,16,128]{2,1,0:T(8,128)(2,1)S(1)}, bf16[32,16,128]{2,1,0:T(8,128)(2,1)S(1)}, u32[]{:S(2)}, u32[]{:S(2)}) collective-permute-start(bf16[32,16,128]{2,1,0:T(8,128)(2,1)S(1)} %get-tuple-element.26), channel_id=1, source_target_pairs={{0,20},{1,16},{2,22},{3,18},{4,21},{5,17},{6,23},{7,19},{8,28},{9,... | collective-permute-start | bytes 393224 | tf_op jit(solution)/shard_map/ppermute | solution.py:442
  109.6 25.0 %collective-permute-start.7 = (bf16[32,16,128]{2,1,0:T(8,128)(2,1)S(1)}, bf16[32,16,128]{2,1,0:T(8,128)(2,1)S(1)}, u32[]{:S(2)}, u32[]{:S(2)}) collective-permute-start(bf16[32,16,128]{2,1,0:T(8,128)(2,1)S(1)} %get-tuple-element.27), channel_id=1, source_target_pairs={{0,0},{1,4},{2,2},{3,6},{4,1},{5,5},{6,3},{7,7},{8,8},{9,12},{10,1... | collective-permute-start | bytes 393224 | tf_op jit(solution)/shard_map/ppermute | solution.py:442
  114.7 19.9 %collective-permute-start.8 = (bf16[32,16,128]{2,1,0:T(8,128)(2,1)S(1)}, bf16[32,16,128]{2,1,0:T(8,128)(2,1)S(1)}, u32[]{:S(2)}, u32[]{:S(2)}) collective-permute-start(bf16[32,16,128]{2,1,0:T(8,128)(2,1)S(1)} %get-tuple-element.28), channel_id=1, source_target_pairs={{0,4},{1,0},{2,6},{3,2},{4,5},{5,1},{6,7},{7,3},{8,12},{9,8},{10,1... | collective-permute-start | bytes 393224 | tf_op jit(solution)/shard_map/ppermute | solution.py:442
  114.8 19.8 %collective-permute-start.9 = (bf16[32,16,128]{2,1,0:T(8,128)(2,1)S(1)}, bf16[32,16,128]{2,1,0:T(8,128)(2,1)S(1)}, u32[]{:S(2)}, u32[]{:S(2)}) collective-permute-start(bf16[32,16,128]{2,1,0:T(8,128)(2,1)S(1)} %get-tuple-element.29), channel_id=1, source_target_pairs={{0,16},{1,20},{2,18},{3,22},{4,17},{5,21},{6,19},{7,23},{8,24},{9,... | collective-permute-start | bytes 393224 | tf_op jit(solution)/shard_map/ppermute | solution.py:442
  118.7 15.9 %collective-permute-start.10 = (bf16[32,16,128]{2,1,0:T(8,128)(2,1)S(1)}, bf16[32,16,128]{2,1,0:T(8,128)(2,1)S(1)}, u32[]{:S(2)}, u32[]{:S(2)}) collective-permute-start(bf16[32,16,128]{2,1,0:T(8,128)(2,1)S(1)} %get-tuple-element.30), channel_id=1, source_target_pairs={{0,20},{1,16},{2,22},{3,18},{4,21},{5,17},{6,23},{7,19},{8,28},{9,... | collective-permute-start | bytes 393224 | tf_op jit(solution)/shard_map/ppermute | solution.py:442
  118.7 15.9 %collective-permute-start.3 = (bf16[32,16,128]{2,1,0:T(8,128)(2,1)S(1)}, bf16[32,16,128]{2,1,0:T(8,128)(2,1)S(1)}, u32[]{:S(2)}, u32[]{:S(2)}) collective-permute-start(bf16[32,16,128]{2,1,0:T(8,128)(2,1)S(1)} %get-tuple-element.23.after_ref), channel_id=1, source_target_pairs={{0,0},{1,4},{2,2},{3,6},{4,1},{5,5},{6,3},{7,7},{8,8},{9,12},{10,1... | collective-permute-start | bytes 393224 | tf_op jit(solution)/shard_map/ppermute | solution.py:442
